TPU v7x, 32 devices: a whole 2x2x4 slice. The times are simulated.
32 devices in a mesh: ens: 2 (over y), wide: 4 (over z), lev: 2 (over x), fld: 2 (over core).
Axes of the slice: x: 2, y: 2, z: 4, core: 2. Of those that a mesh axis runs over, the one named last changes fastest.
Arguments:
- fourier_input_rows: bfloat16 [4, 1280, 4, 4, 256], P('ens', 'wide', None, 'fld', 'lev'), parts along dimension 0, may hold values from -6 to 6
- legendre: bfloat16 [4, 1280, 1280], P('wide', ('lev', 'fld')), may hold values from -0.15625 to 0.15625
- slot_wave: int32 [4], P('wide'), may hold values from 0 to 1279, as said below
- to_modes: bfloat16 [128, 128], replicated, may hold values from -0.5 to 0.5
- from_modes: bfloat16 [128, 128], replicated, may hold values from -0.5 to 0.5
- mode_rate: float32 [128], replicated, may hold values from 0.05 to 5
Outputs:
- fourier_out: bfloat16 [4, 1280, 4, 4, 256], P('ens', 'wide', None, 'fld', 'lev'), parts along dimension 0
- spectral: bfloat16 [8, 1280, 4, 256], P(('ens', 'wide'), None, 'fld', 'lev'), parts along dimension 0
There are 2 independent parts, one for each index of `ens`. A program takes and returns all parts, laid end to end along the dimension named above; an argument that names none is the same for every part. Nothing has to cross between parts.
Inputs may be any that keep to these rules, and one draw needn't show every extreme that they name: `slot_wave`: the wavenumbers of the slots are distinct; one slot holds 0 and one holds 1279.
All inputs are finite; a program needn't handle non-finite values.
Results may differ from a plain program's by a relative error of at most 0.0065.
Values may be sent and summed in bfloat16 or wider, within the bound.
No kernel may reach another device: no remote copies, remote signals or barrier semaphores. Data moves between devices by JAX's collectives and lax.ppermute only.
A program may use at most 64 MiB of HBM per device.

v0:
```python
import functools
import math

import jax
import jax.numpy as jnp
from jax import lax
from jax.experimental import pallas as pl
from jax.experimental.pallas import tpu as pltpu
from jax.sharding import PartitionSpec as P

VMEM_BYTES = 8 * 1024 * 1024


def latitude_weights(count):
    position = jnp.arange(count, dtype=jnp.float32)
    return jnp.sin(math.pi * (position + 0.5) / (2 * count))


def iota2(shape, dim):
    return lax.broadcasted_iota(jnp.int32, shape, dim)


def picks(condition):
    return jnp.where(condition, 1.0, 0.0).astype(jnp.bfloat16)


def dot32(a, b):
    return jnp.dot(a, b, preferred_element_type=jnp.float32)


PIECES = 5


def copy_pieces(source, target, semaphores):
    rows = target.shape[1] // PIECES
    return [
        pltpu.make_async_copy(
            source.at[:, pl.ds(i * rows, rows), :], target.at[:, pl.ds(i * rows, rows), :], semaphores.at[i]
        )
        for i in range(PIECES)
    ]


def call(body, out_shape, name, flops, scratch=(), scalars=1, after=(), out_hbm=False):
    smem = pl.BlockSpec(memory_space=pltpu.SMEM)
    vmem = pl.BlockSpec(memory_space=pltpu.VMEM)
    hbm = pl.BlockSpec(memory_space=pltpu.HBM)

    def run(*operands):
        used = len(operands)

        def kernel(*refs):
            body(*refs[:used], *refs[used + len(after) :])

        return pl.pallas_call(
            kernel,
            out_shape=out_shape,
            in_specs=[smem] * scalars
            + [vmem] * (used - scalars)
            + [pl.BlockSpec(memory_space=pl.ANY)] * len(after),
            out_specs=jax.tree.map(lambda _: hbm if out_hbm else vmem, out_shape),
            scratch_shapes=list(scratch),
            compiler_params=pltpu.CompilerParams(vmem_limit_bytes=VMEM_BYTES),
            cost_estimate=pl.CostEstimate(flops=flops, bytes_accessed=0, transcendentals=0),
            name=name,
        )(*operands, *after)

    return run


def lane_order(lanes, lev, old, new):
    levels = lanes // 4
    part = lax.rem(new // (lanes // 2) + lev, 2)
    field = (new // levels) % 2
    return old == field * (lanes // 2) + 2 * (new % levels) + part


def split_body(slots, fields, block, meta_ref, rows_ref, weight_ref, *outs):
    latitudes = weight_ref.shape[0]
    group = slots * fields
    size = block * group
    out_row, in_row = iota2((size, size), 0), iota2((size, size), 1)
    pair = out_row // block
    slot = lax.rem(meta_ref[1] + pair // fields, slots)
    order = picks(in_row == (out_row % block) * group + slot * fields + pair % fields)
    lanes = fields * 128
    parts = picks(lane_order(lanes, meta_ref[2], iota2((lanes, lanes), 0), iota2((lanes, lanes), 1)))
    for first in range(0, latitudes, block):
        north = rows_ref[0, first * group : first * group + size, :]
        south = rows_ref[1, first * group : first * group + size, :]
        sorted_rows = dot32(order, jnp.concatenate((north, south), axis=1))
        up, down = sorted_rows[:, :128], sorted_rows[:, 128:]
        weight = weight_ref[first : first + block, :]
        halves = []
        for mixed in (up + down, up - down):
            for shift in range(slots):
                at = shift * fields * block
                halves.append(jnp.concatenate(
                    [
                        (weight * mixed[at + f * block : at + f * block + block]).astype(jnp.bfloat16)
                        for f in range(fields)
                    ],
                    axis=1,
                ))
        turned = dot32(jnp.concatenate(halves, axis=0), parts).astype(jnp.bfloat16)
        for odd in range(2):
            for shift in range(slots):
                at = (odd * slots + shift) * block
                for d in range(2):
                    outs[shift * 2 + d][odd, first : first + block, :] = turned[
                        at : at + block, d * 128 : d * 128 + 128
                    ]


def by_parity(meta_ref, rows):
    half = rows // 2
    out_row, in_row = iota2((rows, rows), 0), iota2((rows, rows), 1)
    odd = jnp.where(out_row < half, 0, 1)
    return picks(in_row == 2 * (out_row - odd * half) + (meta_ref[0] + odd) % 2)


def near_table_body(meta_ref, own_ref, beside_ref, even_ref, odd_ref):
    rows, columns = own_ref.shape
    half = rows // 2
    order = by_parity(meta_ref, rows)
    for g, table_ref in enumerate((own_ref, beside_ref)):
        at = slice(g * half, g * half + half)
        for first in range(0, columns, 256):
            lanes = slice(first, first + 256)
            result = dot32(order, table_ref[:, lanes]).astype(jnp.bfloat16)
            even_ref[at, lanes] = result[:half]
            odd_ref[at, lanes] = result[half:]


def far_table_body(meta_ref, first_ref, second_ref, out_ref, whole):
    half, columns = first_ref.shape
    for ens, ref in ((meta_ref[4], first_ref), (1 - meta_ref[4], second_ref)):
        whole[pl.ds(pl.multiple_of(ens * half, half), half), :] = ref[...]
    order = by_parity(meta_ref, 2 * half)
    for first in range(0, columns, 256):
        lanes = slice(first, first + 256)
        out_ref[:, lanes] = dot32(order, whole[:, lanes]).astype(jnp.bfloat16)


def modes_body(sizes, degree_total, meta_ref, to_ref, from_ref, rate_ref, in_ref, out_ref, scale_ref):
    levels = to_ref.shape[0]
    wide = 2 * levels
    own = levels // 2
    lane, row = iota2((levels, wide), 1), iota2((levels, wide), 0)
    owner = lax.rem(meta_ref[2] + lane // levels, 2)
    spread = picks(row == owner * own + lane % own)
    plain = picks(row == lane % levels)
    old, new = iota2((wide, wide), 0), iota2((wide, wide), 1)

    def turned(first, matrix, last):
        half = lax.dot_general(first, matrix, (((0,), (1,)), ((), ())), preferred_element_type=jnp.float32)
        return dot32(half.astype(jnp.bfloat16), last)

    same = (old // own) % 2 == new // levels
    in_ref[...] = jnp.where(same, turned(spread, to_ref[...], plain), 0.0).astype(jnp.bfloat16)
    same = old // levels == (new // own) % 2
    out_ref[...] = jnp.where(same, turned(plain, from_ref[...], spread), 0.0).astype(jnp.bfloat16)
    wide, levs, flds = sizes
    rows = degree_total // (2 * levs * flds)
    for odd in range(2):
        for d in range(levs):
            for g in range(flds):
                block = lax.rem(meta_ref[2] + d, levs) * flds + lax.rem(meta_ref[3] + g, flds)
                degree = block * (2 * rows) + 2 * iota2((rows, 1), 0) + (meta_ref[0] + odd) % 2
                real = degree.astype(jnp.float32)
                factor = 1.0 + real * (real + 1.0) * rate_ref[...] / (degree_total * degree_total)
                at = ((d * 2 + odd) * flds + g) * rows
                scale_ref[at : at + rows, :] = jnp.where(degree >= meta_ref[0], 1.0 / factor, 0.0)


def transform(tables, data, scale_ref, in_ref, out_ref, own_ref, other_ref):
    lanes = own_ref.shape[1]
    rows = own_ref.shape[0] // 2
    for odd in range(2):
        at = slice(odd * rows, odd * rows + rows)
        raw = dot32(tables[odd], data[odd]).astype(jnp.bfloat16)
        scale = jnp.concatenate([scale_ref[at, :]] * 2, axis=1)
        modes = (dot32(raw, in_ref[...]) * scale).astype(jnp.bfloat16)
        spectral = dot32(modes, out_ref[...]).astype(jnp.bfloat16)
        own_ref[at, :] = spectral[:, :lanes]
        other_ref[at, :] = spectral[:, lanes:]


def near_body(wide, meta_ref, in_ref, out_ref, scale_ref, even_ref, odd_ref, *refs):
    parts, (own_ref, other_ref, data_ref) = refs[:-3], refs[-3:]
    latitudes, lanes = parts[0].shape[1:]
    for shift in range(wide):
        owner = lax.rem(meta_ref[1] - shift + wide, wide)
        at = pl.ds(pl.multiple_of(owner * latitudes, latitudes), latitudes)
        for d in range(2):
            data_ref[:, at, d * lanes : d * lanes + lanes] = parts[shift * 2 + d][...]
    scale = scale_ref.at[: scale_ref.shape[0] // 2]
    transform((even_ref[...], odd_ref[...]), data_ref, scale, in_ref, out_ref, own_ref, other_ref)


def far_body(in_ref, out_ref, scale_ref, first_ref, second_ref, data_ref, own_ref, other_ref):
    rows = first_ref.shape[0] // 2
    tables = [
        jnp.concatenate([ref[odd * rows : odd * rows + rows, :] for ref in (first_ref, second_ref)], axis=0)
        for odd in range(2)
    ]
    scale = scale_ref.at[scale_ref.shape[0] // 2 :]
    transform(tables, data_ref, scale, in_ref, out_ref, own_ref, other_ref)


def inverse_body(wide, meta_ref, *refs):
    parts, near, far, outs, total = refs[:4], refs[4:6], refs[6:8], refs[8:-1], refs[-1]
    latitudes, lanes = outs[0].shape[1:]
    rows = parts[0].shape[0] // 2
    spectral = [
        jnp.concatenate(
            [
                jnp.concatenate([ref[odd * rows : odd * rows + rows, :] for ref in pair], axis=1)
                for pair in (parts[:2], parts[2:])
            ],
            axis=0,
        )
        for odd in range(2)
    ]
    for first in range(0, total.shape[1], 256):
        chunk = slice(first, first + 256)
        sums = []
        for odd in range(2):
            at = slice(odd * (rows // 2), (odd + 1) * (rows // 2))
            table = jnp.concatenate([near[odd][:, chunk]] + [ref[at, chunk] for ref in far], axis=0)
            sums.append(lax.dot_general(
                table, spectral[odd], (((0,), (0,)), ((), ())), preferred_element_type=jnp.float32
            ))
        total[0, chunk, :] = (sums[0] + sums[1]).astype(jnp.bfloat16)
        total[1, chunk, :] = (sums[0] - sums[1]).astype(jnp.bfloat16)
    for shift in range(wide):
        owner = lax.rem(meta_ref[1] + shift, wide)
        at = pl.ds(pl.multiple_of(owner * latitudes, latitudes), latitudes)
        for d in range(2):
            outs[shift * 2 + d][...] = total[:, at, d * lanes : d * lanes + lanes]


def join_body(slots, block, meta_ref, *refs):
    parts, out_hbm, out_ref, semaphores = refs[:-3], *refs[-3:]
    copies = copy_pieces(out_ref, out_hbm, semaphores)
    latitudes, lanes = parts[0].shape[1:]
    fields = 2
    group = slots * fields
    size = block * group
    out_row, in_row = iota2((size, size), 0), iota2((size, size), 1)
    place = out_row % group
    shift = lax.rem(meta_ref[1] - place // fields + slots, slots)
    order = picks(in_row == (shift * fields + place % fields) * block + out_row // group)
    both = 2 * lanes
    turn = picks(lane_order(both, meta_ref[2], iota2((both, both), 1), iota2((both, both), 0)))
    for first in range(0, latitudes, block):
        at = slice(first, first + block)
        stacked = jnp.concatenate(
            [
                jnp.concatenate([parts[shift * 2 + d][half, at, :] for d in range(2)], axis=1)
                for half in range(2)
                for shift in range(slots)
            ],
            axis=0,
        )
        turned = dot32(stacked, turn).astype(jnp.bfloat16)
        halves = [
            jnp.concatenate(
                [
                    turned[
                        (half * slots + shift) * block : (half * slots + shift + 1) * block,
                        field * lanes : field * lanes + lanes,
                    ]
                    for shift in range(slots)
                    for field in range(fields)
                ],
                axis=0,
            )
            for half in range(2)
        ]
        result = dot32(order, jnp.concatenate(halves, axis=1)).astype(jnp.bfloat16)
        for half in range(2):
            out_ref[half, first * group : first * group + size, :] = result[:, half * lanes : half * lanes + lanes]
        done = first + block
        if done * PIECES % latitudes == 0:
            copies[done * PIECES // latitudes - 1].start()
    for copy in copies:
        copy.wait()


def rows_body(sizes, block, meta_ref, *refs):
    wide, levs, flds = sizes
    own_refs, other_refs, out_ref = refs[:2], refs[2:4], refs[4]
    total_rows, lanes = own_refs[0].shape
    rows = total_rows // (2 * flds)
    fields = 2
    group = 2 * fields
    size = block * group
    out_row, in_row = iota2((size, size), 0), iota2((size, size), 1)
    place = out_row % group
    odd = (place // fields + meta_ref[0] % 2) % 2
    order = picks(in_row == (odd * fields + place % fields) * block + out_row // group)
    both = 2 * lanes
    turn = picks(lane_order(both, meta_ref[2], iota2((both, both), 1), iota2((both, both), 0)))
    for d in range(levs):
        for g in range(flds):
            index = lax.rem(meta_ref[2] + d, levs) * flds + lax.rem(meta_ref[3] + g, flds)
            halves = []
            for odd in range(2):
                at = slice((odd * flds + g) * rows, (odd * flds + g + 1) * rows)
                halves.append(jnp.concatenate((own_refs[d][at, :], other_refs[1 - d][at, :]), axis=1))
            turned = dot32(jnp.concatenate(halves, axis=0), turn).astype(jnp.bfloat16)
            for first in range(0, rows, block):
                stacked = jnp.concatenate(
                    [
                        turned[
                            odd * rows + first : odd * rows + first + block, field * lanes : field * lanes + lanes
                        ]
                        for odd in range(2)
                        for field in range(fields)
                    ],
                    axis=0,
                )
                start = pl.multiple_of(index * (rows * group), rows * group) + first * group
                out_ref[pl.ds(start, size), :] = dot32(order, stacked).astype(jnp.bfloat16)


def shards(fourier_input_rows, legendre, slot_wave, to_modes, from_modes, mode_rate):
    wide, levs, flds = (lax.axis_size(axis) for axis in ("wide", "lev", "fld"))
    sizes = (wide, levs, flds)
    _, latitudes, slots, fields, lanes = fourier_input_rows.shape
    _, shard_rows, half_count = legendre.shape
    degree_count = shard_rows * levs * flds
    group = slots * fields
    columns = fields * lanes
    block = 256 // group
    levels = to_modes.shape[0]
    bf16 = jnp.bfloat16

    def shape(*dims):
        return jax.ShapeDtypeStruct(dims, bf16)

    def shifted(value, axis, count, step):
        return lax.ppermute(value, axis, [(i, (i + step) % count) for i in range(count)])

    def over_lev(value):
        return shifted(value, "lev", levs, 1)

    def beside(value):
        return shifted(value, "fld", flds, 1)

    def moved(value, k, d):
        pairs = [(w * levs + l, (w + k) % wide * levs + (l + d) % levs) for w in range(wide) for l in range(levs)]
        return lax.ppermute(value, ("wide", "lev"), pairs)

    def behind(value, *others):
        return lax.optimization_barrier((value, *others))

    wide_at, lev_at, fld_at = (lax.axis_index(axis) for axis in ("wide", "lev", "fld"))
    meta = jnp.stack((slot_wave[0], wide_at, lev_at, fld_at, lax.axis_index("ens"))).astype(jnp.int32)
    position = (wide_at * latitudes + jnp.arange(latitudes, dtype=jnp.int32)).astype(jnp.float32)
    weights = jnp.sin(math.pi * (position + 0.5) / (2 * half_count))
    weights = jnp.broadcast_to(weights[:, None], (latitudes, lanes))
    move_flops = 8 * group * latitudes * 128 * 256
    transform_flops = 2 * degree_count * half_count * columns

    table_beside = beside(legendre[0])
    blocks = call(
        functools.partial(split_body, slots, fields, block), (shape(2, latitudes, lanes),) * (wide * levs),
        "split_hemispheres", move_flops,
    )(meta, fourier_input_rows.reshape(2, latitudes * group, lanes), weights)
    table_beside, *blocks = behind(table_beside, *blocks)
    *matrices, scale = call(
        functools.partial(modes_body, sizes, degree_count),
        (shape(2 * levels, 2 * levels),) * 2 + (jax.ShapeDtypeStruct((degree_count, levels), jnp.float32),),
        "spread_modes", 12 * levels * levels * levels, after=(blocks[0],),
    )(meta, to_modes, from_modes, mode_rate[None, :])
    near = call(
        near_table_body, (shape(shard_rows, half_count),) * 2, "split_table",
        4 * shard_rows * shard_rows * half_count, after=(scale,),
    )(meta, legendre[0], table_beside)

    def exchanged(blocks, ahead):
        arrived = {(0, 0): blocks[0]}
        for k, d in ((2, 0), (1, 0), (3, 0), (0, 1)):
            arrived[k, d] = moved(blocks[k * levs + d], k, d)
        for k, first in ((2, (0, 1)), (1, (1, 0)), (3, (3, 0))):
            value, arrived[first], *_ = behind(blocks[k * levs + 1], arrived[first], *ahead)
            arrived[k, 1] = moved(value, k, 1)
        return arrived

    def listed(arrived):
        return [arrived[k, d] for k in range(wide) for d in range(levs)]

    arrived = exchanged(blocks, (near[0], scale))
    half_shard = shard_rows // 2
    own_table, _ = behind(legendre[0], blocks[0])
    first = over_lev(lax.dynamic_slice_in_dim(own_table, lax.axis_index("ens") * half_shard, half_shard, 0))
    steps = [(1, 0), (2, 0), (3, 0), (0, 1)]
    first, *ahead = behind(first, *(arrived[step] for step in steps))
    arrived |= dict(zip(steps, ahead))
    second = shifted(first, "ens", 2, 1)
    far = call(
        far_table_body, shape(shard_rows, half_count), "split_table", 2 * shard_rows * shard_rows * half_count,
        scratch=[pltpu.VMEM((shard_rows, half_count), bf16)],
    )(meta, first, second)
    steps = [(1, 1), (2, 1), (3, 1)]
    far, *ahead = behind(far, *(arrived[step] for step in steps))
    arrived |= dict(zip(steps, ahead))
    far = [far, beside(far)]

    half_rows = degree_count // 2
    *near_spectral, data = call(
        functools.partial(near_body, wide), (shape(half_rows, lanes),) * 2 + (shape(2, half_count, columns),),
        "direct_legendre_and_solve", transform_flops // 2,
    )(meta, *matrices, scale, *near, *listed(arrived))
    far_spectral = call(
        far_body, (shape(half_rows, lanes),) * 2, "direct_legendre_and_solve", transform_flops // 2, scalars=0,
    )(*matrices, scale, *far, data)
    spectral = (near_spectral, far_spectral)
    grid = call(
        functools.partial(inverse_body, wide), (shape(2, latitudes, lanes),) * (wide * levs),
        "inverse_legendre", transform_flops, scratch=[pltpu.VMEM((2, half_count, columns), bf16)],
    )(meta, *near_spectral, *far_spectral, *near, *far)
    arrived = exchanged(grid, ())
    others = [other for _, other in spectral]
    arrived[0, 1], *others = behind(arrived[0, 1], *others)
    result = listed(arrived)
    spectral_rows = call(
        functools.partial(rows_body, sizes, 32), shape(degree_count * fields, lanes), "order_spectral", move_flops,
    )(meta, *(own for own, _ in spectral), *(over_lev(other) for other in others))
    fourier_rows = call(
        functools.partial(join_body, slots, 256 // group), shape(2, latitudes * group, lanes),
        "join_hemispheres", move_flops, out_hbm=True,
        scratch=[pltpu.VMEM((2, latitudes * group, lanes), bf16), pltpu.SemaphoreType.DMA((PIECES,))],
    )(meta, *result)
    return (
        fourier_rows.reshape(2, latitudes, slots, fields, lanes),
        spectral_rows.reshape(1, degree_count, fields, lanes),
    )


def project(level_grid, degree_real, weight_rows, rate_rows, degree_total):
    projected = jnp.einsum(
        "kl,snflr->snfkr", weight_rows, level_grid, preferred_element_type=jnp.float32
    )
    factor = 1.0 + degree_real[:, None] * (degree_real[:, None] + 1.0) * rate_rows[None, :] / (
        degree_total * degree_total
    )
    return (projected / factor[None, :, None, :, None]).astype(jnp.bfloat16)


def plain_shards(fourier_input_rows, legendre, slot_wave, to_modes, from_modes, mode_rate):
    wave_rows = lax.all_to_all(fourier_input_rows, "wide", split_axis=2, concat_axis=1, tiled=True)
    half_count = wave_rows.shape[1]
    slot_count = wave_rows.shape[2]
    field_count = wave_rows.shape[3]
    column_count = wave_rows.shape[4]
    degree_count = legendre.shape[1] * lax.axis_size(("lev", "fld"))
    weights = latitude_weights(half_count)[:, None, None, None]
    north_half = wave_rows[0].astype(jnp.float32)
    south_half = wave_rows[1].astype(jnp.float32)
    symmetric = (weights * (north_half + south_half)).astype(jnp.bfloat16)
    antisym = (weights * (north_half - south_half)).astype(jnp.bfloat16)
    paired = jnp.concatenate((symmetric, antisym), axis=3)

    def direct_rows(section, first_row):
        row_count = section.shape[1]
        degree = first_row + jnp.arange(row_count, dtype=jnp.int32)
        relative = degree[None, :] - slot_wave[:, None]
        product = jnp.einsum("snj,jsfc->snfc", section, paired, preferred_element_type=jnp.float32)
        is_even = (relative % 2 == 0)[:, :, None, None]
        is_live = (relative >= 0)[:, :, None, None]
        picked = jnp.where(is_even, product[..., :column_count], product[..., column_count:])
        return jnp.where(is_live, picked, jnp.zeros_like(picked))

    full_table = lax.all_gather(legendre, ("lev", "fld"), axis=1, tiled=True)
    block_rows = 128
    block_count = degree_count // block_rows

    def direct_step(block_index, buffer):
        first_row = block_index * block_rows
        section = lax.dynamic_slice_in_dim(full_table, first_row, block_rows, 1)
        result = direct_rows(section, first_row).astype(jnp.bfloat16)
        return lax.dynamic_update_slice_in_dim(buffer, result, first_row, 1)

    initial_raw = jnp.zeros((slot_count, degree_count, field_count, column_count), jnp.bfloat16)
    raw_spectral = lax.fori_loop(0, block_count, direct_step, initial_raw)
    own_levels = column_count // 2
    first_level = lax.axis_index("lev") * own_levels
    degree_real = jnp.arange(degree_count, dtype=jnp.float32)
    all_levels = lax.all_gather(raw_spectral, "lev", axis=3, tiled=True)
    level_count = all_levels.shape[3] // 2
    level_grid = all_levels.reshape(slot_count, degree_count, field_count, level_count, 2)
    weight_rows = lax.dynamic_slice_in_dim(to_modes, first_level, own_levels, 0)
    rate_rows = lax.dynamic_slice_in_dim(mode_rate, first_level, own_levels, 0)
    own_modes = project(level_grid, degree_real, weight_rows, rate_rows, degree_count).reshape(
        slot_count, degree_count, field_count, column_count
    )
    mode_values = lax.all_gather(own_modes, "lev", axis=3, tiled=True).reshape(
        slot_count, degree_count, field_count, level_count, 2
    )
    back_rows = lax.dynamic_slice_in_dim(from_modes, first_level, own_levels, 0)
    spectral = jnp.einsum(
        "lk,snfkr->snflr", back_rows, mode_values, preferred_element_type=jnp.float32
    )
    spectral = spectral.astype(jnp.bfloat16).reshape(
        slot_count, degree_count, field_count, column_count
    )

    def inverse_rows(running, section, first_row):
        row_count = section.shape[1]
        degree = first_row + jnp.arange(row_count, dtype=jnp.int32)
        relative = degree[None, :] - slot_wave[:, None]
        spec_rows = lax.dynamic_slice_in_dim(spectral, first_row, row_count, 1)
        even_mask = ((relative >= 0) & (relative % 2 == 0))[:, :, None, None]
        odd_mask = ((relative >= 0) & (relative % 2 == 1))[:, :, None, None]
        empty_rows = jnp.zeros_like(spec_rows)
        parity_split = jnp.concatenate(
            (
                jnp.where(even_mask, spec_rows, empty_rows),
                jnp.where(odd_mask, spec_rows, empty_rows),
            ),
            axis=3,
        )
        return running + jnp.einsum(
            "snj,snfc->jsfc", section, parity_split, preferred_element_type=jnp.float32
        )

    initial_sum = jnp.zeros((half_count, slot_count, field_count, 2 * column_count), jnp.float32)

    def inverse_step(block_index, running):
        first_row = block_index * block_rows
        section = lax.dynamic_slice_in_dim(full_table, first_row, block_rows, 1)
        return inverse_rows(running, section, first_row)

    running = lax.fori_loop(0, block_count, inverse_step, initial_sum)
    even_sum = running[..., :column_count]
    odd_sum = running[..., column_count:]
    fourier_wave = jnp.stack((even_sum + odd_sum, even_sum - odd_sum), axis=0).astype(jnp.bfloat16)
    fourier_out = lax.all_to_all(fourier_wave, "wide", split_axis=1, concat_axis=2, tiled=True)
    return (fourier_out, spectral)


def solution(mesh):
    in_specs = (
        P("ens", "wide", None, "fld", "lev"),
        P("wide", ("lev", "fld"), None),
        P("wide"),
        P(),
        P(),
        P(),
    )
    out_specs = (P("ens", "wide", None, "fld", "lev"), P(("ens", "wide"), None, "fld", "lev"))

    def body(fourier_input_rows, legendre, *rest):
        _, latitudes, slots, fields, lanes = fourier_input_rows.shape
        whole_tiles = (
            latitudes % (32 * PIECES) == 0
            and fields == 2
            and slots == mesh.shape["wide"] == 4
            and mesh.shape["ens"] == mesh.shape["lev"] == mesh.shape["fld"] == 2
            and lanes == 128
            and legendre.shape[1] % 64 == 0
            and legendre.shape[2] % 256 == 0
        )
        form = shards if whole_tiles else plain_shards
        return form(fourier_input_rows, legendre, *rest)

    return jax.shard_map(body, mesh=mesh, in_specs=in_specs, out_specs=out_specs, check_vma=False)
```

profile of v0, /device:TPU:0, one launch (start us, length us, event | category | flops | bytes accessed | tf_op | source)
XLA Modules:
  0.0 83.5 jit_solution(15414811775073635695)
XLA Ops:
  0.6 0.5 collective-permute-start
  1.8 0.1 stack.19.refs_0_
  1.9 0.0 copy-start
  1.9 0.1 broadcast_in_dim.10.refs_2_
  2.0 0.0 copy-start.4
  2.1 1.4 %copy-done.4 = bf16[2,320,4,2,128]{4,3,2,1,0:T(2,128)(2,1)S(1)} copy-done((bf16[2,320,4,2,128]{4,3,2,1,0:T(2,128)(2,1)S(1)}, bf16[2,320,4,2,128]{4,3,2,1,0:T(2,128)(2,1)}, u32[]{:S(2)}) %copy-start.4) | copy-done | bytes 1310744
  3.4 1.5 %split_hemispheres.1 = (bf16[2,320,128]{2,1,0:T(8,128)(2,1)S(1)}, bf16[2,320,128]{2,1,0:T(8,128)(2,1)S(1)}, bf16[2,320,128]{2,1,0:T(8,128)(2,1)S(1)}, bf16[2,320...) custom-call(s32[5]{0:T(128)S(1)} %stack.19.refs_0_, ...), custom_call_target="tpu_custom_call" | custom-call | flops 671088640 | tf_op jit(solution)/shard_map/split_hemispheres/pallas_call | solution.py:55
  5.0 0.0 collective-permute-done.refs_2_
  5.0 2.6 %collective-permute-start.1 = (bf16[160,1280]{1,0:T(8,128)(2,1)S(1)}, bf16[160,1280]{1,0:T(8,128)(2,1)S(1)}, u32[]{:S(2)}, u32[]{:S(2)}) collective-permute-start(bf16[160,1280]{1,0:T(8,128)(2,1)S(1)} %constant_dynamic-slice_fusion), channel_id=1, source_target_pairs={{0,2},{2,0},{1,3},{3,1},{4,6},{6,4},{5,7},{7,5},{8,10},{10,8},{9,1... | collective-permute-start | bytes 1228808 | tf_op jit(solution)/shard_map/ppermute | solution.py:344
  7.6 0.1 collective-permute-start.5
  7.7 4.1 %collective-permute-start.4 = (bf16[2,320,128]{2,1,0:T(8,128)(2,1)S(1)}, bf16[2,320,128]{2,1,0:T(8,128)(2,1)S(1)}, u32[]{:S(2)}, u32[]{:S(2)}) collective-permute-start(bf16[2,320,128]{2,1,0:T(8,128)(2,1)S(1)} %get-tuple-element.83), channel_id=1, source_target_pairs={{0,12},{2,14},{4,0},{6,2},{8,4},{10,6},{12,8},{14,10},{1,13},{3,15... | collective-permute-start | bytes 491528 | tf_op jit(solution)/shard_map/ppermute | solution.py:354
  11.8 0.0 collective-permute-start.2
  11.8 1.0 %collective-permute-start.3 = (bf16[2,320,128]{2,1,0:T(8,128)(2,1)S(1)}, bf16[2,320,128]{2,1,0:T(8,128)(2,1)S(1)}, u32[]{:S(2)}, u32[]{:S(2)}) collective-permute-start(bf16[2,320,128]{2,1,0:T(8,128)(2,1)S(1)} %get-tuple-element.81), channel_id=1, source_target_pairs={{0,8},{2,10},{4,12},{6,14},{8,0},{10,2},{12,4},{14,6},{1,9},{3,11}... | collective-permute-start | bytes 491528 | tf_op jit(solution)/shard_map/ppermute | solution.py:354
  12.8 1.1 %spread_modes.1 = (bf16[256,256]{1,0:T(8,128)(2,1)S(1)}, bf16[256,256]{1,0:T(8,128)(2,1)S(1)}, f32[1280,128]{1,0:T(8,128)S(1)}) custom-call(s32[5]{0:T(128)S(1)} %stack.19.refs_0_, bf16[128,128]{1,0:T(8,128)(2,1)S(1)} %copy-done.1, bf16[128,128]{1,0:T(8,128)(2,1)S(1)} %copy-done.2, f32[1,128]{1,0:T(1,128)S(1)} %bitcast.12, ...), custom_call_target="tpu_custom_call" | custom-call | flops 25165824 | tf_op jit(solution)/shard_map/spread_modes/pallas_call | solution.py:55
  13.9 1.5 %split_table.2 = (bf16[320,1280]{1,0:T(8,128)(2,1)S(1)}, bf16[320,1280]{1,0:T(8,128)(2,1)S(1)}) custom-call(s32[5]{0:T(128)S(1)} %stack.19.refs_0_, bf16[320,1280]{1,0:T(8,128)(2,1)S(1)} %bitcast.11, bf16[320,1280]{1,0:T(8,128)(2,1)S(1)} %collective-permute-done.refs_2_, f32[1280,128]{1,0:T(8,128)S(1)} %get-tuple-element.73.refs_3_.refs_2_), custom_call_target="tpu_custom_call" | custom-call | flops 524288000 | tf_op jit(solution)/shard_map/split_table/pallas_call | solution.py:55
  15.5 5.8 %collective-permute-done.5.refs_7_ = bf16[2,320,128]{2,1,0:T(8,128)(2,1)S(1)} collective-permute-done((bf16[2,320,128]{2,1,0:T(8,128)(2,1)S(1)}, bf16[2,320,128]{2,1,0:T(8,128)(2,1)S(1)}, u32[]{:S(2)}, u32[]{:S(2)}) %collective-permute-start.5) | collective-permute-done | bytes 163872 | tf_op jit(solution)/shard_map/ppermute | solution.py:354
  21.2 0.0 collective-permute-done.4.refs_12_
  21.2 0.0 collective-permute-done.2.refs_8_
  21.3 4.5 %collective-permute-done.3.refs_10_ = bf16[2,320,128]{2,1,0:T(8,128)(2,1)S(1)} collective-permute-done((bf16[2,320,128]{2,1,0:T(8,128)(2,1)S(1)}, bf16[2,320,128]{2,1,0:T(8,128)(2,1)S(1)}, u32[]{:S(2)}, u32[]{:S(2)}) %collective-permute-start.3) | collective-permute-done | bytes 163872 | tf_op jit(solution)/shard_map/ppermute | solution.py:354
  25.7 0.0 collective-permute-done.1.refs_1_
  25.7 1.5 %collective-permute-start.6 = (bf16[160,1280]{1,0:T(8,128)(2,1)S(1)}, bf16[160,1280]{1,0:T(8,128)(2,1)S(1)}, u32[]{:S(2)}, u32[]{:S(2)}) collective-permute-start(bf16[160,1280]{1,0:T(8,128)(2,1)S(1)} %collective-permute-done.1.refs_1_), channel_id=1, source_target_pairs={{0,16},{16,0},{1,17},{17,1},{2,18},{18,2},{3,19},{19,3},{4,20},{20... | collective-permute-start | bytes 1228808 | tf_op jit(solution)/shard_map/ppermute | solution.py:344
  27.3 0.8 collective-permute-start.7
  28.0 4.0 %collective-permute-start.9 = (bf16[2,320,128]{2,1,0:T(8,128)(2,1)S(1)}, bf16[2,320,128]{2,1,0:T(8,128)(2,1)S(1)}, u32[]{:S(2)}, u32[]{:S(2)}) collective-permute-start(bf16[2,320,128]{2,1,0:T(8,128)(2,1)S(1)} %get-tuple-element.93), channel_id=1, source_target_pairs={{0,14},{2,12},{4,2},{6,0},{8,6},{10,4},{12,10},{14,8},{1,15},{3,13... | collective-permute-start | bytes 491528 | tf_op jit(solution)/shard_map/ppermute | solution.py:354
  32.0 4.4 %collective-permute-done.6.refs_2_ = bf16[160,1280]{1,0:T(8,128)(2,1)S(1)} collective-permute-done((bf16[160,1280]{1,0:T(8,128)(2,1)S(1)}, bf16[160,1280]{1,0:T(8,128)(2,1)S(1)}, u32[]{:S(2)}, u32[]{:S(2)}) %collective-permute-start.6) | collective-permute-done | bytes 409632 | tf_op jit(solution)/shard_map/ppermute | solution.py:344
  36.3 1.2 %split_table.3.refs_3_.refs_7_ = bf16[320,1280]{1,0:T(8,128)(2,1)S(1)} custom-call(s32[5]{0:T(128)S(1)} %stack.19.refs_0_, bf16[160,1280]{1,0:T(8,128)(2,1)S(1)} %collective-permute-done.1.refs_1_, bf16[160,1280]{1,0:T(8,128)(2,1)S(1)} %collective-permute-done.6.refs_2_), custom_call_target="tpu_custom_call" | custom-call | flops 262144000 | tf_op jit(solution)/shard_map/split_table/pallas_call | solution.py:55
  37.5 0.0 collective-permute-done.9.refs_13_
  37.5 6.9 %collective-permute-done.8.refs_11_ = bf16[2,320,128]{2,1,0:T(8,128)(2,1)S(1)} collective-permute-done((bf16[2,320,128]{2,1,0:T(8,128)(2,1)S(1)}, bf16[2,320,128]{2,1,0:T(8,128)(2,1)S(1)}, u32[]{:S(2)}, u32[]{:S(2)}) %collective-permute-start.8) | collective-permute-done | bytes 163872 | tf_op jit(solution)/shard_map/ppermute | solution.py:354
  44.5 2.2 %direct_legendre_and_solve.2 = (bf16[640,128]{1,0:T(8,128)(2,1)S(1)}, bf16[640,128]{1,0:T(8,128)(2,1)S(1)}, bf16[2,1280,256]{2,1,0:T(8,128)(2,1)S(1)}) custom-call(s32[5]{0:T(128)S(1)} %stack.19.refs_0_, bf16[256,256]{1,0:T(8,128)(2,1)S(1)} %get-tuple-element.71.refs_1_.refs_0_, bf16[256,256]{1,0:T(8,128)(2,1)S(1)} %get-tuple-element.72.refs_2_.refs_1_, ...), custom_call_target="tpu_custom_call" | custom-call | flops 419430400 | tf_op jit(solution)/shard_map/direct_legendre_and_solve/pallas_call | solution.py:55
  46.7 0.1 collective-permute-done.10.refs_4_.refs_8_
  46.8 1.5 %direct_legendre_and_solve.3 = (bf16[640,128]{1,0:T(8,128)(2,1)S(1)}, bf16[640,128]{1,0:T(8,128)(2,1)S(1)}) custom-call(bf16[256,256]{1,0:T(8,128)(2,1)S(1)} %get-tuple-element.71.refs_1_.refs_0_, bf16[256,256]{1,0:T(8,128)(2,1)S(1)} %get-tuple-element.72.refs_2_.refs_1_, f32[1280,128]{1,0:T(8,128)S(1)} %get-tuple-element.73.refs_3_.refs_2_, ...), custom_call_target="tpu_custom_call" | custom-call | flops 419430400 | tf_op jit(solution)/shard_map/direct_legendre_and_solve/pallas_call | solution.py:55
  48.3 2.0 %inverse_legendre.1 = (bf16[2,320,128]{2,1,0:T(8,128)(2,1)S(1)}, bf16[2,320,128]{2,1,0:T(8,128)(2,1)S(1)}, bf16[2,320,128]{2,1,0:T(8,128)(2,1)S(1)}, bf16[2,320,...) custom-call(s32[5]{0:T(128)S(1)} %stack.19.refs_0_, ...), custom_call_target="tpu_custom_call" | custom-call | flops 838860800 | tf_op jit(solution)/shard_map/inverse_legendre/pallas_call | solution.py:55
  50.3 1.5 %collective-permute-start.11 = (bf16[2,320,128]{2,1,0:T(8,128)(2,1)S(1)}, bf16[2,320,128]{2,1,0:T(8,128)(2,1)S(1)}, u32[]{:S(2)}, u32[]{:S(2)}) collective-permute-start(bf16[2,320,128]{2,1,0:T(8,128)(2,1)S(1)} %get-tuple-element.107), channel_id=1, source_target_pairs={{0,2},{2,0},{4,6},{6,4},{8,10},{10,8},{12,14},{14,12},{1,3},{3,1},... | collective-permute-start | bytes 491528 | tf_op jit(solution)/shard_map/ppermute | solution.py:354
  51.9 3.8 %collective-permute-start.16 = (bf16[2,320,128]{2,1,0:T(8,128)(2,1)S(1)}, bf16[2,320,128]{2,1,0:T(8,128)(2,1)S(1)}, u32[]{:S(2)}, u32[]{:S(2)}) collective-permute-start(bf16[2,320,128]{2,1,0:T(8,128)(2,1)S(1)} %get-tuple-element.117), channel_id=1, source_target_pairs={{0,12},{2,14},{4,0},{6,2},{8,4},{10,6},{12,8},{14,10},{1,13},{3,15... | collective-permute-start | bytes 491528 | tf_op jit(solution)/shard_map/ppermute | solution.py:354
  55.7 1.2 %collective-permute-done.11.refs_2_ = bf16[2,320,128]{2,1,0:T(8,128)(2,1)S(1)} collective-permute-done((bf16[2,320,128]{2,1,0:T(8,128)(2,1)S(1)}, bf16[2,320,128]{2,1,0:T(8,128)(2,1)S(1)}, u32[]{:S(2)}, u32[]{:S(2)}) %collective-permute-start.11) | collective-permute-done | bytes 163872 | tf_op jit(solution)/shard_map/ppermute | solution.py:354
  56.9 1.4 %collective-permute-start.18 = (bf16[640,128]{1,0:T(8,128)(2,1)S(1)}, bf16[640,128]{1,0:T(8,128)(2,1)S(1)}, u32[]{:S(2)}, u32[]{:S(2)}) collective-permute-start(bf16[640,128]{1,0:T(8,128)(2,1)S(1)} %get-tuple-element.120.refs_2_), channel_id=1, source_target_pairs={{0,2},{2,0},{1,3},{3,1},{4,6},{6,4},{5,7},{7,5},{8,10},{10,8},{9,1... | collective-permute-start | bytes 491528 | tf_op jit(solution)/shard_map/ppermute | solution.py:344
  58.4 0.6 collective-permute-start.19
  59.0 0.0 collective-permute-start.14
  59.0 1.8 %collective-permute-done.12.refs_3_ = bf16[2,320,128]{2,1,0:T(8,128)(2,1)S(1)} collective-permute-done((bf16[2,320,128]{2,1,0:T(8,128)(2,1)S(1)}, bf16[2,320,128]{2,1,0:T(8,128)(2,1)S(1)}, u32[]{:S(2)}, u32[]{:S(2)}) %collective-permute-start.12) | collective-permute-done | bytes 163872 | tf_op jit(solution)/shard_map/ppermute | solution.py:354
  60.8 2.0 %collective-permute-start.15 = (bf16[2,320,128]{2,1,0:T(8,128)(2,1)S(1)}, bf16[2,320,128]{2,1,0:T(8,128)(2,1)S(1)}, u32[]{:S(2)}, u32[]{:S(2)}) collective-permute-start(bf16[2,320,128]{2,1,0:T(8,128)(2,1)S(1)} %get-tuple-element.115), channel_id=1, source_target_pairs={{0,10},{2,8},{4,14},{6,12},{8,2},{10,0},{12,6},{14,4},{1,11},{3,9}... | collective-permute-start | bytes 491528 | tf_op jit(solution)/shard_map/ppermute | solution.py:354
  62.7 0.0 collective-permute-done.16.refs_7_
  62.7 0.0 collective-permute-start.13
  62.8 1.3 %collective-permute-done.18.refs_3_ = bf16[640,128]{1,0:T(8,128)(2,1)S(1)} collective-permute-done((bf16[640,128]{1,0:T(8,128)(2,1)S(1)}, bf16[640,128]{1,0:T(8,128)(2,1)S(1)}, u32[]{:S(2)}, u32[]{:S(2)}) %collective-permute-start.18) | collective-permute-done | bytes 163872 | tf_op jit(solution)/shard_map/ppermute | solution.py:344
  64.1 3.4 %collective-permute-start.17 = (bf16[2,320,128]{2,1,0:T(8,128)(2,1)S(1)}, bf16[2,320,128]{2,1,0:T(8,128)(2,1)S(1)}, u32[]{:S(2)}, u32[]{:S(2)}) collective-permute-start(bf16[2,320,128]{2,1,0:T(8,128)(2,1)S(1)} %get-tuple-element.119), channel_id=1, source_target_pairs={{0,14},{2,12},{4,2},{6,0},{8,6},{10,4},{12,10},{14,8},{1,15},{3,13... | collective-permute-start | bytes 491528 | tf_op jit(solution)/shard_map/ppermute | solution.py:354
  67.5 0.5 collective-permute-done.19.refs_4_
  67.9 2.2 %order_spectral.1 = bf16[2560,128]{1,0:T(8,128)(2,1)} custom-call(s32[5]{0:T(128)S(1)} %stack.19.refs_0_, bf16[640,128]{1,0:T(8,128)(2,1)S(1)} %get-tuple-element.99.refs_1_, bf16[640,128]{1,0:T(8,128)(2,1)S(1)} %get-tuple-element.103.refs_3_.refs_2_, bf16[640,128]{1,0:T(8,128)(2,1)S(1)} %collective-permute-done.18.refs_3_, ...), custom_call_target="tpu_custom_call" | custom-call | flops 671088640 | tf_op jit(solution)/shard_map/order_spectral/pallas_call | solution.py:55
  70.1 7.0 %collective-permute-done.14.refs_5_ = bf16[2,320,128]{2,1,0:T(8,128)(2,1)S(1)} collective-permute-done((bf16[2,320,128]{2,1,0:T(8,128)(2,1)S(1)}, bf16[2,320,128]{2,1,0:T(8,128)(2,1)S(1)}, u32[]{:S(2)}, u32[]{:S(2)}) %collective-permute-start.14) | collective-permute-done | bytes 163872 | tf_op jit(solution)/shard_map/ppermute | solution.py:354
  77.1 4.0 %collective-permute-done.15.refs_6_ = bf16[2,320,128]{2,1,0:T(8,128)(2,1)S(1)} collective-permute-done((bf16[2,320,128]{2,1,0:T(8,128)(2,1)S(1)}, bf16[2,320,128]{2,1,0:T(8,128)(2,1)S(1)}, u32[]{:S(2)}, u32[]{:S(2)}) %collective-permute-start.15) | collective-permute-done | bytes 163872 | tf_op jit(solution)/shard_map/ppermute | solution.py:354
  81.1 2.4 %join_hemispheres.1 = bf16[2,2560,128]{2,1,0:T(8,128)(2,1)} custom-call(s32[5]{0:T(128)S(1)} %stack.19.refs_0_, bf16[2,320,128]{2,1,0:T(8,128)(2,1)S(1)} %get-tuple-element.105.refs_1_, bf16[2,320,128]{2,1,0:T(8,128)(2,1)S(1)} %collective-permute-done.11.refs_2_, bf16[2,320,128]{2,1,0:T(8,128)(2,1)S(1)} %collective-permute-done.12.refs_3_, ...), custom_call_target="tpu_custom_call" | custom-call | flops 671088640 | tf_op jit(solution)/shard_map/join_hemispheres/pallas_call | solution.py:55
  (15 shorter events, 0.1 us)
Async XLA Ops:
  0.6 4.4 %collective-permute-start = (bf16[320,1280]{1,0:T(8,128)(2,1)}, bf16[320,1280]{1,0:T(8,128)(2,1)S(1)}, u32[]{:S(2)}, u32[]{:S(2)}) collective-permute-start(bf16[320,1280]{1,0:T(8,128)(2,1)} %bitcast.9), channel_id=1, source_target_pairs={{0,1},{1,0},{2,3},{3,2},{4,5},{5,4},{6,7},{7,6},{8,9},{9,8},{10,11... | collective-permute-start | bytes 2457608 | tf_op jit(solution)/shard_map/ppermute | solution.py:344
  1.9 3.1 %copy-start = (bf16[1,320,1280]{2,1,0:T(8,128)(2,1)S(1)}, bf16[1,320,1280]{2,1,0:T(8,128)(2,1)}, u32[]{:S(2)}) copy-start(bf16[1,320,1280]{2,1,0:T(8,128)(2,1)} %param.7) | copy-start | bytes 2457604
  2.0 1.4 %copy-start.4 = (bf16[2,320,4,2,128]{4,3,2,1,0:T(2,128)(2,1)S(1)}, bf16[2,320,4,2,128]{4,3,2,1,0:T(2,128)(2,1)}, u32[]{:S(2)}) copy-start(bf16[2,320,4,2,128]{4,3,2,1,0:T(2,128)(2,1)} %param.6) | copy-start | bytes 3932164
  3.4 9.3 %copy-start.1 = (bf16[128,128]{1,0:T(8,128)(2,1)S(1)}, bf16[128,128]{1,0:T(8,128)(2,1)}, u32[]{:S(2)}) copy-start(bf16[128,128]{1,0:T(8,128)(2,1)} %refs_1_.1) | copy-start | bytes 98308
  3.4 9.3 %copy-start.2 = (bf16[128,128]{1,0:T(8,128)(2,1)S(1)}, bf16[128,128]{1,0:T(8,128)(2,1)}, u32[]{:S(2)}) copy-start(bf16[128,128]{1,0:T(8,128)(2,1)} %refs_2_.1) | copy-start | bytes 98308
  3.4 9.3 %copy-start.3 = (f32[128]{0:T(128)S(1)}, f32[128]{0:T(128)}, u32[]{:S(2)}) copy-start(f32[128]{0:T(128)} %param.11) | copy-start | bytes 1540
  5.0 20.7 %collective-permute-start.1 = (bf16[160,1280]{1,0:T(8,128)(2,1)S(1)}, bf16[160,1280]{1,0:T(8,128)(2,1)S(1)}, u32[]{:S(2)}, u32[]{:S(2)}) collective-permute-start(bf16[160,1280]{1,0:T(8,128)(2,1)S(1)} %constant_dynamic-slice_fusion), channel_id=1, source_target_pairs={{0,2},{2,0},{1,3},{3,1},{4,6},{6,4},{5,7},{7,5},{8,10},{10,8},{9,1... | collective-permute-start | bytes 1228808 | tf_op jit(solution)/shard_map/ppermute | solution.py:344
  7.6 13.6 %collective-permute-start.5 = (bf16[2,320,128]{2,1,0:T(8,128)(2,1)S(1)}, bf16[2,320,128]{2,1,0:T(8,128)(2,1)S(1)}, u32[]{:S(2)}, u32[]{:S(2)}) collective-permute-start(bf16[2,320,128]{2,1,0:T(8,128)(2,1)S(1)} %get-tuple-element.86), channel_id=1, source_target_pairs={{0,2},{2,0},{4,6},{6,4},{8,10},{10,8},{12,14},{14,12},{1,3},{3,1},... | collective-permute-start | bytes 491528 | tf_op jit(solution)/shard_map/ppermute | solution.py:354
  7.7 13.6 %collective-permute-start.4 = (bf16[2,320,128]{2,1,0:T(8,128)(2,1)S(1)}, bf16[2,320,128]{2,1,0:T(8,128)(2,1)S(1)}, u32[]{:S(2)}, u32[]{:S(2)}) collective-permute-start(bf16[2,320,128]{2,1,0:T(8,128)(2,1)S(1)} %get-tuple-element.83), channel_id=1, source_target_pairs={{0,12},{2,14},{4,0},{6,2},{8,4},{10,6},{12,8},{14,10},{1,13},{3,15... | collective-permute-start | bytes 491528 | tf_op jit(solution)/shard_map/ppermute | solution.py:354
  11.8 9.5 %collective-permute-start.2 = (bf16[2,320,128]{2,1,0:T(8,128)(2,1)S(1)}, bf16[2,320,128]{2,1,0:T(8,128)(2,1)S(1)}, u32[]{:S(2)}, u32[]{:S(2)}) collective-permute-start(bf16[2,320,128]{2,1,0:T(8,128)(2,1)S(1)} %get-tuple-element.79), channel_id=1, source_target_pairs={{0,4},{2,6},{4,8},{6,10},{8,12},{10,14},{12,0},{14,2},{1,5},{3,7},... | collective-permute-start | bytes 491528 | tf_op jit(solution)/shard_map/ppermute | solution.py:354
  11.8 14.0 %collective-permute-start.3 = (bf16[2,320,128]{2,1,0:T(8,128)(2,1)S(1)}, bf16[2,320,128]{2,1,0:T(8,128)(2,1)S(1)}, u32[]{:S(2)}, u32[]{:S(2)}) collective-permute-start(bf16[2,320,128]{2,1,0:T(8,128)(2,1)S(1)} %get-tuple-element.81), channel_id=1, source_target_pairs={{0,8},{2,10},{4,12},{6,14},{8,0},{10,2},{12,4},{14,6},{1,9},{3,11}... | collective-permute-start | bytes 491528 | tf_op jit(solution)/shard_map/ppermute | solution.py:354
  25.7 10.6 %collective-permute-start.6 = (bf16[160,1280]{1,0:T(8,128)(2,1)S(1)}, bf16[160,1280]{1,0:T(8,128)(2,1)S(1)}, u32[]{:S(2)}, u32[]{:S(2)}) collective-permute-start(bf16[160,1280]{1,0:T(8,128)(2,1)S(1)} %collective-permute-done.1.refs_1_), channel_id=1, source_target_pairs={{0,16},{16,0},{1,17},{17,1},{2,18},{18,2},{3,19},{19,3},{4,20},{20... | collective-permute-start | bytes 1228808 | tf_op jit(solution)/shard_map/ppermute | solution.py:344
  27.3 10.3 %collective-permute-start.7 = (bf16[2,320,128]{2,1,0:T(8,128)(2,1)S(1)}, bf16[2,320,128]{2,1,0:T(8,128)(2,1)S(1)}, u32[]{:S(2)}, u32[]{:S(2)}) collective-permute-start(bf16[2,320,128]{2,1,0:T(8,128)(2,1)S(1)} %get-tuple-element.91), channel_id=1, source_target_pairs={{0,6},{2,4},{4,10},{6,8},{8,14},{10,12},{12,2},{14,0},{1,7},{3,5},... | collective-permute-start | bytes 491528 | tf_op jit(solution)/shard_map/ppermute | solution.py:354
  28.0 9.5 %collective-permute-start.9 = (bf16[2,320,128]{2,1,0:T(8,128)(2,1)S(1)}, bf16[2,320,128]{2,1,0:T(8,128)(2,1)S(1)}, u32[]{:S(2)}, u32[]{:S(2)}) collective-permute-start(bf16[2,320,128]{2,1,0:T(8,128)(2,1)S(1)} %get-tuple-element.93), channel_id=1, source_target_pairs={{0,14},{2,12},{4,2},{6,0},{8,6},{10,4},{12,10},{14,8},{1,15},{3,13... | collective-permute-start | bytes 491528 | tf_op jit(solution)/shard_map/ppermute | solution.py:354
  32.0 12.5 %collective-permute-start.8 = (bf16[2,320,128]{2,1,0:T(8,128)(2,1)S(1)}, bf16[2,320,128]{2,1,0:T(8,128)(2,1)S(1)}, u32[]{:S(2)}, u32[]{:S(2)}) collective-permute-start(bf16[2,320,128]{2,1,0:T(8,128)(2,1)S(1)} %get-tuple-element.92), channel_id=1, source_target_pairs={{0,10},{2,8},{4,14},{6,12},{8,2},{10,0},{12,6},{14,4},{1,11},{3,9}... | collective-permute-start | bytes 491528 | tf_op jit(solution)/shard_map/ppermute | solution.py:354
  44.5 2.3 %collective-permute-start.10 = (bf16[320,1280]{1,0:T(8,128)(2,1)S(1)}, bf16[320,1280]{1,0:T(8,128)(2,1)S(1)}, u32[]{:S(2)}, u32[]{:S(2)}) collective-permute-start(bf16[320,1280]{1,0:T(8,128)(2,1)S(1)} %split_table.3.refs_3_.refs_7_), channel_id=1, source_target_pairs={{0,1},{1,0},{2,3},{3,2},{4,5},{5,4},{6,7},{7,6},{8,9},{9,8},{10,11... | collective-permute-start | bytes 2457608 | tf_op jit(solution)/shard_map/ppermute | solution.py:344
  50.3 6.6 %collective-permute-start.11 = (bf16[2,320,128]{2,1,0:T(8,128)(2,1)S(1)}, bf16[2,320,128]{2,1,0:T(8,128)(2,1)S(1)}, u32[]{:S(2)}, u32[]{:S(2)}) collective-permute-start(bf16[2,320,128]{2,1,0:T(8,128)(2,1)S(1)} %get-tuple-element.107), channel_id=1, source_target_pairs={{0,2},{2,0},{4,6},{6,4},{8,10},{10,8},{12,14},{14,12},{1,3},{3,1},... | collective-permute-start | bytes 491528 | tf_op jit(solution)/shard_map/ppermute | solution.py:354
  51.9 8.9 %collective-permute-start.12 = (bf16[2,320,128]{2,1,0:T(8,128)(2,1)S(1)}, bf16[2,320,128]{2,1,0:T(8,128)(2,1)S(1)}, u32[]{:S(2)}, u32[]{:S(2)}) collective-permute-start(bf16[2,320,128]{2,1,0:T(8,128)(2,1)S(1)} %get-tuple-element.111), channel_id=1, source_target_pairs={{0,4},{2,6},{4,8},{6,10},{8,12},{10,14},{12,0},{14,2},{1,5},{3,7},... | collective-permute-start | bytes 491528 | tf_op jit(solution)/shard_map/ppermute | solution.py:354
  51.9 10.9 %collective-permute-start.16 = (bf16[2,320,128]{2,1,0:T(8,128)(2,1)S(1)}, bf16[2,320,128]{2,1,0:T(8,128)(2,1)S(1)}, u32[]{:S(2)}, u32[]{:S(2)}) collective-permute-start(bf16[2,320,128]{2,1,0:T(8,128)(2,1)S(1)} %get-tuple-element.117), channel_id=1, source_target_pairs={{0,12},{2,14},{4,0},{6,2},{8,4},{10,6},{12,8},{14,10},{1,13},{3,15... | collective-permute-start | bytes 491528 | tf_op jit(solution)/shard_map/ppermute | solution.py:354
  56.9 7.1 %collective-permute-start.18 = (bf16[640,128]{1,0:T(8,128)(2,1)S(1)}, bf16[640,128]{1,0:T(8,128)(2,1)S(1)}, u32[]{:S(2)}, u32[]{:S(2)}) collective-permute-start(bf16[640,128]{1,0:T(8,128)(2,1)S(1)} %get-tuple-element.120.refs_2_), channel_id=1, source_target_pairs={{0,2},{2,0},{1,3},{3,1},{4,6},{6,4},{5,7},{7,5},{8,10},{10,8},{9,1... | collective-permute-start | bytes 491528 | tf_op jit(solution)/shard_map/ppermute | solution.py:344
  58.4 9.6 %collective-permute-start.19 = (bf16[640,128]{1,0:T(8,128)(2,1)S(1)}, bf16[640,128]{1,0:T(8,128)(2,1)S(1)}, u32[]{:S(2)}, u32[]{:S(2)}) collective-permute-start(bf16[640,128]{1,0:T(8,128)(2,1)S(1)} %get-tuple-element.121.refs_4_), channel_id=1, source_target_pairs={{0,2},{2,0},{1,3},{3,1},{4,6},{6,4},{5,7},{7,5},{8,10},{10,8},{9,1... | collective-permute-start | bytes 491528 | tf_op jit(solution)/shard_map/ppermute | solution.py:344
  59.0 18.1 %collective-permute-start.14 = (bf16[2,320,128]{2,1,0:T(8,128)(2,1)S(1)}, bf16[2,320,128]{2,1,0:T(8,128)(2,1)S(1)}, u32[]{:S(2)}, u32[]{:S(2)}) collective-permute-start(bf16[2,320,128]{2,1,0:T(8,128)(2,1)S(1)} %get-tuple-element.114), channel_id=1, source_target_pairs={{0,8},{2,10},{4,12},{6,14},{8,0},{10,2},{12,4},{14,6},{1,9},{3,11}... | collective-permute-start | bytes 491528 | tf_op jit(solution)/shard_map/ppermute | solution.py:354
  60.8 20.3 %collective-permute-start.15 = (bf16[2,320,128]{2,1,0:T(8,128)(2,1)S(1)}, bf16[2,320,128]{2,1,0:T(8,128)(2,1)S(1)}, u32[]{:S(2)}, u32[]{:S(2)}) collective-permute-start(bf16[2,320,128]{2,1,0:T(8,128)(2,1)S(1)} %get-tuple-element.115), channel_id=1, source_target_pairs={{0,10},{2,8},{4,14},{6,12},{8,2},{10,0},{12,6},{14,4},{1,11},{3,9}... | collective-permute-start | bytes 491528 | tf_op jit(solution)/shard_map/ppermute | solution.py:354
  62.7 18.3 %collective-permute-start.13 = (bf16[2,320,128]{2,1,0:T(8,128)(2,1)S(1)}, bf16[2,320,128]{2,1,0:T(8,128)(2,1)S(1)}, u32[]{:S(2)}, u32[]{:S(2)}) collective-permute-start(bf16[2,320,128]{2,1,0:T(8,128)(2,1)S(1)} %get-tuple-element.113), channel_id=1, source_target_pairs={{0,6},{2,4},{4,10},{6,8},{8,14},{10,12},{12,2},{14,0},{1,7},{3,5},... | collective-permute-start | bytes 491528 | tf_op jit(solution)/shard_map/ppermute | solution.py:354
  64.1 17.0 %collective-permute-start.17 = (bf16[2,320,128]{2,1,0:T(8,128)(2,1)S(1)}, bf16[2,320,128]{2,1,0:T(8,128)(2,1)S(1)}, u32[]{:S(2)}, u32[]{:S(2)}) collective-permute-start(bf16[2,320,128]{2,1,0:T(8,128)(2,1)S(1)} %get-tuple-element.119), channel_id=1, source_target_pairs={{0,14},{2,12},{4,2},{6,0},{8,6},{10,4},{12,10},{14,8},{1,15},{3,13... | collective-permute-start | bytes 491528 | tf_op jit(solution)/shard_map/ppermute | solution.py:354
where the time goes:
time: 83.7 us; the launch traced here: 83.5 us
  waiting for transfers between devices  37.5 us (45%)
  starting transfers between devices  27.3 us (33%)
  Pallas kernels  15.6 us (19%)
  local copies, waits for them, and re-layouts  1.61 us (2%)
  between operations  1.42 us (2%)
    ppermute x14, waiting for transfers between devices, moved(): return lax.ppermute(value, ('wide', 'lev'), pairs)  31.3 us
    ppermute x14, starting transfers between devices, moved(): return lax.ppermute(value, ('wide', 'lev'), pairs)  20.6 us
    pallas_call x9, Pallas kernels, run(): pl.pallas_call(kernel, out_shape=out_shape, in_specs=[smem] * scalars + [...  15.6 us
    ppermute x6, starting transfers between devices, shifted(): lax.ppermute(value, axis, [(i, (i + step) % count) for i in range(count)])  6.64 us
    ppermute x6, waiting for transfers between devices, shifted(): lax.ppermute(value, axis, [(i, (i + step) % count) for i in range(count)])  6.25 us
  transfers between devices with their start and end apart: 20, of which 11 were waited for; matrix products, arithmetic and copies ran while one was open for 0% of the time, Pallas kernels for 12%

commit v1 on v0

--- a/solution.py
+++ b/solution.py
@@ -68,13 +68,6 @@
     return run
 
 
-def lane_order(lanes, lev, old, new):
-    levels = lanes // 4
-    part = lax.rem(new // (lanes // 2) + lev, 2)
-    field = (new // levels) % 2
-    return old == field * (lanes // 2) + 2 * (new % levels) + part
-
-
 def split_body(slots, fields, block, meta_ref, rows_ref, weight_ref, *outs):
     latitudes = weight_ref.shape[0]
     group = slots * fields
@@ -82,34 +75,19 @@
     out_row, in_row = iota2((size, size), 0), iota2((size, size), 1)
     pair = out_row // block
     slot = lax.rem(meta_ref[1] + pair // fields, slots)
-    order = picks(in_row == (out_row % block) * group + slot * fields + pair % fields)
-    lanes = fields * 128
-    parts = picks(lane_order(lanes, meta_ref[2], iota2((lanes, lanes), 0), iota2((lanes, lanes), 1)))
+    field = (meta_ref[2] + pair) % fields
+    order = picks(in_row == (out_row % block) * group + slot * fields + field)
     for first in range(0, latitudes, block):
         north = rows_ref[0, first * group : first * group + size, :]
         south = rows_ref[1, first * group : first * group + size, :]
         sorted_rows = dot32(order, jnp.concatenate((north, south), axis=1))
         up, down = sorted_rows[:, :128], sorted_rows[:, 128:]
         weight = weight_ref[first : first + block, :]
-        halves = []
-        for mixed in (up + down, up - down):
-            for shift in range(slots):
-                at = shift * fields * block
-                halves.append(jnp.concatenate(
-                    [
-                        (weight * mixed[at + f * block : at + f * block + block]).astype(jnp.bfloat16)
-                        for f in range(fields)
-                    ],
-                    axis=1,
-                ))
-        turned = dot32(jnp.concatenate(halves, axis=0), parts).astype(jnp.bfloat16)
-        for odd in range(2):
-            for shift in range(slots):
-                at = (odd * slots + shift) * block
-                for d in range(2):
-                    outs[shift * 2 + d][odd, first : first + block, :] = turned[
-                        at : at + block, d * 128 : d * 128 + 128
-                    ]
+        for odd, mixed in enumerate((up + down, up - down)):
+            for i, out_ref in enumerate(outs):
+                out_ref[odd, first : first + block, :] = (weight * mixed[i * block : i * block + block]).astype(
+                    jnp.bfloat16
+                )
 
 
 def by_parity(meta_ref, rows):
@@ -148,7 +126,7 @@
     own = levels // 2
     lane, row = iota2((levels, wide), 1), iota2((levels, wide), 0)
     owner = lax.rem(meta_ref[2] + lane // levels, 2)
-    spread = picks(row == owner * own + lane % own)
+    spread = picks(row == owner * own + lane % levels // 2)
     plain = picks(row == lane % levels)
     old, new = iota2((wide, wide), 0), iota2((wide, wide), 1)
 
@@ -156,9 +134,9 @@
         half = lax.dot_general(first, matrix, (((0,), (1,)), ((), ())), preferred_element_type=jnp.float32)
         return dot32(half.astype(jnp.bfloat16), last)
 
-    same = (old // own) % 2 == new // levels
+    same = old % 2 == new // levels
     in_ref[...] = jnp.where(same, turned(spread, to_ref[...], plain), 0.0).astype(jnp.bfloat16)
-    same = old // levels == (new // own) % 2
+    same = old // levels == new % 2
     out_ref[...] = jnp.where(same, turned(plain, from_ref[...], spread), 0.0).astype(jnp.bfloat16)
     wide, levs, flds = sizes
     rows = degree_total // (2 * levs * flds)
@@ -250,35 +228,11 @@
     out_row, in_row = iota2((size, size), 0), iota2((size, size), 1)
     place = out_row % group
     shift = lax.rem(meta_ref[1] - place // fields + slots, slots)
-    order = picks(in_row == (shift * fields + place % fields) * block + out_row // group)
-    both = 2 * lanes
-    turn = picks(lane_order(both, meta_ref[2], iota2((both, both), 1), iota2((both, both), 0)))
+    order = picks(in_row == (shift * fields + (place + meta_ref[2]) % fields) * block + out_row // group)
     for first in range(0, latitudes, block):
         at = slice(first, first + block)
-        stacked = jnp.concatenate(
-            [
-                jnp.concatenate([parts[shift * 2 + d][half, at, :] for d in range(2)], axis=1)
-                for half in range(2)
-                for shift in range(slots)
-            ],
-            axis=0,
-        )
-        turned = dot32(stacked, turn).astype(jnp.bfloat16)
-        halves = [
-            jnp.concatenate(
-                [
-                    turned[
-                        (half * slots + shift) * block : (half * slots + shift + 1) * block,
-                        field * lanes : field * lanes + lanes,
-                    ]
-                    for shift in range(slots)
-                    for field in range(fields)
-                ],
-                axis=0,
-            )
-            for half in range(2)
-        ]
-        result = dot32(order, jnp.concatenate(halves, axis=1)).astype(jnp.bfloat16)
+        stacked = [jnp.concatenate([part[half, at, :] for part in parts], axis=0) for half in range(2)]
+        result = dot32(order, jnp.concatenate(stacked, axis=1)).astype(jnp.bfloat16)
         for half in range(2):
             out_ref[half, first * group : first * group + size, :] = result[:, half * lanes : half * lanes + lanes]
         done = first + block
@@ -291,33 +245,23 @@
 def rows_body(sizes, block, meta_ref, *refs):
     wide, levs, flds = sizes
     own_refs, other_refs, out_ref = refs[:2], refs[2:4], refs[4]
-    total_rows, lanes = own_refs[0].shape
-    rows = total_rows // (2 * flds)
+    rows = own_refs[0].shape[0] // (2 * flds)
     fields = 2
     group = 2 * fields
     size = block * group
     out_row, in_row = iota2((size, size), 0), iota2((size, size), 1)
     place = out_row % group
     odd = (place // fields + meta_ref[0] % 2) % 2
-    order = picks(in_row == (odd * fields + place % fields) * block + out_row // group)
-    both = 2 * lanes
-    turn = picks(lane_order(both, meta_ref[2], iota2((both, both), 1), iota2((both, both), 0)))
+    order = picks(in_row == (odd * fields + (place + meta_ref[2]) % fields) * block + out_row // group)
     for d in range(levs):
         for g in range(flds):
             index = lax.rem(meta_ref[2] + d, levs) * flds + lax.rem(meta_ref[3] + g, flds)
-            halves = []
-            for odd in range(2):
-                at = slice((odd * flds + g) * rows, (odd * flds + g + 1) * rows)
-                halves.append(jnp.concatenate((own_refs[d][at, :], other_refs[1 - d][at, :]), axis=1))
-            turned = dot32(jnp.concatenate(halves, axis=0), turn).astype(jnp.bfloat16)
             for first in range(0, rows, block):
                 stacked = jnp.concatenate(
                     [
-                        turned[
-                            odd * rows + first : odd * rows + first + block, field * lanes : field * lanes + lanes
-                        ]
+                        ref[(odd * flds + g) * rows + first : (odd * flds + g) * rows + first + block, :]
                         for odd in range(2)
-                        for field in range(fields)
+                        for ref in (own_refs[d], other_refs[1 - d])
                     ],
                     axis=0,
                 )

time: 83.7 us -> 82.8 us (0.989)
  Pallas kernels: 15.6 us -> 14.4 us
    pallas_call x9, Pallas kernels: 15.6 us -> 14.4 us  [run(): pl.pallas_call(kernel, out_shape=out_shape, in_specs=[smem] * scalars + [...]
  transfers between devices with their start and end apart: 20 -> 20, of which waited for: 11 -> 11; matrix products, arithmetic and copies ran while one was open for 0% -> 0% of each run, Pallas kernels for 12% -> 11%
where the time goes in v1:
time: 82.8 us; the launch traced here: 82.7 us
  waiting for transfers between devices  37.9 us (46%)
  starting transfers between devices  27.3 us (33%)
  Pallas kernels  14.4 us (17%)
  local copies, waits for them, and re-layouts  1.61 us (2%)
  between operations  1.42 us (2%)
    ppermute x14, waiting for transfers between devices, moved(): return lax.ppermute(value, ('wide', 'lev'), pairs)  31.7 us
    ppermute x14, starting transfers between devices, moved(): return lax.ppermute(value, ('wide', 'lev'), pairs)  20.7 us
    pallas_call x9, Pallas kernels, run(): pl.pallas_call(kernel, out_shape=out_shape, in_specs=[smem] * scalars + [...  14.4 us
    ppermute x6, starting transfers between devices, shifted(): lax.ppermute(value, axis, [(i, (i + step) % count) for i in range(count)])  6.65 us
    ppermute x6, waiting for transfers between devices, shifted(): lax.ppermute(value, axis, [(i, (i + step) % count) for i in range(count)])  6.21 us
  transfers between devices with their start and end apart: 20, of which 11 were waited for; matrix products, arithmetic and copies ran while one was open for 0% of the time, Pallas kernels for 11%

profile of v1, /device:TPU:0, one launch (start us, length us, event | category | flops | bytes accessed | tf_op | source)
XLA Modules:
  0.0 82.7 jit_solution(15043776937262064782)
XLA Ops:
  0.6 0.5 collective-permute-start
  1.8 0.1 stack.19.refs_0_
  1.9 0.0 copy-start
  1.9 0.1 broadcast_in_dim.10.refs_2_
  2.0 0.0 copy-start.4
  2.1 1.4 %copy-done.4 = bf16[2,320,4,2,128]{4,3,2,1,0:T(2,128)(2,1)S(1)} copy-done((bf16[2,320,4,2,128]{4,3,2,1,0:T(2,128)(2,1)S(1)}, bf16[2,320,4,2,128]{4,3,2,1,0:T(2,128)(2,1)}, u32[]{:S(2)}) %copy-start.4) | copy-done | bytes 1310744
  3.4 1.1 %split_hemispheres.1 = (bf16[2,320,128]{2,1,0:T(8,128)(2,1)S(1)}, bf16[2,320,128]{2,1,0:T(8,128)(2,1)S(1)}, bf16[2,320,128]{2,1,0:T(8,128)(2,1)S(1)}, bf16[2,320...) custom-call(s32[5]{0:T(128)S(1)} %stack.19.refs_0_, ...), custom_call_target="tpu_custom_call" | custom-call | flops 671088640 | tf_op jit(solution)/shard_map/split_hemispheres/pallas_call | solution.py:55
  4.6 0.0 collective-permute-done.refs_2_
  4.6 2.6 %collective-permute-start.1 = (bf16[160,1280]{1,0:T(8,128)(2,1)S(1)}, bf16[160,1280]{1,0:T(8,128)(2,1)S(1)}, u32[]{:S(2)}, u32[]{:S(2)}) collective-permute-start(bf16[160,1280]{1,0:T(8,128)(2,1)S(1)} %constant_dynamic-slice_fusion), channel_id=1, source_target_pairs={{0,2},{2,0},{1,3},{3,1},{4,6},{6,4},{5,7},{7,5},{8,10},{10,8},{9,1... | collective-permute-start | bytes 1228808 | tf_op jit(solution)/shard_map/ppermute | solution.py:288
  7.2 0.1 collective-permute-start.5
  7.3 4.0 %collective-permute-start.4 = (bf16[2,320,128]{2,1,0:T(8,128)(2,1)S(1)}, bf16[2,320,128]{2,1,0:T(8,128)(2,1)S(1)}, u32[]{:S(2)}, u32[]{:S(2)}) collective-permute-start(bf16[2,320,128]{2,1,0:T(8,128)(2,1)S(1)} %get-tuple-element.83), channel_id=1, source_target_pairs={{0,12},{2,14},{4,0},{6,2},{8,4},{10,6},{12,8},{14,10},{1,13},{3,15... | collective-permute-start | bytes 491528 | tf_op jit(solution)/shard_map/ppermute | solution.py:298
  11.3 1.0 %collective-permute-start.3 = (bf16[2,320,128]{2,1,0:T(8,128)(2,1)S(1)}, bf16[2,320,128]{2,1,0:T(8,128)(2,1)S(1)}, u32[]{:S(2)}, u32[]{:S(2)}) collective-permute-start(bf16[2,320,128]{2,1,0:T(8,128)(2,1)S(1)} %get-tuple-element.81), channel_id=1, source_target_pairs={{0,8},{2,10},{4,12},{6,14},{8,0},{10,2},{12,4},{14,6},{1,9},{3,11}... | collective-permute-start | bytes 491528 | tf_op jit(solution)/shard_map/ppermute | solution.py:298
  12.4 1.1 %spread_modes.1 = (bf16[256,256]{1,0:T(8,128)(2,1)S(1)}, bf16[256,256]{1,0:T(8,128)(2,1)S(1)}, f32[1280,128]{1,0:T(8,128)S(1)}) custom-call(s32[5]{0:T(128)S(1)} %stack.19.refs_0_, bf16[128,128]{1,0:T(8,128)(2,1)S(1)} %copy-done.1, bf16[128,128]{1,0:T(8,128)(2,1)S(1)} %copy-done.2, f32[1,128]{1,0:T(1,128)S(1)} %bitcast.12, ...), custom_call_target="tpu_custom_call" | custom-call | flops 25165824 | tf_op jit(solution)/shard_map/spread_modes/pallas_call | solution.py:55
  13.5 1.6 %split_table.2 = (bf16[320,1280]{1,0:T(8,128)(2,1)S(1)}, bf16[320,1280]{1,0:T(8,128)(2,1)S(1)}) custom-call(s32[5]{0:T(128)S(1)} %stack.19.refs_0_, bf16[320,1280]{1,0:T(8,128)(2,1)S(1)} %bitcast.11, bf16[320,1280]{1,0:T(8,128)(2,1)S(1)} %collective-permute-done.refs_2_, f32[1280,128]{1,0:T(8,128)S(1)} %get-tuple-element.73.refs_3_.refs_2_), custom_call_target="tpu_custom_call" | custom-call | flops 524288000 | tf_op jit(solution)/shard_map/split_table/pallas_call | solution.py:55
  15.1 5.8 %collective-permute-done.5.refs_7_ = bf16[2,320,128]{2,1,0:T(8,128)(2,1)S(1)} collective-permute-done((bf16[2,320,128]{2,1,0:T(8,128)(2,1)S(1)}, bf16[2,320,128]{2,1,0:T(8,128)(2,1)S(1)}, u32[]{:S(2)}, u32[]{:S(2)}) %collective-permute-start.5) | collective-permute-done | bytes 163872 | tf_op jit(solution)/shard_map/ppermute | solution.py:298
  20.8 0.0 collective-permute-done.2.refs_8_
  20.9 4.5 %collective-permute-done.3.refs_10_ = bf16[2,320,128]{2,1,0:T(8,128)(2,1)S(1)} collective-permute-done((bf16[2,320,128]{2,1,0:T(8,128)(2,1)S(1)}, bf16[2,320,128]{2,1,0:T(8,128)(2,1)S(1)}, u32[]{:S(2)}, u32[]{:S(2)}) %collective-permute-start.3) | collective-permute-done | bytes 163872 | tf_op jit(solution)/shard_map/ppermute | solution.py:298
  25.3 1.5 %collective-permute-start.6 = (bf16[160,1280]{1,0:T(8,128)(2,1)S(1)}, bf16[160,1280]{1,0:T(8,128)(2,1)S(1)}, u32[]{:S(2)}, u32[]{:S(2)}) collective-permute-start(bf16[160,1280]{1,0:T(8,128)(2,1)S(1)} %collective-permute-done.1.refs_1_), channel_id=1, source_target_pairs={{0,16},{16,0},{1,17},{17,1},{2,18},{18,2},{3,19},{19,3},{4,20},{20... | collective-permute-start | bytes 1228808 | tf_op jit(solution)/shard_map/ppermute | solution.py:288
  26.8 0.8 collective-permute-start.7
  27.6 4.0 %collective-permute-start.9 = (bf16[2,320,128]{2,1,0:T(8,128)(2,1)S(1)}, bf16[2,320,128]{2,1,0:T(8,128)(2,1)S(1)}, u32[]{:S(2)}, u32[]{:S(2)}) collective-permute-start(bf16[2,320,128]{2,1,0:T(8,128)(2,1)S(1)} %get-tuple-element.93), channel_id=1, source_target_pairs={{0,14},{2,12},{4,2},{6,0},{8,6},{10,4},{12,10},{14,8},{1,15},{3,13... | collective-permute-start | bytes 491528 | tf_op jit(solution)/shard_map/ppermute | solution.py:298
  31.6 0.0 collective-permute-start.8
  31.6 4.3 %collective-permute-done.6.refs_2_ = bf16[160,1280]{1,0:T(8,128)(2,1)S(1)} collective-permute-done((bf16[160,1280]{1,0:T(8,128)(2,1)S(1)}, bf16[160,1280]{1,0:T(8,128)(2,1)S(1)}, u32[]{:S(2)}, u32[]{:S(2)}) %collective-permute-start.6) | collective-permute-done | bytes 409632 | tf_op jit(solution)/shard_map/ppermute | solution.py:288
  35.9 1.2 %split_table.3.refs_3_.refs_7_ = bf16[320,1280]{1,0:T(8,128)(2,1)S(1)} custom-call(s32[5]{0:T(128)S(1)} %stack.19.refs_0_, bf16[160,1280]{1,0:T(8,128)(2,1)S(1)} %collective-permute-done.1.refs_1_, bf16[160,1280]{1,0:T(8,128)(2,1)S(1)} %collective-permute-done.6.refs_2_), custom_call_target="tpu_custom_call" | custom-call | flops 262144000 | tf_op jit(solution)/shard_map/split_table/pallas_call | solution.py:55
  37.1 6.9 %collective-permute-done.8.refs_11_ = bf16[2,320,128]{2,1,0:T(8,128)(2,1)S(1)} collective-permute-done((bf16[2,320,128]{2,1,0:T(8,128)(2,1)S(1)}, bf16[2,320,128]{2,1,0:T(8,128)(2,1)S(1)}, u32[]{:S(2)}, u32[]{:S(2)}) %collective-permute-start.8) | collective-permute-done | bytes 163872 | tf_op jit(solution)/shard_map/ppermute | solution.py:298
  44.1 2.2 %direct_legendre_and_solve.2 = (bf16[640,128]{1,0:T(8,128)(2,1)S(1)}, bf16[640,128]{1,0:T(8,128)(2,1)S(1)}, bf16[2,1280,256]{2,1,0:T(8,128)(2,1)S(1)}) custom-call(s32[5]{0:T(128)S(1)} %stack.19.refs_0_, bf16[256,256]{1,0:T(8,128)(2,1)S(1)} %get-tuple-element.71.refs_1_.refs_0_, bf16[256,256]{1,0:T(8,128)(2,1)S(1)} %get-tuple-element.72.refs_2_.refs_1_, ...), custom_call_target="tpu_custom_call" | custom-call | flops 419430400 | tf_op jit(solution)/shard_map/direct_legendre_and_solve/pallas_call | solution.py:55
  46.3 0.1 collective-permute-done.10.refs_4_.refs_8_
  46.4 1.5 %direct_legendre_and_solve.3 = (bf16[640,128]{1,0:T(8,128)(2,1)S(1)}, bf16[640,128]{1,0:T(8,128)(2,1)S(1)}) custom-call(bf16[256,256]{1,0:T(8,128)(2,1)S(1)} %get-tuple-element.71.refs_1_.refs_0_, bf16[256,256]{1,0:T(8,128)(2,1)S(1)} %get-tuple-element.72.refs_2_.refs_1_, f32[1280,128]{1,0:T(8,128)S(1)} %get-tuple-element.73.refs_3_.refs_2_, ...), custom_call_target="tpu_custom_call" | custom-call | flops 419430400 | tf_op jit(solution)/shard_map/direct_legendre_and_solve/pallas_call | solution.py:55
  47.9 2.0 %inverse_legendre.1 = (bf16[2,320,128]{2,1,0:T(8,128)(2,1)S(1)}, bf16[2,320,128]{2,1,0:T(8,128)(2,1)S(1)}, bf16[2,320,128]{2,1,0:T(8,128)(2,1)S(1)}, bf16[2,320,...) custom-call(s32[5]{0:T(128)S(1)} %stack.19.refs_0_, ...), custom_call_target="tpu_custom_call" | custom-call | flops 838860800 | tf_op jit(solution)/shard_map/inverse_legendre/pallas_call | solution.py:55
  49.9 1.6 %collective-permute-start.11 = (bf16[2,320,128]{2,1,0:T(8,128)(2,1)S(1)}, bf16[2,320,128]{2,1,0:T(8,128)(2,1)S(1)}, u32[]{:S(2)}, u32[]{:S(2)}) collective-permute-start(bf16[2,320,128]{2,1,0:T(8,128)(2,1)S(1)} %get-tuple-element.107), channel_id=1, source_target_pairs={{0,2},{2,0},{4,6},{6,4},{8,10},{10,8},{12,14},{14,12},{1,3},{3,1},... | collective-permute-start | bytes 491528 | tf_op jit(solution)/shard_map/ppermute | solution.py:298
  51.5 0.0 collective-permute-start.12
  51.5 3.8 %collective-permute-start.16 = (bf16[2,320,128]{2,1,0:T(8,128)(2,1)S(1)}, bf16[2,320,128]{2,1,0:T(8,128)(2,1)S(1)}, u32[]{:S(2)}, u32[]{:S(2)}) collective-permute-start(bf16[2,320,128]{2,1,0:T(8,128)(2,1)S(1)} %get-tuple-element.117), channel_id=1, source_target_pairs={{0,12},{2,14},{4,0},{6,2},{8,4},{10,6},{12,8},{14,10},{1,13},{3,15... | collective-permute-start | bytes 491528 | tf_op jit(solution)/shard_map/ppermute | solution.py:298
  55.3 1.2 %collective-permute-done.11.refs_2_ = bf16[2,320,128]{2,1,0:T(8,128)(2,1)S(1)} collective-permute-done((bf16[2,320,128]{2,1,0:T(8,128)(2,1)S(1)}, bf16[2,320,128]{2,1,0:T(8,128)(2,1)S(1)}, u32[]{:S(2)}, u32[]{:S(2)}) %collective-permute-start.11) | collective-permute-done | bytes 163872 | tf_op jit(solution)/shard_map/ppermute | solution.py:298
  56.5 1.4 %collective-permute-start.18 = (bf16[640,128]{1,0:T(8,128)(2,1)S(1)}, bf16[640,128]{1,0:T(8,128)(2,1)S(1)}, u32[]{:S(2)}, u32[]{:S(2)}) collective-permute-start(bf16[640,128]{1,0:T(8,128)(2,1)S(1)} %get-tuple-element.120.refs_2_), channel_id=1, source_target_pairs={{0,2},{2,0},{1,3},{3,1},{4,6},{6,4},{5,7},{7,5},{8,10},{10,8},{9,1... | collective-permute-start | bytes 491528 | tf_op jit(solution)/shard_map/ppermute | solution.py:288
  58.0 0.6 collective-permute-start.19
  58.6 0.0 collective-permute-start.14
  58.6 1.8 %collective-permute-done.12.refs_3_ = bf16[2,320,128]{2,1,0:T(8,128)(2,1)S(1)} collective-permute-done((bf16[2,320,128]{2,1,0:T(8,128)(2,1)S(1)}, bf16[2,320,128]{2,1,0:T(8,128)(2,1)S(1)}, u32[]{:S(2)}, u32[]{:S(2)}) %collective-permute-start.12) | collective-permute-done | bytes 163872 | tf_op jit(solution)/shard_map/ppermute | solution.py:298
  60.4 2.0 %collective-permute-start.15 = (bf16[2,320,128]{2,1,0:T(8,128)(2,1)S(1)}, bf16[2,320,128]{2,1,0:T(8,128)(2,1)S(1)}, u32[]{:S(2)}, u32[]{:S(2)}) collective-permute-start(bf16[2,320,128]{2,1,0:T(8,128)(2,1)S(1)} %get-tuple-element.115), channel_id=1, source_target_pairs={{0,10},{2,8},{4,14},{6,12},{8,2},{10,0},{12,6},{14,4},{1,11},{3,9}... | collective-permute-start | bytes 491528 | tf_op jit(solution)/shard_map/ppermute | solution.py:298
  62.3 0.0 collective-permute-done.16.refs_7_
  62.4 0.0 collective-permute-start.13
  62.4 1.3 %collective-permute-done.18.refs_3_ = bf16[640,128]{1,0:T(8,128)(2,1)S(1)} collective-permute-done((bf16[640,128]{1,0:T(8,128)(2,1)S(1)}, bf16[640,128]{1,0:T(8,128)(2,1)S(1)}, u32[]{:S(2)}, u32[]{:S(2)}) %collective-permute-start.18) | collective-permute-done | bytes 163872 | tf_op jit(solution)/shard_map/ppermute | solution.py:288
  63.6 3.4 %collective-permute-start.17 = (bf16[2,320,128]{2,1,0:T(8,128)(2,1)S(1)}, bf16[2,320,128]{2,1,0:T(8,128)(2,1)S(1)}, u32[]{:S(2)}, u32[]{:S(2)}) collective-permute-start(bf16[2,320,128]{2,1,0:T(8,128)(2,1)S(1)} %get-tuple-element.119), channel_id=1, source_target_pairs={{0,14},{2,12},{4,2},{6,0},{8,6},{10,4},{12,10},{14,8},{1,15},{3,13... | collective-permute-start | bytes 491528 | tf_op jit(solution)/shard_map/ppermute | solution.py:298
  67.1 0.5 collective-permute-done.19.refs_4_
  67.5 1.8 %order_spectral.1 = bf16[2560,128]{1,0:T(8,128)(2,1)} custom-call(s32[5]{0:T(128)S(1)} %stack.19.refs_0_, bf16[640,128]{1,0:T(8,128)(2,1)S(1)} %get-tuple-element.99.refs_1_, bf16[640,128]{1,0:T(8,128)(2,1)S(1)} %get-tuple-element.103.refs_3_.refs_2_, bf16[640,128]{1,0:T(8,128)(2,1)S(1)} %collective-permute-done.18.refs_3_, ...), custom_call_target="tpu_custom_call" | custom-call | flops 671088640 | tf_op jit(solution)/shard_map/order_spectral/pallas_call | solution.py:55
  69.3 7.4 %collective-permute-done.14.refs_5_ = bf16[2,320,128]{2,1,0:T(8,128)(2,1)S(1)} collective-permute-done((bf16[2,320,128]{2,1,0:T(8,128)(2,1)S(1)}, bf16[2,320,128]{2,1,0:T(8,128)(2,1)S(1)}, u32[]{:S(2)}, u32[]{:S(2)}) %collective-permute-start.14) | collective-permute-done | bytes 163872 | tf_op jit(solution)/shard_map/ppermute | solution.py:298
  76.7 4.0 %collective-permute-done.15.refs_6_ = bf16[2,320,128]{2,1,0:T(8,128)(2,1)S(1)} collective-permute-done((bf16[2,320,128]{2,1,0:T(8,128)(2,1)S(1)}, bf16[2,320,128]{2,1,0:T(8,128)(2,1)S(1)}, u32[]{:S(2)}, u32[]{:S(2)}) %collective-permute-start.15) | collective-permute-done | bytes 163872 | tf_op jit(solution)/shard_map/ppermute | solution.py:298
  80.7 0.0 collective-permute-done.13.refs_4_
  80.7 0.0 collective-permute-done.17.refs_8_
  80.7 2.0 %join_hemispheres.1 = bf16[2,2560,128]{2,1,0:T(8,128)(2,1)} custom-call(s32[5]{0:T(128)S(1)} %stack.19.refs_0_, bf16[2,320,128]{2,1,0:T(8,128)(2,1)S(1)} %get-tuple-element.105.refs_1_, bf16[2,320,128]{2,1,0:T(8,128)(2,1)S(1)} %collective-permute-done.11.refs_2_, bf16[2,320,128]{2,1,0:T(8,128)(2,1)S(1)} %collective-permute-done.12.refs_3_, ...), custom_call_target="tpu_custom_call" | custom-call | flops 671088640 | tf_op jit(solution)/shard_map/join_hemispheres/pallas_call | solution.py:55
  (15 shorter events, 0.1 us)
Async XLA Ops:
  0.6 3.9 %collective-permute-start = (bf16[320,1280]{1,0:T(8,128)(2,1)}, bf16[320,1280]{1,0:T(8,128)(2,1)S(1)}, u32[]{:S(2)}, u32[]{:S(2)}) collective-permute-start(bf16[320,1280]{1,0:T(8,128)(2,1)} %bitcast.9), channel_id=1, source_target_pairs={{0,1},{1,0},{2,3},{3,2},{4,5},{5,4},{6,7},{7,6},{8,9},{9,8},{10,11... | collective-permute-start | bytes 2457608 | tf_op jit(solution)/shard_map/ppermute | solution.py:288
  1.9 2.6 %copy-start = (bf16[1,320,1280]{2,1,0:T(8,128)(2,1)S(1)}, bf16[1,320,1280]{2,1,0:T(8,128)(2,1)}, u32[]{:S(2)}) copy-start(bf16[1,320,1280]{2,1,0:T(8,128)(2,1)} %param.7) | copy-start | bytes 2457604
  2.0 1.4 %copy-start.4 = (bf16[2,320,4,2,128]{4,3,2,1,0:T(2,128)(2,1)S(1)}, bf16[2,320,4,2,128]{4,3,2,1,0:T(2,128)(2,1)}, u32[]{:S(2)}) copy-start(bf16[2,320,4,2,128]{4,3,2,1,0:T(2,128)(2,1)} %param.6) | copy-start | bytes 3932164
  3.4 8.9 %copy-start.1 = (bf16[128,128]{1,0:T(8,128)(2,1)S(1)}, bf16[128,128]{1,0:T(8,128)(2,1)}, u32[]{:S(2)}) copy-start(bf16[128,128]{1,0:T(8,128)(2,1)} %refs_1_.1) | copy-start | bytes 98308
  3.4 8.9 %copy-start.2 = (bf16[128,128]{1,0:T(8,128)(2,1)S(1)}, bf16[128,128]{1,0:T(8,128)(2,1)}, u32[]{:S(2)}) copy-start(bf16[128,128]{1,0:T(8,128)(2,1)} %refs_2_.1) | copy-start | bytes 98308
  3.4 8.9 %copy-start.3 = (f32[128]{0:T(128)S(1)}, f32[128]{0:T(128)}, u32[]{:S(2)}) copy-start(f32[128]{0:T(128)} %param.11) | copy-start | bytes 1540
  4.6 20.7 %collective-permute-start.1 = (bf16[160,1280]{1,0:T(8,128)(2,1)S(1)}, bf16[160,1280]{1,0:T(8,128)(2,1)S(1)}, u32[]{:S(2)}, u32[]{:S(2)}) collective-permute-start(bf16[160,1280]{1,0:T(8,128)(2,1)S(1)} %constant_dynamic-slice_fusion), channel_id=1, source_target_pairs={{0,2},{2,0},{1,3},{3,1},{4,6},{6,4},{5,7},{7,5},{8,10},{10,8},{9,1... | collective-permute-start | bytes 1228808 | tf_op jit(solution)/shard_map/ppermute | solution.py:288
  7.2 13.6 %collective-permute-start.5 = (bf16[2,320,128]{2,1,0:T(8,128)(2,1)S(1)}, bf16[2,320,128]{2,1,0:T(8,128)(2,1)S(1)}, u32[]{:S(2)}, u32[]{:S(2)}) collective-permute-start(bf16[2,320,128]{2,1,0:T(8,128)(2,1)S(1)} %get-tuple-element.86), channel_id=1, source_target_pairs={{0,2},{2,0},{4,6},{6,4},{8,10},{10,8},{12,14},{14,12},{1,3},{3,1},... | collective-permute-start | bytes 491528 | tf_op jit(solution)/shard_map/ppermute | solution.py:298
  7.3 13.6 %collective-permute-start.4 = (bf16[2,320,128]{2,1,0:T(8,128)(2,1)S(1)}, bf16[2,320,128]{2,1,0:T(8,128)(2,1)S(1)}, u32[]{:S(2)}, u32[]{:S(2)}) collective-permute-start(bf16[2,320,128]{2,1,0:T(8,128)(2,1)S(1)} %get-tuple-element.83), channel_id=1, source_target_pairs={{0,12},{2,14},{4,0},{6,2},{8,4},{10,6},{12,8},{14,10},{1,13},{3,15... | collective-permute-start | bytes 491528 | tf_op jit(solution)/shard_map/ppermute | solution.py:298
  11.3 9.5 %collective-permute-start.2 = (bf16[2,320,128]{2,1,0:T(8,128)(2,1)S(1)}, bf16[2,320,128]{2,1,0:T(8,128)(2,1)S(1)}, u32[]{:S(2)}, u32[]{:S(2)}) collective-permute-start(bf16[2,320,128]{2,1,0:T(8,128)(2,1)S(1)} %get-tuple-element.79), channel_id=1, source_target_pairs={{0,4},{2,6},{4,8},{6,10},{8,12},{10,14},{12,0},{14,2},{1,5},{3,7},... | collective-permute-start | bytes 491528 | tf_op jit(solution)/shard_map/ppermute | solution.py:298
  11.3 14.0 %collective-permute-start.3 = (bf16[2,320,128]{2,1,0:T(8,128)(2,1)S(1)}, bf16[2,320,128]{2,1,0:T(8,128)(2,1)S(1)}, u32[]{:S(2)}, u32[]{:S(2)}) collective-permute-start(bf16[2,320,128]{2,1,0:T(8,128)(2,1)S(1)} %get-tuple-element.81), channel_id=1, source_target_pairs={{0,8},{2,10},{4,12},{6,14},{8,0},{10,2},{12,4},{14,6},{1,9},{3,11}... | collective-permute-start | bytes 491528 | tf_op jit(solution)/shard_map/ppermute | solution.py:298
  25.3 10.6 %collective-permute-start.6 = (bf16[160,1280]{1,0:T(8,128)(2,1)S(1)}, bf16[160,1280]{1,0:T(8,128)(2,1)S(1)}, u32[]{:S(2)}, u32[]{:S(2)}) collective-permute-start(bf16[160,1280]{1,0:T(8,128)(2,1)S(1)} %collective-permute-done.1.refs_1_), channel_id=1, source_target_pairs={{0,16},{16,0},{1,17},{17,1},{2,18},{18,2},{3,19},{19,3},{4,20},{20... | collective-permute-start | bytes 1228808 | tf_op jit(solution)/shard_map/ppermute | solution.py:288
  26.8 10.3 %collective-permute-start.7 = (bf16[2,320,128]{2,1,0:T(8,128)(2,1)S(1)}, bf16[2,320,128]{2,1,0:T(8,128)(2,1)S(1)}, u32[]{:S(2)}, u32[]{:S(2)}) collective-permute-start(bf16[2,320,128]{2,1,0:T(8,128)(2,1)S(1)} %get-tuple-element.91), channel_id=1, source_target_pairs={{0,6},{2,4},{4,10},{6,8},{8,14},{10,12},{12,2},{14,0},{1,7},{3,5},... | collective-permute-start | bytes 491528 | tf_op jit(solution)/shard_map/ppermute | solution.py:298
  27.6 9.5 %collective-permute-start.9 = (bf16[2,320,128]{2,1,0:T(8,128)(2,1)S(1)}, bf16[2,320,128]{2,1,0:T(8,128)(2,1)S(1)}, u32[]{:S(2)}, u32[]{:S(2)}) collective-permute-start(bf16[2,320,128]{2,1,0:T(8,128)(2,1)S(1)} %get-tuple-element.93), channel_id=1, source_target_pairs={{0,14},{2,12},{4,2},{6,0},{8,6},{10,4},{12,10},{14,8},{1,15},{3,13... | collective-permute-start | bytes 491528 | tf_op jit(solution)/shard_map/ppermute | solution.py:298
  31.6 12.5 %collective-permute-start.8 = (bf16[2,320,128]{2,1,0:T(8,128)(2,1)S(1)}, bf16[2,320,128]{2,1,0:T(8,128)(2,1)S(1)}, u32[]{:S(2)}, u32[]{:S(2)}) collective-permute-start(bf16[2,320,128]{2,1,0:T(8,128)(2,1)S(1)} %get-tuple-element.92), channel_id=1, source_target_pairs={{0,10},{2,8},{4,14},{6,12},{8,2},{10,0},{12,6},{14,4},{1,11},{3,9}... | collective-permute-start | bytes 491528 | tf_op jit(solution)/shard_map/ppermute | solution.py:298
  44.1 2.3 %collective-permute-start.10 = (bf16[320,1280]{1,0:T(8,128)(2,1)S(1)}, bf16[320,1280]{1,0:T(8,128)(2,1)S(1)}, u32[]{:S(2)}, u32[]{:S(2)}) collective-permute-start(bf16[320,1280]{1,0:T(8,128)(2,1)S(1)} %split_table.3.refs_3_.refs_7_), channel_id=1, source_target_pairs={{0,1},{1,0},{2,3},{3,2},{4,5},{5,4},{6,7},{7,6},{8,9},{9,8},{10,11... | collective-permute-start | bytes 2457608 | tf_op jit(solution)/shard_map/ppermute | solution.py:288
  49.9 6.6 %collective-permute-start.11 = (bf16[2,320,128]{2,1,0:T(8,128)(2,1)S(1)}, bf16[2,320,128]{2,1,0:T(8,128)(2,1)S(1)}, u32[]{:S(2)}, u32[]{:S(2)}) collective-permute-start(bf16[2,320,128]{2,1,0:T(8,128)(2,1)S(1)} %get-tuple-element.107), channel_id=1, source_target_pairs={{0,2},{2,0},{4,6},{6,4},{8,10},{10,8},{12,14},{14,12},{1,3},{3,1},... | collective-permute-start | bytes 491528 | tf_op jit(solution)/shard_map/ppermute | solution.py:298
  51.5 8.9 %collective-permute-start.12 = (bf16[2,320,128]{2,1,0:T(8,128)(2,1)S(1)}, bf16[2,320,128]{2,1,0:T(8,128)(2,1)S(1)}, u32[]{:S(2)}, u32[]{:S(2)}) collective-permute-start(bf16[2,320,128]{2,1,0:T(8,128)(2,1)S(1)} %get-tuple-element.111), channel_id=1, source_target_pairs={{0,4},{2,6},{4,8},{6,10},{8,12},{10,14},{12,0},{14,2},{1,5},{3,7},... | collective-permute-start | bytes 491528 | tf_op jit(solution)/shard_map/ppermute | solution.py:298
  51.5 10.9 %collective-permute-start.16 = (bf16[2,320,128]{2,1,0:T(8,128)(2,1)S(1)}, bf16[2,320,128]{2,1,0:T(8,128)(2,1)S(1)}, u32[]{:S(2)}, u32[]{:S(2)}) collective-permute-start(bf16[2,320,128]{2,1,0:T(8,128)(2,1)S(1)} %get-tuple-element.117), channel_id=1, source_target_pairs={{0,12},{2,14},{4,0},{6,2},{8,4},{10,6},{12,8},{14,10},{1,13},{3,15... | collective-permute-start | bytes 491528 | tf_op jit(solution)/shard_map/ppermute | solution.py:298
  56.5 7.1 %collective-permute-start.18 = (bf16[640,128]{1,0:T(8,128)(2,1)S(1)}, bf16[640,128]{1,0:T(8,128)(2,1)S(1)}, u32[]{:S(2)}, u32[]{:S(2)}) collective-permute-start(bf16[640,128]{1,0:T(8,128)(2,1)S(1)} %get-tuple-element.120.refs_2_), channel_id=1, source_target_pairs={{0,2},{2,0},{1,3},{3,1},{4,6},{6,4},{5,7},{7,5},{8,10},{10,8},{9,1... | collective-permute-start | bytes 491528 | tf_op jit(solution)/shard_map/ppermute | solution.py:288
  58.0 9.6 %collective-permute-start.19 = (bf16[640,128]{1,0:T(8,128)(2,1)S(1)}, bf16[640,128]{1,0:T(8,128)(2,1)S(1)}, u32[]{:S(2)}, u32[]{:S(2)}) collective-permute-start(bf16[640,128]{1,0:T(8,128)(2,1)S(1)} %get-tuple-element.121.refs_4_), channel_id=1, source_target_pairs={{0,2},{2,0},{1,3},{3,1},{4,6},{6,4},{5,7},{7,5},{8,10},{10,8},{9,1... | collective-permute-start | bytes 491528 | tf_op jit(solution)/shard_map/ppermute | solution.py:288
  58.6 18.1 %collective-permute-start.14 = (bf16[2,320,128]{2,1,0:T(8,128)(2,1)S(1)}, bf16[2,320,128]{2,1,0:T(8,128)(2,1)S(1)}, u32[]{:S(2)}, u32[]{:S(2)}) collective-permute-start(bf16[2,320,128]{2,1,0:T(8,128)(2,1)S(1)} %get-tuple-element.114), channel_id=1, source_target_pairs={{0,8},{2,10},{4,12},{6,14},{8,0},{10,2},{12,4},{14,6},{1,9},{3,11}... | collective-permute-start | bytes 491528 | tf_op jit(solution)/shard_map/ppermute | solution.py:298
  60.4 20.3 %collective-permute-start.15 = (bf16[2,320,128]{2,1,0:T(8,128)(2,1)S(1)}, bf16[2,320,128]{2,1,0:T(8,128)(2,1)S(1)}, u32[]{:S(2)}, u32[]{:S(2)}) collective-permute-start(bf16[2,320,128]{2,1,0:T(8,128)(2,1)S(1)} %get-tuple-element.115), channel_id=1, source_target_pairs={{0,10},{2,8},{4,14},{6,12},{8,2},{10,0},{12,6},{14,4},{1,11},{3,9}... | collective-permute-start | bytes 491528 | tf_op jit(solution)/shard_map/ppermute | solution.py:298
  62.4 18.3 %collective-permute-start.13 = (bf16[2,320,128]{2,1,0:T(8,128)(2,1)S(1)}, bf16[2,320,128]{2,1,0:T(8,128)(2,1)S(1)}, u32[]{:S(2)}, u32[]{:S(2)}) collective-permute-start(bf16[2,320,128]{2,1,0:T(8,128)(2,1)S(1)} %get-tuple-element.113), channel_id=1, source_target_pairs={{0,6},{2,4},{4,10},{6,8},{8,14},{10,12},{12,2},{14,0},{1,7},{3,5},... | collective-permute-start | bytes 491528 | tf_op jit(solution)/shard_map/ppermute | solution.py:298
  63.6 17.1 %collective-permute-start.17 = (bf16[2,320,128]{2,1,0:T(8,128)(2,1)S(1)}, bf16[2,320,128]{2,1,0:T(8,128)(2,1)S(1)}, u32[]{:S(2)}, u32[]{:S(2)}) collective-permute-start(bf16[2,320,128]{2,1,0:T(8,128)(2,1)S(1)} %get-tuple-element.119), channel_id=1, source_target_pairs={{0,14},{2,12},{4,2},{6,0},{8,6},{10,4},{12,10},{14,8},{1,15},{3,13... | collective-permute-start | bytes 491528 | tf_op jit(solution)/shard_map/ppermute | solution.py:298

commit v2 on v1

--- a/solution.py
+++ b/solution.py
@@ -302,6 +302,7 @@
 
     wide_at, lev_at, fld_at = (lax.axis_index(axis) for axis in ("wide", "lev", "fld"))
     meta = jnp.stack((slot_wave[0], wide_at, lev_at, fld_at, lax.axis_index("ens"))).astype(jnp.int32)
+    place = jnp.stack((jnp.zeros_like(wide_at), wide_at, lev_at, fld_at)).astype(jnp.int32)
     position = (wide_at * latitudes + jnp.arange(latitudes, dtype=jnp.int32)).astype(jnp.float32)
     weights = jnp.sin(math.pi * (position + 0.5) / (2 * half_count))
     weights = jnp.broadcast_to(weights[:, None], (latitudes, lanes))
@@ -312,7 +313,7 @@
     blocks = call(
         functools.partial(split_body, slots, fields, block), (shape(2, latitudes, lanes),) * (wide * levs),
         "split_hemispheres", move_flops,
-    )(meta, fourier_input_rows.reshape(2, latitudes * group, lanes), weights)
+    )(place, fourier_input_rows.reshape(2, latitudes * group, lanes), weights)
     table_beside, *blocks = behind(table_beside, *blocks)
     *matrices, scale = call(
         functools.partial(modes_body, sizes, degree_count),
@@ -367,12 +368,10 @@
         "inverse_legendre", transform_flops, scratch=[pltpu.VMEM((2, half_count, columns), bf16)],
     )(meta, *near_spectral, *far_spectral, *near, *far)
     arrived = exchanged(grid, ())
-    others = [other for _, other in spectral]
-    arrived[0, 1], *others = behind(arrived[0, 1], *others)
     result = listed(arrived)
     spectral_rows = call(
         functools.partial(rows_body, sizes, 32), shape(degree_count * fields, lanes), "order_spectral", move_flops,
-    )(meta, *(own for own, _ in spectral), *(over_lev(other) for other in others))
+    )(meta, *(own for own, _ in spectral), *(over_lev(other) for _, other in spectral))
     fourier_rows = call(
         functools.partial(join_body, slots, 256 // group), shape(2, latitudes * group, lanes),
         "join_hemispheres", move_flops, out_hbm=True,

time: 82.8 us -> 82.7 us (level)
  waiting for transfers between devices: 37.9 us -> 36.8 us
    ppermute x6, waiting for transfers between devices: 6.21 us -> 4.47 us  [shifted(): lax.ppermute(value, axis, [(i, (i + step) % count) for i in range(count)])]
  transfers between devices with their start and end apart: 20 -> 20, of which waited for: 11 -> 9; matrix products, arithmetic and copies ran while one was open for 0% -> 0% of each run, Pallas kernels for 11% -> 12%
where the time goes in v2:
time: 82.7 us; the launch traced here: 82.4 us
  waiting for transfers between devices  36.8 us (44%)
  starting transfers between devices  26.5 us (32%)
  Pallas kernels  15.2 us (18%)
  local copies, waits for them, and re-layouts  2.36 us (3%)
  between operations  1.39 us (2%)
    ppermute x14, waiting for transfers between devices, moved(): return lax.ppermute(value, ('wide', 'lev'), pairs)  32.3 us
    ppermute x14, starting transfers between devices, moved(): return lax.ppermute(value, ('wide', 'lev'), pairs)  20 us
    pallas_call x9, Pallas kernels, run(): pl.pallas_call(kernel, out_shape=out_shape, in_specs=[smem] * scalars + [...  15.2 us
    ppermute x6, starting transfers between devices, shifted(): lax.ppermute(value, axis, [(i, (i + step) % count) for i in range(count)])  6.58 us
    ppermute x6, waiting for transfers between devices, shifted(): lax.ppermute(value, axis, [(i, (i + step) % count) for i in range(count)])  4.47 us
  transfers between devices with their start and end apart: 20, of which 9 were waited for; matrix products, arithmetic and copies ran while one was open for 0% of the time, Pallas kernels for 12%

profile of v2, /device:TPU:0, one launch (start us, length us, event | category | flops | bytes accessed | tf_op | source)
XLA Modules:
  0.0 82.4 jit_solution(5969382516029831916)
XLA Ops:
  0.6 0.5 collective-permute-start
  1.1 0.1 pad_add_fusion.refs_0_
  1.3 0.0 copy-start
  1.3 0.1 broadcast_in_dim.10.refs_2_
  1.4 0.0 copy-start.4
  1.4 1.4 %copy-done.4 = bf16[2,320,4,2,128]{4,3,2,1,0:T(2,128)(2,1)S(1)} copy-done((bf16[2,320,4,2,128]{4,3,2,1,0:T(2,128)(2,1)S(1)}, bf16[2,320,4,2,128]{4,3,2,1,0:T(2,128)(2,1)}, u32[]{:S(2)}) %copy-start.4) | copy-done | bytes 1310744
  2.8 1.9 %split_hemispheres.1 = (bf16[2,320,128]{2,1,0:T(8,128)(2,1)S(1)}, bf16[2,320,128]{2,1,0:T(8,128)(2,1)}, bf16[2,320,128]{2,1,0:T(8,128)(2,1)}, bf16[2,320,128]{2,...) custom-call(s32[4]{0:T(128)S(1)} %pad_add_fusion.refs_0_, ...), custom_call_target="tpu_custom_call" | custom-call | flops 671088640 | tf_op jit(solution)/shard_map/split_hemispheres/pallas_call | solution.py:55
  4.7 0.8 constant_dynamic-slice_fusion
  5.4 2.5 %collective-permute-start.1 = (bf16[160,1280]{1,0:T(8,128)(2,1)}, bf16[160,1280]{1,0:T(8,128)(2,1)S(1)}, u32[]{:S(2)}, u32[]{:S(2)}) collective-permute-start(bf16[160,1280]{1,0:T(8,128)(2,1)} %constant_dynamic-slice_fusion), channel_id=1, source_target_pairs={{0,2},{2,0},{1,3},{3,1},{4,6},{6,4},{5,7},{7,5},{8,10},{10,8},{9,1... | collective-permute-start | bytes 1228808 | tf_op jit(solution)/shard_map/ppermute | solution.py:288
  8.0 0.0 collective-permute-start.5
  8.0 4.1 %collective-permute-start.4 = (bf16[2,320,128]{2,1,0:T(8,128)(2,1)}, bf16[2,320,128]{2,1,0:T(8,128)(2,1)S(1)}, u32[]{:S(2)}, u32[]{:S(2)}) collective-permute-start(bf16[2,320,128]{2,1,0:T(8,128)(2,1)} %get-tuple-element.80), channel_id=1, source_target_pairs={{0,12},{2,14},{4,0},{6,2},{8,4},{10,6},{12,8},{14,10},{1,13},{3,15... | collective-permute-start | bytes 491528 | tf_op jit(solution)/shard_map/ppermute | solution.py:298
  12.1 0.0 collective-permute-start.2
  12.1 1.0 %collective-permute-start.3 = (bf16[2,320,128]{2,1,0:T(8,128)(2,1)}, bf16[2,320,128]{2,1,0:T(8,128)(2,1)S(1)}, u32[]{:S(2)}, u32[]{:S(2)}) collective-permute-start(bf16[2,320,128]{2,1,0:T(8,128)(2,1)} %get-tuple-element.78), channel_id=1, source_target_pairs={{0,8},{2,10},{4,12},{6,14},{8,0},{10,2},{12,4},{14,6},{1,9},{3,11}... | collective-permute-start | bytes 491528 | tf_op jit(solution)/shard_map/ppermute | solution.py:298
  13.8 0.1 stack.25.refs_0_
  13.9 1.1 %spread_modes.1 = (bf16[256,256]{1,0:T(8,128)(2,1)S(1)}, bf16[256,256]{1,0:T(8,128)(2,1)S(1)}, f32[1280,128]{1,0:T(8,128)S(1)}) custom-call(s32[5]{0:T(128)S(1)} %stack.25.refs_0_, bf16[128,128]{1,0:T(8,128)(2,1)S(1)} %copy-done.1, bf16[128,128]{1,0:T(8,128)(2,1)S(1)} %copy-done.2, f32[1,128]{1,0:T(1,128)S(1)} %bitcast.12, ...), custom_call_target="tpu_custom_call" | custom-call | flops 25165824 | tf_op jit(solution)/shard_map/spread_modes/pallas_call | solution.py:55
  15.0 1.5 %split_table.2 = (bf16[320,1280]{1,0:T(8,128)(2,1)S(1)}, bf16[320,1280]{1,0:T(8,128)(2,1)S(1)}) custom-call(s32[5]{0:T(128)S(1)} %stack.25.refs_0_, bf16[320,1280]{1,0:T(8,128)(2,1)S(1)} %bitcast.11, bf16[320,1280]{1,0:T(8,128)(2,1)S(1)} %collective-permute-done.refs_2_, f32[1280,128]{1,0:T(8,128)S(1)} %get-tuple-element.70.refs_3_.refs_2_), custom_call_target="tpu_custom_call" | custom-call | flops 524288000 | tf_op jit(solution)/shard_map/split_table/pallas_call | solution.py:55
  16.6 5.2 %collective-permute-done.5.refs_7_ = bf16[2,320,128]{2,1,0:T(8,128)(2,1)S(1)} collective-permute-done((bf16[2,320,128]{2,1,0:T(8,128)(2,1)}, bf16[2,320,128]{2,1,0:T(8,128)(2,1)S(1)}, u32[]{:S(2)}, u32[]{:S(2)}) %collective-permute-start.5) | collective-permute-done | bytes 163872 | tf_op jit(solution)/shard_map/ppermute | solution.py:298
  21.8 0.0 collective-permute-done.4.refs_12_
  21.8 0.0 collective-permute-done.2.refs_8_
  21.8 4.5 %collective-permute-done.3.refs_10_ = bf16[2,320,128]{2,1,0:T(8,128)(2,1)S(1)} collective-permute-done((bf16[2,320,128]{2,1,0:T(8,128)(2,1)}, bf16[2,320,128]{2,1,0:T(8,128)(2,1)S(1)}, u32[]{:S(2)}, u32[]{:S(2)}) %collective-permute-start.3) | collective-permute-done | bytes 163872 | tf_op jit(solution)/shard_map/ppermute | solution.py:298
  26.3 0.0 collective-permute-done.1.refs_1_
  26.3 1.5 %collective-permute-start.6 = (bf16[160,1280]{1,0:T(8,128)(2,1)S(1)}, bf16[160,1280]{1,0:T(8,128)(2,1)S(1)}, u32[]{:S(2)}, u32[]{:S(2)}) collective-permute-start(bf16[160,1280]{1,0:T(8,128)(2,1)S(1)} %collective-permute-done.1.refs_1_), channel_id=1, source_target_pairs={{0,16},{16,0},{1,17},{17,1},{2,18},{18,2},{3,19},{19,3},{4,20},{20... | collective-permute-start | bytes 1228808 | tf_op jit(solution)/shard_map/ppermute | solution.py:288
  27.8 0.9 %collective-permute-start.7 = (bf16[2,320,128]{2,1,0:T(8,128)(2,1)S(1)}, bf16[2,320,128]{2,1,0:T(8,128)(2,1)S(1)}, u32[]{:S(2)}, u32[]{:S(2)}) collective-permute-start(bf16[2,320,128]{2,1,0:T(8,128)(2,1)S(1)} %get-tuple-element.88), channel_id=1, source_target_pairs={{0,6},{2,4},{4,10},{6,8},{8,14},{10,12},{12,2},{14,0},{1,7},{3,5},... | collective-permute-start | bytes 491528 | tf_op jit(solution)/shard_map/ppermute | solution.py:298
  28.7 3.9 %collective-permute-start.9 = (bf16[2,320,128]{2,1,0:T(8,128)(2,1)S(1)}, bf16[2,320,128]{2,1,0:T(8,128)(2,1)S(1)}, u32[]{:S(2)}, u32[]{:S(2)}) collective-permute-start(bf16[2,320,128]{2,1,0:T(8,128)(2,1)S(1)} %get-tuple-element.90), channel_id=1, source_target_pairs={{0,14},{2,12},{4,2},{6,0},{8,6},{10,4},{12,10},{14,8},{1,15},{3,13... | collective-permute-start | bytes 491528 | tf_op jit(solution)/shard_map/ppermute | solution.py:298
  32.5 0.0 collective-permute-start.8
  32.5 4.3 %collective-permute-done.6.refs_2_ = bf16[160,1280]{1,0:T(8,128)(2,1)S(1)} collective-permute-done((bf16[160,1280]{1,0:T(8,128)(2,1)S(1)}, bf16[160,1280]{1,0:T(8,128)(2,1)S(1)}, u32[]{:S(2)}, u32[]{:S(2)}) %collective-permute-start.6) | collective-permute-done | bytes 409632 | tf_op jit(solution)/shard_map/ppermute | solution.py:288
  36.9 1.2 %split_table.3.refs_3_.refs_7_ = bf16[320,1280]{1,0:T(8,128)(2,1)S(1)} custom-call(s32[5]{0:T(128)S(1)} %stack.25.refs_0_, bf16[160,1280]{1,0:T(8,128)(2,1)S(1)} %collective-permute-done.1.refs_1_, bf16[160,1280]{1,0:T(8,128)(2,1)S(1)} %collective-permute-done.6.refs_2_), custom_call_target="tpu_custom_call" | custom-call | flops 262144000 | tf_op jit(solution)/shard_map/split_table/pallas_call | solution.py:55
  38.1 0.0 collective-permute-done.9.refs_13_
  38.1 6.9 %collective-permute-done.8.refs_11_ = bf16[2,320,128]{2,1,0:T(8,128)(2,1)S(1)} collective-permute-done((bf16[2,320,128]{2,1,0:T(8,128)(2,1)S(1)}, bf16[2,320,128]{2,1,0:T(8,128)(2,1)S(1)}, u32[]{:S(2)}, u32[]{:S(2)}) %collective-permute-start.8) | collective-permute-done | bytes 163872 | tf_op jit(solution)/shard_map/ppermute | solution.py:298
  45.0 2.2 %direct_legendre_and_solve.2 = (bf16[640,128]{1,0:T(8,128)(2,1)S(1)}, bf16[640,128]{1,0:T(8,128)(2,1)S(1)}, bf16[2,1280,256]{2,1,0:T(8,128)(2,1)S(1)}) custom-call(s32[5]{0:T(128)S(1)} %stack.25.refs_0_, bf16[256,256]{1,0:T(8,128)(2,1)S(1)} %get-tuple-element.68.refs_1_.refs_0_, bf16[256,256]{1,0:T(8,128)(2,1)S(1)} %get-tuple-element.69.refs_2_.refs_1_, ...), custom_call_target="tpu_custom_call" | custom-call | flops 419430400 | tf_op jit(solution)/shard_map/direct_legendre_and_solve/pallas_call | solution.py:55
  47.2 0.1 collective-permute-done.10.refs_4_.refs_8_
  47.4 1.5 %direct_legendre_and_solve.3 = (bf16[640,128]{1,0:T(8,128)(2,1)S(1)}, bf16[640,128]{1,0:T(8,128)(2,1)S(1)}) custom-call(bf16[256,256]{1,0:T(8,128)(2,1)S(1)} %get-tuple-element.68.refs_1_.refs_0_, bf16[256,256]{1,0:T(8,128)(2,1)S(1)} %get-tuple-element.69.refs_2_.refs_1_, f32[1280,128]{1,0:T(8,128)S(1)} %get-tuple-element.70.refs_3_.refs_2_, ...), custom_call_target="tpu_custom_call" | custom-call | flops 419430400 | tf_op jit(solution)/shard_map/direct_legendre_and_solve/pallas_call | solution.py:55
  48.8 2.0 %inverse_legendre.1 = (bf16[2,320,128]{2,1,0:T(8,128)(2,1)S(1)}, bf16[2,320,128]{2,1,0:T(8,128)(2,1)S(1)}, bf16[2,320,128]{2,1,0:T(8,128)(2,1)S(1)}, bf16[2,320,...) custom-call(s32[5]{0:T(128)S(1)} %stack.25.refs_0_, ...), custom_call_target="tpu_custom_call" | custom-call | flops 838860800 | tf_op jit(solution)/shard_map/inverse_legendre/pallas_call | solution.py:55
  50.9 1.5 %collective-permute-start.11 = (bf16[2,320,128]{2,1,0:T(8,128)(2,1)S(1)}, bf16[2,320,128]{2,1,0:T(8,128)(2,1)S(1)}, u32[]{:S(2)}, u32[]{:S(2)}) collective-permute-start(bf16[2,320,128]{2,1,0:T(8,128)(2,1)S(1)} %get-tuple-element.104), channel_id=1, source_target_pairs={{0,2},{2,0},{4,6},{6,4},{8,10},{10,8},{12,14},{14,12},{1,3},{3,1},... | collective-permute-start | bytes 491528 | tf_op jit(solution)/shard_map/ppermute | solution.py:298
  52.4 3.8 %collective-permute-start.16 = (bf16[2,320,128]{2,1,0:T(8,128)(2,1)S(1)}, bf16[2,320,128]{2,1,0:T(8,128)(2,1)S(1)}, u32[]{:S(2)}, u32[]{:S(2)}) collective-permute-start(bf16[2,320,128]{2,1,0:T(8,128)(2,1)S(1)} %get-tuple-element.113), channel_id=1, source_target_pairs={{0,12},{2,14},{4,0},{6,2},{8,4},{10,6},{12,8},{14,10},{1,13},{3,15... | collective-permute-start | bytes 491528 | tf_op jit(solution)/shard_map/ppermute | solution.py:298
  56.2 0.6 collective-permute-start.18
  56.8 1.5 %collective-permute-start.19 = (bf16[640,128]{1,0:T(8,128)(2,1)S(1)}, bf16[640,128]{1,0:T(8,128)(2,1)S(1)}, u32[]{:S(2)}, u32[]{:S(2)}) collective-permute-start(bf16[640,128]{1,0:T(8,128)(2,1)S(1)} %get-tuple-element.101.refs_4_), channel_id=1, source_target_pairs={{0,2},{2,0},{1,3},{3,1},{4,6},{6,4},{5,7},{7,5},{8,10},{10,8},{9,1... | collective-permute-start | bytes 491528 | tf_op jit(solution)/shard_map/ppermute | solution.py:288
  58.3 3.0 %collective-permute-done.12.refs_3_ = bf16[2,320,128]{2,1,0:T(8,128)(2,1)S(1)} collective-permute-done((bf16[2,320,128]{2,1,0:T(8,128)(2,1)S(1)}, bf16[2,320,128]{2,1,0:T(8,128)(2,1)S(1)}, u32[]{:S(2)}, u32[]{:S(2)}) %collective-permute-start.12) | collective-permute-done | bytes 163872 | tf_op jit(solution)/shard_map/ppermute | solution.py:298
  61.3 0.0 collective-permute-start.15
  61.3 2.3 %collective-permute-done.16.refs_7_ = bf16[2,320,128]{2,1,0:T(8,128)(2,1)S(1)} collective-permute-done((bf16[2,320,128]{2,1,0:T(8,128)(2,1)S(1)}, bf16[2,320,128]{2,1,0:T(8,128)(2,1)S(1)}, u32[]{:S(2)}, u32[]{:S(2)}) %collective-permute-start.16) | collective-permute-done | bytes 163872 | tf_op jit(solution)/shard_map/ppermute | solution.py:298
  63.6 0.0 collective-permute-start.13
  63.6 0.0 collective-permute-done.18.refs_3_
  63.6 4.7 %collective-permute-start.17 = (bf16[2,320,128]{2,1,0:T(8,128)(2,1)S(1)}, bf16[2,320,128]{2,1,0:T(8,128)(2,1)S(1)}, u32[]{:S(2)}, u32[]{:S(2)}) collective-permute-start(bf16[2,320,128]{2,1,0:T(8,128)(2,1)S(1)} %get-tuple-element.115), channel_id=1, source_target_pairs={{0,14},{2,12},{4,2},{6,0},{8,6},{10,4},{12,10},{14,8},{1,15},{3,13... | collective-permute-start | bytes 491528 | tf_op jit(solution)/shard_map/ppermute | solution.py:298
  68.3 1.8 %order_spectral.1 = bf16[2560,128]{1,0:T(8,128)(2,1)} custom-call(s32[5]{0:T(128)S(1)} %stack.25.refs_0_, bf16[640,128]{1,0:T(8,128)(2,1)S(1)} %get-tuple-element.96.refs_1_, bf16[640,128]{1,0:T(8,128)(2,1)S(1)} %get-tuple-element.100.refs_3_.refs_2_, bf16[640,128]{1,0:T(8,128)(2,1)S(1)} %collective-permute-done.18.refs_3_, ...), custom_call_target="tpu_custom_call" | custom-call | flops 671088640 | tf_op jit(solution)/shard_map/order_spectral/pallas_call | solution.py:55
  70.1 6.7 %collective-permute-done.14.refs_5_ = bf16[2,320,128]{2,1,0:T(8,128)(2,1)S(1)} collective-permute-done((bf16[2,320,128]{2,1,0:T(8,128)(2,1)S(1)}, bf16[2,320,128]{2,1,0:T(8,128)(2,1)S(1)}, u32[]{:S(2)}, u32[]{:S(2)}) %collective-permute-start.14) | collective-permute-done | bytes 163872 | tf_op jit(solution)/shard_map/ppermute | solution.py:298
  76.8 3.6 %collective-permute-done.15.refs_6_ = bf16[2,320,128]{2,1,0:T(8,128)(2,1)S(1)} collective-permute-done((bf16[2,320,128]{2,1,0:T(8,128)(2,1)S(1)}, bf16[2,320,128]{2,1,0:T(8,128)(2,1)S(1)}, u32[]{:S(2)}, u32[]{:S(2)}) %collective-permute-start.15) | collective-permute-done | bytes 163872 | tf_op jit(solution)/shard_map/ppermute | solution.py:298
  80.4 0.0 collective-permute-done.13.refs_4_
  80.4 2.0 %join_hemispheres.1 = bf16[2,2560,128]{2,1,0:T(8,128)(2,1)} custom-call(s32[5]{0:T(128)S(1)} %stack.25.refs_0_, bf16[2,320,128]{2,1,0:T(8,128)(2,1)S(1)} %get-tuple-element.102.refs_1_, bf16[2,320,128]{2,1,0:T(8,128)(2,1)S(1)} %collective-permute-done.11.refs_2_, bf16[2,320,128]{2,1,0:T(8,128)(2,1)S(1)} %collective-permute-done.12.refs_3_, ...), custom_call_target="tpu_custom_call" | custom-call | flops 671088640 | tf_op jit(solution)/shard_map/join_hemispheres/pallas_call | solution.py:55
  (16 shorter events, 0.1 us)
Async XLA Ops:
  0.6 4.0 %collective-permute-start = (bf16[320,1280]{1,0:T(8,128)(2,1)}, bf16[320,1280]{1,0:T(8,128)(2,1)S(1)}, u32[]{:S(2)}, u32[]{:S(2)}) collective-permute-start(bf16[320,1280]{1,0:T(8,128)(2,1)} %bitcast.9), channel_id=1, source_target_pairs={{0,1},{1,0},{2,3},{3,2},{4,5},{5,4},{6,7},{7,6},{8,9},{9,8},{10,11... | collective-permute-start | bytes 2457608 | tf_op jit(solution)/shard_map/ppermute | solution.py:288
  1.3 3.4 %copy-start = (bf16[1,320,1280]{2,1,0:T(8,128)(2,1)S(1)}, bf16[1,320,1280]{2,1,0:T(8,128)(2,1)}, u32[]{:S(2)}) copy-start(bf16[1,320,1280]{2,1,0:T(8,128)(2,1)} %param.7) | copy-start | bytes 2457604
  1.4 1.4 %copy-start.4 = (bf16[2,320,4,2,128]{4,3,2,1,0:T(2,128)(2,1)S(1)}, bf16[2,320,4,2,128]{4,3,2,1,0:T(2,128)(2,1)}, u32[]{:S(2)}) copy-start(bf16[2,320,4,2,128]{4,3,2,1,0:T(2,128)(2,1)} %param.6) | copy-start | bytes 3932164
  2.8 11.1 %copy-start.1 = (bf16[128,128]{1,0:T(8,128)(2,1)S(1)}, bf16[128,128]{1,0:T(8,128)(2,1)}, u32[]{:S(2)}) copy-start(bf16[128,128]{1,0:T(8,128)(2,1)} %refs_1_.1) | copy-start | bytes 98308
  2.8 11.1 %copy-start.2 = (bf16[128,128]{1,0:T(8,128)(2,1)S(1)}, bf16[128,128]{1,0:T(8,128)(2,1)}, u32[]{:S(2)}) copy-start(bf16[128,128]{1,0:T(8,128)(2,1)} %refs_2_.1) | copy-start | bytes 98308
  2.8 11.1 %copy-start.3 = (f32[128]{0:T(128)S(1)}, f32[128]{0:T(128)}, u32[]{:S(2)}) copy-start(f32[128]{0:T(128)} %param.11) | copy-start | bytes 1540
  5.4 20.8 %collective-permute-start.1 = (bf16[160,1280]{1,0:T(8,128)(2,1)}, bf16[160,1280]{1,0:T(8,128)(2,1)S(1)}, u32[]{:S(2)}, u32[]{:S(2)}) collective-permute-start(bf16[160,1280]{1,0:T(8,128)(2,1)} %constant_dynamic-slice_fusion), channel_id=1, source_target_pairs={{0,2},{2,0},{1,3},{3,1},{4,6},{6,4},{5,7},{7,5},{8,10},{10,8},{9,1... | collective-permute-start | bytes 1228808 | tf_op jit(solution)/shard_map/ppermute | solution.py:288
  8.0 13.8 %collective-permute-start.5 = (bf16[2,320,128]{2,1,0:T(8,128)(2,1)}, bf16[2,320,128]{2,1,0:T(8,128)(2,1)S(1)}, u32[]{:S(2)}, u32[]{:S(2)}) collective-permute-start(bf16[2,320,128]{2,1,0:T(8,128)(2,1)} %get-tuple-element.83), channel_id=1, source_target_pairs={{0,2},{2,0},{4,6},{6,4},{8,10},{10,8},{12,14},{14,12},{1,3},{3,1},... | collective-permute-start | bytes 491528 | tf_op jit(solution)/shard_map/ppermute | solution.py:298
  8.0 13.8 %collective-permute-start.4 = (bf16[2,320,128]{2,1,0:T(8,128)(2,1)}, bf16[2,320,128]{2,1,0:T(8,128)(2,1)S(1)}, u32[]{:S(2)}, u32[]{:S(2)}) collective-permute-start(bf16[2,320,128]{2,1,0:T(8,128)(2,1)} %get-tuple-element.80), channel_id=1, source_target_pairs={{0,12},{2,14},{4,0},{6,2},{8,4},{10,6},{12,8},{14,10},{1,13},{3,15... | collective-permute-start | bytes 491528 | tf_op jit(solution)/shard_map/ppermute | solution.py:298
  12.1 9.7 %collective-permute-start.2 = (bf16[2,320,128]{2,1,0:T(8,128)(2,1)}, bf16[2,320,128]{2,1,0:T(8,128)(2,1)S(1)}, u32[]{:S(2)}, u32[]{:S(2)}) collective-permute-start(bf16[2,320,128]{2,1,0:T(8,128)(2,1)} %get-tuple-element.76), channel_id=1, source_target_pairs={{0,4},{2,6},{4,8},{6,10},{8,12},{10,14},{12,0},{14,2},{1,5},{3,7},... | collective-permute-start | bytes 491528 | tf_op jit(solution)/shard_map/ppermute | solution.py:298
  12.1 14.2 %collective-permute-start.3 = (bf16[2,320,128]{2,1,0:T(8,128)(2,1)}, bf16[2,320,128]{2,1,0:T(8,128)(2,1)S(1)}, u32[]{:S(2)}, u32[]{:S(2)}) collective-permute-start(bf16[2,320,128]{2,1,0:T(8,128)(2,1)} %get-tuple-element.78), channel_id=1, source_target_pairs={{0,8},{2,10},{4,12},{6,14},{8,0},{10,2},{12,4},{14,6},{1,9},{3,11}... | collective-permute-start | bytes 491528 | tf_op jit(solution)/shard_map/ppermute | solution.py:298
  26.3 10.6 %collective-permute-start.6 = (bf16[160,1280]{1,0:T(8,128)(2,1)S(1)}, bf16[160,1280]{1,0:T(8,128)(2,1)S(1)}, u32[]{:S(2)}, u32[]{:S(2)}) collective-permute-start(bf16[160,1280]{1,0:T(8,128)(2,1)S(1)} %collective-permute-done.1.refs_1_), channel_id=1, source_target_pairs={{0,16},{16,0},{1,17},{17,1},{2,18},{18,2},{3,19},{19,3},{4,20},{20... | collective-permute-start | bytes 1228808 | tf_op jit(solution)/shard_map/ppermute | solution.py:288
  27.8 10.3 %collective-permute-start.7 = (bf16[2,320,128]{2,1,0:T(8,128)(2,1)S(1)}, bf16[2,320,128]{2,1,0:T(8,128)(2,1)S(1)}, u32[]{:S(2)}, u32[]{:S(2)}) collective-permute-start(bf16[2,320,128]{2,1,0:T(8,128)(2,1)S(1)} %get-tuple-element.88), channel_id=1, source_target_pairs={{0,6},{2,4},{4,10},{6,8},{8,14},{10,12},{12,2},{14,0},{1,7},{3,5},... | collective-permute-start | bytes 491528 | tf_op jit(solution)/shard_map/ppermute | solution.py:298
  28.7 9.4 %collective-permute-start.9 = (bf16[2,320,128]{2,1,0:T(8,128)(2,1)S(1)}, bf16[2,320,128]{2,1,0:T(8,128)(2,1)S(1)}, u32[]{:S(2)}, u32[]{:S(2)}) collective-permute-start(bf16[2,320,128]{2,1,0:T(8,128)(2,1)S(1)} %get-tuple-element.90), channel_id=1, source_target_pairs={{0,14},{2,12},{4,2},{6,0},{8,6},{10,4},{12,10},{14,8},{1,15},{3,13... | collective-permute-start | bytes 491528 | tf_op jit(solution)/shard_map/ppermute | solution.py:298
  32.5 12.5 %collective-permute-start.8 = (bf16[2,320,128]{2,1,0:T(8,128)(2,1)S(1)}, bf16[2,320,128]{2,1,0:T(8,128)(2,1)S(1)}, u32[]{:S(2)}, u32[]{:S(2)}) collective-permute-start(bf16[2,320,128]{2,1,0:T(8,128)(2,1)S(1)} %get-tuple-element.89), channel_id=1, source_target_pairs={{0,10},{2,8},{4,14},{6,12},{8,2},{10,0},{12,6},{14,4},{1,11},{3,9}... | collective-permute-start | bytes 491528 | tf_op jit(solution)/shard_map/ppermute | solution.py:298
  45.0 2.3 %collective-permute-start.10 = (bf16[320,1280]{1,0:T(8,128)(2,1)S(1)}, bf16[320,1280]{1,0:T(8,128)(2,1)S(1)}, u32[]{:S(2)}, u32[]{:S(2)}) collective-permute-start(bf16[320,1280]{1,0:T(8,128)(2,1)S(1)} %split_table.3.refs_3_.refs_7_), channel_id=1, source_target_pairs={{0,1},{1,0},{2,3},{3,2},{4,5},{5,4},{6,7},{7,6},{8,9},{9,8},{10,11... | collective-permute-start | bytes 2457608 | tf_op jit(solution)/shard_map/ppermute | solution.py:288
  50.9 7.4 %collective-permute-start.11 = (bf16[2,320,128]{2,1,0:T(8,128)(2,1)S(1)}, bf16[2,320,128]{2,1,0:T(8,128)(2,1)S(1)}, u32[]{:S(2)}, u32[]{:S(2)}) collective-permute-start(bf16[2,320,128]{2,1,0:T(8,128)(2,1)S(1)} %get-tuple-element.104), channel_id=1, source_target_pairs={{0,2},{2,0},{4,6},{6,4},{8,10},{10,8},{12,14},{14,12},{1,3},{3,1},... | collective-permute-start | bytes 491528 | tf_op jit(solution)/shard_map/ppermute | solution.py:298
  52.4 8.9 %collective-permute-start.12 = (bf16[2,320,128]{2,1,0:T(8,128)(2,1)S(1)}, bf16[2,320,128]{2,1,0:T(8,128)(2,1)S(1)}, u32[]{:S(2)}, u32[]{:S(2)}) collective-permute-start(bf16[2,320,128]{2,1,0:T(8,128)(2,1)S(1)} %get-tuple-element.107), channel_id=1, source_target_pairs={{0,4},{2,6},{4,8},{6,10},{8,12},{10,14},{12,0},{14,2},{1,5},{3,7},... | collective-permute-start | bytes 491528 | tf_op jit(solution)/shard_map/ppermute | solution.py:298
  52.4 11.2 %collective-permute-start.16 = (bf16[2,320,128]{2,1,0:T(8,128)(2,1)S(1)}, bf16[2,320,128]{2,1,0:T(8,128)(2,1)S(1)}, u32[]{:S(2)}, u32[]{:S(2)}) collective-permute-start(bf16[2,320,128]{2,1,0:T(8,128)(2,1)S(1)} %get-tuple-element.113), channel_id=1, source_target_pairs={{0,12},{2,14},{4,0},{6,2},{8,4},{10,6},{12,8},{14,10},{1,13},{3,15... | collective-permute-start | bytes 491528 | tf_op jit(solution)/shard_map/ppermute | solution.py:298
  56.2 7.4 %collective-permute-start.18 = (bf16[640,128]{1,0:T(8,128)(2,1)S(1)}, bf16[640,128]{1,0:T(8,128)(2,1)S(1)}, u32[]{:S(2)}, u32[]{:S(2)}) collective-permute-start(bf16[640,128]{1,0:T(8,128)(2,1)S(1)} %get-tuple-element.97.refs_2_), channel_id=1, source_target_pairs={{0,2},{2,0},{1,3},{3,1},{4,6},{6,4},{5,7},{7,5},{8,10},{10,8},{9,1... | collective-permute-start | bytes 491528 | tf_op jit(solution)/shard_map/ppermute | solution.py:288
  56.8 11.5 %collective-permute-start.19 = (bf16[640,128]{1,0:T(8,128)(2,1)S(1)}, bf16[640,128]{1,0:T(8,128)(2,1)S(1)}, u32[]{:S(2)}, u32[]{:S(2)}) collective-permute-start(bf16[640,128]{1,0:T(8,128)(2,1)S(1)} %get-tuple-element.101.refs_4_), channel_id=1, source_target_pairs={{0,2},{2,0},{1,3},{3,1},{4,6},{6,4},{5,7},{7,5},{8,10},{10,8},{9,1... | collective-permute-start | bytes 491528 | tf_op jit(solution)/shard_map/ppermute | solution.py:288
  58.3 18.5 %collective-permute-start.14 = (bf16[2,320,128]{2,1,0:T(8,128)(2,1)S(1)}, bf16[2,320,128]{2,1,0:T(8,128)(2,1)S(1)}, u32[]{:S(2)}, u32[]{:S(2)}) collective-permute-start(bf16[2,320,128]{2,1,0:T(8,128)(2,1)S(1)} %get-tuple-element.110), channel_id=1, source_target_pairs={{0,8},{2,10},{4,12},{6,14},{8,0},{10,2},{12,4},{14,6},{1,9},{3,11}... | collective-permute-start | bytes 491528 | tf_op jit(solution)/shard_map/ppermute | solution.py:298
  61.3 19.1 %collective-permute-start.15 = (bf16[2,320,128]{2,1,0:T(8,128)(2,1)S(1)}, bf16[2,320,128]{2,1,0:T(8,128)(2,1)S(1)}, u32[]{:S(2)}, u32[]{:S(2)}) collective-permute-start(bf16[2,320,128]{2,1,0:T(8,128)(2,1)S(1)} %get-tuple-element.111), channel_id=1, source_target_pairs={{0,10},{2,8},{4,14},{6,12},{8,2},{10,0},{12,6},{14,4},{1,11},{3,9}... | collective-permute-start | bytes 491528 | tf_op jit(solution)/shard_map/ppermute | solution.py:298
  63.6 16.8 %collective-permute-start.13 = (bf16[2,320,128]{2,1,0:T(8,128)(2,1)S(1)}, bf16[2,320,128]{2,1,0:T(8,128)(2,1)S(1)}, u32[]{:S(2)}, u32[]{:S(2)}) collective-permute-start(bf16[2,320,128]{2,1,0:T(8,128)(2,1)S(1)} %get-tuple-element.109), channel_id=1, source_target_pairs={{0,6},{2,4},{4,10},{6,8},{8,14},{10,12},{12,2},{14,0},{1,7},{3,5},... | collective-permute-start | bytes 491528 | tf_op jit(solution)/shard_map/ppermute | solution.py:298
  63.6 16.8 %collective-permute-start.17 = (bf16[2,320,128]{2,1,0:T(8,128)(2,1)S(1)}, bf16[2,320,128]{2,1,0:T(8,128)(2,1)S(1)}, u32[]{:S(2)}, u32[]{:S(2)}) collective-permute-start(bf16[2,320,128]{2,1,0:T(8,128)(2,1)S(1)} %get-tuple-element.115), channel_id=1, source_target_pairs={{0,14},{2,12},{4,2},{6,0},{8,6},{10,4},{12,10},{14,8},{1,15},{3,13... | collective-permute-start | bytes 491528 | tf_op jit(solution)/shard_map/ppermute | solution.py:298

commit v3 on v2

--- a/solution.py
+++ b/solution.py
@@ -302,7 +302,6 @@
 
     wide_at, lev_at, fld_at = (lax.axis_index(axis) for axis in ("wide", "lev", "fld"))
     meta = jnp.stack((slot_wave[0], wide_at, lev_at, fld_at, lax.axis_index("ens"))).astype(jnp.int32)
-    place = jnp.stack((jnp.zeros_like(wide_at), wide_at, lev_at, fld_at)).astype(jnp.int32)
     position = (wide_at * latitudes + jnp.arange(latitudes, dtype=jnp.int32)).astype(jnp.float32)
     weights = jnp.sin(math.pi * (position + 0.5) / (2 * half_count))
     weights = jnp.broadcast_to(weights[:, None], (latitudes, lanes))
@@ -313,7 +312,7 @@
     blocks = call(
         functools.partial(split_body, slots, fields, block), (shape(2, latitudes, lanes),) * (wide * levs),
         "split_hemispheres", move_flops,
-    )(place, fourier_input_rows.reshape(2, latitudes * group, lanes), weights)
+    )(meta, fourier_input_rows.reshape(2, latitudes * group, lanes), weights)
     table_beside, *blocks = behind(table_beside, *blocks)
     *matrices, scale = call(
         functools.partial(modes_body, sizes, degree_count),

time: 82.7 us -> 81.8 us (0.989)
  transfers between devices with their start and end apart: 20 -> 20, of which waited for: 9 -> 9; matrix products, arithmetic and copies ran while one was open for 0% -> 0% of each run, Pallas kernels for 12% -> 11%
where the time goes in v3:
time: 81.8 us; the launch traced here: 81.4 us
  waiting for transfers between devices  37.3 us (46%)
  starting transfers between devices  26.6 us (33%)
  Pallas kernels  14.4 us (18%)
  local copies, waits for them, and re-layouts  1.61 us (2%)
  between operations  1.42 us (2%)
    ppermute x14, waiting for transfers between devices, moved(): return lax.ppermute(value, ('wide', 'lev'), pairs)  32.8 us
    ppermute x14, starting transfers between devices, moved(): return lax.ppermute(value, ('wide', 'lev'), pairs)  20 us
    pallas_call x9, Pallas kernels, run(): pl.pallas_call(kernel, out_shape=out_shape, in_specs=[smem] * scalars + [...  14.4 us
    ppermute x6, starting transfers between devices, shifted(): lax.ppermute(value, axis, [(i, (i + step) % count) for i in range(count)])  6.65 us
    ppermute x6, waiting for transfers between devices, shifted(): lax.ppermute(value, axis, [(i, (i + step) % count) for i in range(count)])  4.48 us
  transfers between devices with their start and end apart: 20, of which 9 were waited for; matrix products, arithmetic and copies ran while one was open for 0% of the time, Pallas kernels for 11%

profile of v3, /device:TPU:0, one launch (start us, length us, event | category | flops | bytes accessed | tf_op | source)
XLA Modules:
  0.0 81.4 jit_solution(8992286324235620266)
XLA Ops:
  0.6 0.5 collective-permute-start
  1.8 0.1 stack.19.refs_0_
  1.9 0.0 copy-start
  1.9 0.1 broadcast_in_dim.10.refs_2_
  2.0 0.0 copy-start.4
  2.1 1.4 %copy-done.4 = bf16[2,320,4,2,128]{4,3,2,1,0:T(2,128)(2,1)S(1)} copy-done((bf16[2,320,4,2,128]{4,3,2,1,0:T(2,128)(2,1)S(1)}, bf16[2,320,4,2,128]{4,3,2,1,0:T(2,128)(2,1)}, u32[]{:S(2)}) %copy-start.4) | copy-done | bytes 1310744
  3.4 1.1 %split_hemispheres.1 = (bf16[2,320,128]{2,1,0:T(8,128)(2,1)S(1)}, bf16[2,320,128]{2,1,0:T(8,128)(2,1)S(1)}, bf16[2,320,128]{2,1,0:T(8,128)(2,1)S(1)}, bf16[2,320...) custom-call(s32[5]{0:T(128)S(1)} %stack.19.refs_0_, ...), custom_call_target="tpu_custom_call" | custom-call | flops 671088640 | tf_op jit(solution)/shard_map/split_hemispheres/pallas_call | solution.py:55
  4.6 0.0 collective-permute-done.refs_2_
  4.6 2.6 %collective-permute-start.1 = (bf16[160,1280]{1,0:T(8,128)(2,1)S(1)}, bf16[160,1280]{1,0:T(8,128)(2,1)S(1)}, u32[]{:S(2)}, u32[]{:S(2)}) collective-permute-start(bf16[160,1280]{1,0:T(8,128)(2,1)S(1)} %constant_dynamic-slice_fusion), channel_id=1, source_target_pairs={{0,2},{2,0},{1,3},{3,1},{4,6},{6,4},{5,7},{7,5},{8,10},{10,8},{9,1... | collective-permute-start | bytes 1228808 | tf_op jit(solution)/shard_map/ppermute | solution.py:288
  7.2 0.1 collective-permute-start.5
  7.3 4.0 %collective-permute-start.4 = (bf16[2,320,128]{2,1,0:T(8,128)(2,1)S(1)}, bf16[2,320,128]{2,1,0:T(8,128)(2,1)S(1)}, u32[]{:S(2)}, u32[]{:S(2)}) collective-permute-start(bf16[2,320,128]{2,1,0:T(8,128)(2,1)S(1)} %get-tuple-element.80), channel_id=1, source_target_pairs={{0,12},{2,14},{4,0},{6,2},{8,4},{10,6},{12,8},{14,10},{1,13},{3,15... | collective-permute-start | bytes 491528 | tf_op jit(solution)/shard_map/ppermute | solution.py:298
  11.3 0.0 collective-permute-start.2
  11.3 1.0 %collective-permute-start.3 = (bf16[2,320,128]{2,1,0:T(8,128)(2,1)S(1)}, bf16[2,320,128]{2,1,0:T(8,128)(2,1)S(1)}, u32[]{:S(2)}, u32[]{:S(2)}) collective-permute-start(bf16[2,320,128]{2,1,0:T(8,128)(2,1)S(1)} %get-tuple-element.78), channel_id=1, source_target_pairs={{0,8},{2,10},{4,12},{6,14},{8,0},{10,2},{12,4},{14,6},{1,9},{3,11}... | collective-permute-start | bytes 491528 | tf_op jit(solution)/shard_map/ppermute | solution.py:298
  12.4 1.1 %spread_modes.1 = (bf16[256,256]{1,0:T(8,128)(2,1)S(1)}, bf16[256,256]{1,0:T(8,128)(2,1)S(1)}, f32[1280,128]{1,0:T(8,128)S(1)}) custom-call(s32[5]{0:T(128)S(1)} %stack.19.refs_0_, bf16[128,128]{1,0:T(8,128)(2,1)S(1)} %copy-done.1, bf16[128,128]{1,0:T(8,128)(2,1)S(1)} %copy-done.2, f32[1,128]{1,0:T(1,128)S(1)} %bitcast.12, ...), custom_call_target="tpu_custom_call" | custom-call | flops 25165824 | tf_op jit(solution)/shard_map/spread_modes/pallas_call | solution.py:55
  13.5 1.6 %split_table.2 = (bf16[320,1280]{1,0:T(8,128)(2,1)S(1)}, bf16[320,1280]{1,0:T(8,128)(2,1)S(1)}) custom-call(s32[5]{0:T(128)S(1)} %stack.19.refs_0_, bf16[320,1280]{1,0:T(8,128)(2,1)S(1)} %bitcast.11, bf16[320,1280]{1,0:T(8,128)(2,1)S(1)} %collective-permute-done.refs_2_, f32[1280,128]{1,0:T(8,128)S(1)} %get-tuple-element.70.refs_3_.refs_2_), custom_call_target="tpu_custom_call" | custom-call | flops 524288000 | tf_op jit(solution)/shard_map/split_table/pallas_call | solution.py:55
  15.1 5.8 %collective-permute-done.5.refs_7_ = bf16[2,320,128]{2,1,0:T(8,128)(2,1)S(1)} collective-permute-done((bf16[2,320,128]{2,1,0:T(8,128)(2,1)S(1)}, bf16[2,320,128]{2,1,0:T(8,128)(2,1)S(1)}, u32[]{:S(2)}, u32[]{:S(2)}) %collective-permute-start.5) | collective-permute-done | bytes 163872 | tf_op jit(solution)/shard_map/ppermute | solution.py:298
  20.8 0.0 collective-permute-done.4.refs_12_
  20.8 0.0 collective-permute-done.2.refs_8_
  20.9 4.5 %collective-permute-done.3.refs_10_ = bf16[2,320,128]{2,1,0:T(8,128)(2,1)S(1)} collective-permute-done((bf16[2,320,128]{2,1,0:T(8,128)(2,1)S(1)}, bf16[2,320,128]{2,1,0:T(8,128)(2,1)S(1)}, u32[]{:S(2)}, u32[]{:S(2)}) %collective-permute-start.3) | collective-permute-done | bytes 163872 | tf_op jit(solution)/shard_map/ppermute | solution.py:298
  25.3 0.0 collective-permute-done.1.refs_1_
  25.3 1.5 %collective-permute-start.6 = (bf16[160,1280]{1,0:T(8,128)(2,1)S(1)}, bf16[160,1280]{1,0:T(8,128)(2,1)S(1)}, u32[]{:S(2)}, u32[]{:S(2)}) collective-permute-start(bf16[160,1280]{1,0:T(8,128)(2,1)S(1)} %collective-permute-done.1.refs_1_), channel_id=1, source_target_pairs={{0,16},{16,0},{1,17},{17,1},{2,18},{18,2},{3,19},{19,3},{4,20},{20... | collective-permute-start | bytes 1228808 | tf_op jit(solution)/shard_map/ppermute | solution.py:288
  26.8 0.8 collective-permute-start.7
  27.6 4.0 %collective-permute-start.9 = (bf16[2,320,128]{2,1,0:T(8,128)(2,1)S(1)}, bf16[2,320,128]{2,1,0:T(8,128)(2,1)S(1)}, u32[]{:S(2)}, u32[]{:S(2)}) collective-permute-start(bf16[2,320,128]{2,1,0:T(8,128)(2,1)S(1)} %get-tuple-element.90), channel_id=1, source_target_pairs={{0,14},{2,12},{4,2},{6,0},{8,6},{10,4},{12,10},{14,8},{1,15},{3,13... | collective-permute-start | bytes 491528 | tf_op jit(solution)/shard_map/ppermute | solution.py:298
  31.6 0.0 collective-permute-start.8
  31.6 4.3 %collective-permute-done.6.refs_2_ = bf16[160,1280]{1,0:T(8,128)(2,1)S(1)} collective-permute-done((bf16[160,1280]{1,0:T(8,128)(2,1)S(1)}, bf16[160,1280]{1,0:T(8,128)(2,1)S(1)}, u32[]{:S(2)}, u32[]{:S(2)}) %collective-permute-start.6) | collective-permute-done | bytes 409632 | tf_op jit(solution)/shard_map/ppermute | solution.py:288
  35.9 1.2 %split_table.3.refs_3_.refs_7_ = bf16[320,1280]{1,0:T(8,128)(2,1)S(1)} custom-call(s32[5]{0:T(128)S(1)} %stack.19.refs_0_, bf16[160,1280]{1,0:T(8,128)(2,1)S(1)} %collective-permute-done.1.refs_1_, bf16[160,1280]{1,0:T(8,128)(2,1)S(1)} %collective-permute-done.6.refs_2_), custom_call_target="tpu_custom_call" | custom-call | flops 262144000 | tf_op jit(solution)/shard_map/split_table/pallas_call | solution.py:55
  37.1 0.0 collective-permute-done.7.refs_9_
  37.1 6.9 %collective-permute-done.8.refs_11_ = bf16[2,320,128]{2,1,0:T(8,128)(2,1)S(1)} collective-permute-done((bf16[2,320,128]{2,1,0:T(8,128)(2,1)S(1)}, bf16[2,320,128]{2,1,0:T(8,128)(2,1)S(1)}, u32[]{:S(2)}, u32[]{:S(2)}) %collective-permute-start.8) | collective-permute-done | bytes 163872 | tf_op jit(solution)/shard_map/ppermute | solution.py:298
  44.1 0.0 collective-permute-start.10
  44.1 2.2 %direct_legendre_and_solve.2 = (bf16[640,128]{1,0:T(8,128)(2,1)S(1)}, bf16[640,128]{1,0:T(8,128)(2,1)S(1)}, bf16[2,1280,256]{2,1,0:T(8,128)(2,1)S(1)}) custom-call(s32[5]{0:T(128)S(1)} %stack.19.refs_0_, bf16[256,256]{1,0:T(8,128)(2,1)S(1)} %get-tuple-element.68.refs_1_.refs_0_, bf16[256,256]{1,0:T(8,128)(2,1)S(1)} %get-tuple-element.69.refs_2_.refs_1_, ...), custom_call_target="tpu_custom_call" | custom-call | flops 419430400 | tf_op jit(solution)/shard_map/direct_legendre_and_solve/pallas_call | solution.py:55
  46.3 0.1 collective-permute-done.10.refs_4_.refs_8_
  46.4 1.5 %direct_legendre_and_solve.3 = (bf16[640,128]{1,0:T(8,128)(2,1)S(1)}, bf16[640,128]{1,0:T(8,128)(2,1)S(1)}) custom-call(bf16[256,256]{1,0:T(8,128)(2,1)S(1)} %get-tuple-element.68.refs_1_.refs_0_, bf16[256,256]{1,0:T(8,128)(2,1)S(1)} %get-tuple-element.69.refs_2_.refs_1_, f32[1280,128]{1,0:T(8,128)S(1)} %get-tuple-element.70.refs_3_.refs_2_, ...), custom_call_target="tpu_custom_call" | custom-call | flops 419430400 | tf_op jit(solution)/shard_map/direct_legendre_and_solve/pallas_call | solution.py:55
  47.9 2.0 %inverse_legendre.1 = (bf16[2,320,128]{2,1,0:T(8,128)(2,1)S(1)}, bf16[2,320,128]{2,1,0:T(8,128)(2,1)S(1)}, bf16[2,320,128]{2,1,0:T(8,128)(2,1)S(1)}, bf16[2,320,...) custom-call(s32[5]{0:T(128)S(1)} %stack.19.refs_0_, ...), custom_call_target="tpu_custom_call" | custom-call | flops 838860800 | tf_op jit(solution)/shard_map/inverse_legendre/pallas_call | solution.py:55
  49.9 1.6 %collective-permute-start.11 = (bf16[2,320,128]{2,1,0:T(8,128)(2,1)S(1)}, bf16[2,320,128]{2,1,0:T(8,128)(2,1)S(1)}, u32[]{:S(2)}, u32[]{:S(2)}) collective-permute-start(bf16[2,320,128]{2,1,0:T(8,128)(2,1)S(1)} %get-tuple-element.104), channel_id=1, source_target_pairs={{0,2},{2,0},{4,6},{6,4},{8,10},{10,8},{12,14},{14,12},{1,3},{3,1},... | collective-permute-start | bytes 491528 | tf_op jit(solution)/shard_map/ppermute | solution.py:298
  51.5 3.8 %collective-permute-start.16 = (bf16[2,320,128]{2,1,0:T(8,128)(2,1)S(1)}, bf16[2,320,128]{2,1,0:T(8,128)(2,1)S(1)}, u32[]{:S(2)}, u32[]{:S(2)}) collective-permute-start(bf16[2,320,128]{2,1,0:T(8,128)(2,1)S(1)} %get-tuple-element.113), channel_id=1, source_target_pairs={{0,12},{2,14},{4,0},{6,2},{8,4},{10,6},{12,8},{14,10},{1,13},{3,15... | collective-permute-start | bytes 491528 | tf_op jit(solution)/shard_map/ppermute | solution.py:298
  55.3 0.5 collective-permute-start.18
  55.8 1.5 %collective-permute-start.19 = (bf16[640,128]{1,0:T(8,128)(2,1)S(1)}, bf16[640,128]{1,0:T(8,128)(2,1)S(1)}, u32[]{:S(2)}, u32[]{:S(2)}) collective-permute-start(bf16[640,128]{1,0:T(8,128)(2,1)S(1)} %get-tuple-element.101.refs_4_), channel_id=1, source_target_pairs={{0,2},{2,0},{1,3},{3,1},{4,6},{6,4},{5,7},{7,5},{8,10},{10,8},{9,1... | collective-permute-start | bytes 491528 | tf_op jit(solution)/shard_map/ppermute | solution.py:288
  57.3 3.0 %collective-permute-done.12.refs_3_ = bf16[2,320,128]{2,1,0:T(8,128)(2,1)S(1)} collective-permute-done((bf16[2,320,128]{2,1,0:T(8,128)(2,1)S(1)}, bf16[2,320,128]{2,1,0:T(8,128)(2,1)S(1)}, u32[]{:S(2)}, u32[]{:S(2)}) %collective-permute-start.12) | collective-permute-done | bytes 163872 | tf_op jit(solution)/shard_map/ppermute | solution.py:298
  60.4 2.2 %collective-permute-done.16.refs_7_ = bf16[2,320,128]{2,1,0:T(8,128)(2,1)S(1)} collective-permute-done((bf16[2,320,128]{2,1,0:T(8,128)(2,1)S(1)}, bf16[2,320,128]{2,1,0:T(8,128)(2,1)S(1)}, u32[]{:S(2)}, u32[]{:S(2)}) %collective-permute-start.16) | collective-permute-done | bytes 163872 | tf_op jit(solution)/shard_map/ppermute | solution.py:298
  62.6 0.0 collective-permute-start.13
  62.6 4.7 %collective-permute-start.17 = (bf16[2,320,128]{2,1,0:T(8,128)(2,1)S(1)}, bf16[2,320,128]{2,1,0:T(8,128)(2,1)S(1)}, u32[]{:S(2)}, u32[]{:S(2)}) collective-permute-start(bf16[2,320,128]{2,1,0:T(8,128)(2,1)S(1)} %get-tuple-element.115), channel_id=1, source_target_pairs={{0,14},{2,12},{4,2},{6,0},{8,6},{10,4},{12,10},{14,8},{1,15},{3,13... | collective-permute-start | bytes 491528 | tf_op jit(solution)/shard_map/ppermute | solution.py:298
  67.3 0.0 collective-permute-done.19.refs_4_
  67.3 1.8 %order_spectral.1 = bf16[2560,128]{1,0:T(8,128)(2,1)} custom-call(s32[5]{0:T(128)S(1)} %stack.19.refs_0_, bf16[640,128]{1,0:T(8,128)(2,1)S(1)} %get-tuple-element.96.refs_1_, bf16[640,128]{1,0:T(8,128)(2,1)S(1)} %get-tuple-element.100.refs_3_.refs_2_, bf16[640,128]{1,0:T(8,128)(2,1)S(1)} %collective-permute-done.18.refs_3_, ...), custom_call_target="tpu_custom_call" | custom-call | flops 671088640 | tf_op jit(solution)/shard_map/order_spectral/pallas_call | solution.py:55
  69.1 6.9 %collective-permute-done.14.refs_5_ = bf16[2,320,128]{2,1,0:T(8,128)(2,1)S(1)} collective-permute-done((bf16[2,320,128]{2,1,0:T(8,128)(2,1)S(1)}, bf16[2,320,128]{2,1,0:T(8,128)(2,1)S(1)}, u32[]{:S(2)}, u32[]{:S(2)}) %collective-permute-start.14) | collective-permute-done | bytes 163872 | tf_op jit(solution)/shard_map/ppermute | solution.py:298
  75.9 3.6 %collective-permute-done.15.refs_6_ = bf16[2,320,128]{2,1,0:T(8,128)(2,1)S(1)} collective-permute-done((bf16[2,320,128]{2,1,0:T(8,128)(2,1)S(1)}, bf16[2,320,128]{2,1,0:T(8,128)(2,1)S(1)}, u32[]{:S(2)}, u32[]{:S(2)}) %collective-permute-start.15) | collective-permute-done | bytes 163872 | tf_op jit(solution)/shard_map/ppermute | solution.py:298
  79.5 0.0 collective-permute-done.13.refs_4_
  79.5 0.0 collective-permute-done.17.refs_8_
  79.5 1.9 %join_hemispheres.1 = bf16[2,2560,128]{2,1,0:T(8,128)(2,1)} custom-call(s32[5]{0:T(128)S(1)} %stack.19.refs_0_, bf16[2,320,128]{2,1,0:T(8,128)(2,1)S(1)} %get-tuple-element.102.refs_1_, bf16[2,320,128]{2,1,0:T(8,128)(2,1)S(1)} %collective-permute-done.11.refs_2_, bf16[2,320,128]{2,1,0:T(8,128)(2,1)S(1)} %collective-permute-done.12.refs_3_, ...), custom_call_target="tpu_custom_call" | custom-call | flops 671088640 | tf_op jit(solution)/shard_map/join_hemispheres/pallas_call | solution.py:55
  (15 shorter events, 0.1 us)
Async XLA Ops:
  0.6 3.9 %collective-permute-start = (bf16[320,1280]{1,0:T(8,128)(2,1)}, bf16[320,1280]{1,0:T(8,128)(2,1)S(1)}, u32[]{:S(2)}, u32[]{:S(2)}) collective-permute-start(bf16[320,1280]{1,0:T(8,128)(2,1)} %bitcast.9), channel_id=1, source_target_pairs={{0,1},{1,0},{2,3},{3,2},{4,5},{5,4},{6,7},{7,6},{8,9},{9,8},{10,11... | collective-permute-start | bytes 2457608 | tf_op jit(solution)/shard_map/ppermute | solution.py:288
  1.9 2.6 %copy-start = (bf16[1,320,1280]{2,1,0:T(8,128)(2,1)S(1)}, bf16[1,320,1280]{2,1,0:T(8,128)(2,1)}, u32[]{:S(2)}) copy-start(bf16[1,320,1280]{2,1,0:T(8,128)(2,1)} %param.7) | copy-start | bytes 2457604
  2.0 1.4 %copy-start.4 = (bf16[2,320,4,2,128]{4,3,2,1,0:T(2,128)(2,1)S(1)}, bf16[2,320,4,2,128]{4,3,2,1,0:T(2,128)(2,1)}, u32[]{:S(2)}) copy-start(bf16[2,320,4,2,128]{4,3,2,1,0:T(2,128)(2,1)} %param.6) | copy-start | bytes 3932164
  3.4 8.9 %copy-start.1 = (bf16[128,128]{1,0:T(8,128)(2,1)S(1)}, bf16[128,128]{1,0:T(8,128)(2,1)}, u32[]{:S(2)}) copy-start(bf16[128,128]{1,0:T(8,128)(2,1)} %refs_1_.1) | copy-start | bytes 98308
  3.4 8.9 %copy-start.2 = (bf16[128,128]{1,0:T(8,128)(2,1)S(1)}, bf16[128,128]{1,0:T(8,128)(2,1)}, u32[]{:S(2)}) copy-start(bf16[128,128]{1,0:T(8,128)(2,1)} %refs_2_.1) | copy-start | bytes 98308
  3.4 8.9 %copy-start.3 = (f32[128]{0:T(128)S(1)}, f32[128]{0:T(128)}, u32[]{:S(2)}) copy-start(f32[128]{0:T(128)} %param.11) | copy-start | bytes 1540
  4.6 20.7 %collective-permute-start.1 = (bf16[160,1280]{1,0:T(8,128)(2,1)S(1)}, bf16[160,1280]{1,0:T(8,128)(2,1)S(1)}, u32[]{:S(2)}, u32[]{:S(2)}) collective-permute-start(bf16[160,1280]{1,0:T(8,128)(2,1)S(1)} %constant_dynamic-slice_fusion), channel_id=1, source_target_pairs={{0,2},{2,0},{1,3},{3,1},{4,6},{6,4},{5,7},{7,5},{8,10},{10,8},{9,1... | collective-permute-start | bytes 1228808 | tf_op jit(solution)/shard_map/ppermute | solution.py:288
  7.2 13.6 %collective-permute-start.5 = (bf16[2,320,128]{2,1,0:T(8,128)(2,1)S(1)}, bf16[2,320,128]{2,1,0:T(8,128)(2,1)S(1)}, u32[]{:S(2)}, u32[]{:S(2)}) collective-permute-start(bf16[2,320,128]{2,1,0:T(8,128)(2,1)S(1)} %get-tuple-element.83), channel_id=1, source_target_pairs={{0,2},{2,0},{4,6},{6,4},{8,10},{10,8},{12,14},{14,12},{1,3},{3,1},... | collective-permute-start | bytes 491528 | tf_op jit(solution)/shard_map/ppermute | solution.py:298
  7.3 13.6 %collective-permute-start.4 = (bf16[2,320,128]{2,1,0:T(8,128)(2,1)S(1)}, bf16[2,320,128]{2,1,0:T(8,128)(2,1)S(1)}, u32[]{:S(2)}, u32[]{:S(2)}) collective-permute-start(bf16[2,320,128]{2,1,0:T(8,128)(2,1)S(1)} %get-tuple-element.80), channel_id=1, source_target_pairs={{0,12},{2,14},{4,0},{6,2},{8,4},{10,6},{12,8},{14,10},{1,13},{3,15... | collective-permute-start | bytes 491528 | tf_op jit(solution)/shard_map/ppermute | solution.py:298
  11.3 9.5 %collective-permute-start.2 = (bf16[2,320,128]{2,1,0:T(8,128)(2,1)S(1)}, bf16[2,320,128]{2,1,0:T(8,128)(2,1)S(1)}, u32[]{:S(2)}, u32[]{:S(2)}) collective-permute-start(bf16[2,320,128]{2,1,0:T(8,128)(2,1)S(1)} %get-tuple-element.76), channel_id=1, source_target_pairs={{0,4},{2,6},{4,8},{6,10},{8,12},{10,14},{12,0},{14,2},{1,5},{3,7},... | collective-permute-start | bytes 491528 | tf_op jit(solution)/shard_map/ppermute | solution.py:298
  11.3 14.0 %collective-permute-start.3 = (bf16[2,320,128]{2,1,0:T(8,128)(2,1)S(1)}, bf16[2,320,128]{2,1,0:T(8,128)(2,1)S(1)}, u32[]{:S(2)}, u32[]{:S(2)}) collective-permute-start(bf16[2,320,128]{2,1,0:T(8,128)(2,1)S(1)} %get-tuple-element.78), channel_id=1, source_target_pairs={{0,8},{2,10},{4,12},{6,14},{8,0},{10,2},{12,4},{14,6},{1,9},{3,11}... | collective-permute-start | bytes 491528 | tf_op jit(solution)/shard_map/ppermute | solution.py:298
  25.3 10.6 %collective-permute-start.6 = (bf16[160,1280]{1,0:T(8,128)(2,1)S(1)}, bf16[160,1280]{1,0:T(8,128)(2,1)S(1)}, u32[]{:S(2)}, u32[]{:S(2)}) collective-permute-start(bf16[160,1280]{1,0:T(8,128)(2,1)S(1)} %collective-permute-done.1.refs_1_), channel_id=1, source_target_pairs={{0,16},{16,0},{1,17},{17,1},{2,18},{18,2},{3,19},{19,3},{4,20},{20... | collective-permute-start | bytes 1228808 | tf_op jit(solution)/shard_map/ppermute | solution.py:288
  26.8 10.3 %collective-permute-start.7 = (bf16[2,320,128]{2,1,0:T(8,128)(2,1)S(1)}, bf16[2,320,128]{2,1,0:T(8,128)(2,1)S(1)}, u32[]{:S(2)}, u32[]{:S(2)}) collective-permute-start(bf16[2,320,128]{2,1,0:T(8,128)(2,1)S(1)} %get-tuple-element.88), channel_id=1, source_target_pairs={{0,6},{2,4},{4,10},{6,8},{8,14},{10,12},{12,2},{14,0},{1,7},{3,5},... | collective-permute-start | bytes 491528 | tf_op jit(solution)/shard_map/ppermute | solution.py:298
  27.6 9.5 %collective-permute-start.9 = (bf16[2,320,128]{2,1,0:T(8,128)(2,1)S(1)}, bf16[2,320,128]{2,1,0:T(8,128)(2,1)S(1)}, u32[]{:S(2)}, u32[]{:S(2)}) collective-permute-start(bf16[2,320,128]{2,1,0:T(8,128)(2,1)S(1)} %get-tuple-element.90), channel_id=1, source_target_pairs={{0,14},{2,12},{4,2},{6,0},{8,6},{10,4},{12,10},{14,8},{1,15},{3,13... | collective-permute-start | bytes 491528 | tf_op jit(solution)/shard_map/ppermute | solution.py:298
  31.6 12.5 %collective-permute-start.8 = (bf16[2,320,128]{2,1,0:T(8,128)(2,1)S(1)}, bf16[2,320,128]{2,1,0:T(8,128)(2,1)S(1)}, u32[]{:S(2)}, u32[]{:S(2)}) collective-permute-start(bf16[2,320,128]{2,1,0:T(8,128)(2,1)S(1)} %get-tuple-element.89), channel_id=1, source_target_pairs={{0,10},{2,8},{4,14},{6,12},{8,2},{10,0},{12,6},{14,4},{1,11},{3,9}... | collective-permute-start | bytes 491528 | tf_op jit(solution)/shard_map/ppermute | solution.py:298
  44.1 2.3 %collective-permute-start.10 = (bf16[320,1280]{1,0:T(8,128)(2,1)S(1)}, bf16[320,1280]{1,0:T(8,128)(2,1)S(1)}, u32[]{:S(2)}, u32[]{:S(2)}) collective-permute-start(bf16[320,1280]{1,0:T(8,128)(2,1)S(1)} %split_table.3.refs_3_.refs_7_), channel_id=1, source_target_pairs={{0,1},{1,0},{2,3},{3,2},{4,5},{5,4},{6,7},{7,6},{8,9},{9,8},{10,11... | collective-permute-start | bytes 2457608 | tf_op jit(solution)/shard_map/ppermute | solution.py:288
  49.9 7.4 %collective-permute-start.11 = (bf16[2,320,128]{2,1,0:T(8,128)(2,1)S(1)}, bf16[2,320,128]{2,1,0:T(8,128)(2,1)S(1)}, u32[]{:S(2)}, u32[]{:S(2)}) collective-permute-start(bf16[2,320,128]{2,1,0:T(8,128)(2,1)S(1)} %get-tuple-element.104), channel_id=1, source_target_pairs={{0,2},{2,0},{4,6},{6,4},{8,10},{10,8},{12,14},{14,12},{1,3},{3,1},... | collective-permute-start | bytes 491528 | tf_op jit(solution)/shard_map/ppermute | solution.py:298
  51.5 8.9 %collective-permute-start.12 = (bf16[2,320,128]{2,1,0:T(8,128)(2,1)S(1)}, bf16[2,320,128]{2,1,0:T(8,128)(2,1)S(1)}, u32[]{:S(2)}, u32[]{:S(2)}) collective-permute-start(bf16[2,320,128]{2,1,0:T(8,128)(2,1)S(1)} %get-tuple-element.107), channel_id=1, source_target_pairs={{0,4},{2,6},{4,8},{6,10},{8,12},{10,14},{12,0},{14,2},{1,5},{3,7},... | collective-permute-start | bytes 491528 | tf_op jit(solution)/shard_map/ppermute | solution.py:298
  51.5 11.1 %collective-permute-start.16 = (bf16[2,320,128]{2,1,0:T(8,128)(2,1)S(1)}, bf16[2,320,128]{2,1,0:T(8,128)(2,1)S(1)}, u32[]{:S(2)}, u32[]{:S(2)}) collective-permute-start(bf16[2,320,128]{2,1,0:T(8,128)(2,1)S(1)} %get-tuple-element.113), channel_id=1, source_target_pairs={{0,12},{2,14},{4,0},{6,2},{8,4},{10,6},{12,8},{14,10},{1,13},{3,15... | collective-permute-start | bytes 491528 | tf_op jit(solution)/shard_map/ppermute | solution.py:298
  55.3 7.2 %collective-permute-start.18 = (bf16[640,128]{1,0:T(8,128)(2,1)S(1)}, bf16[640,128]{1,0:T(8,128)(2,1)S(1)}, u32[]{:S(2)}, u32[]{:S(2)}) collective-permute-start(bf16[640,128]{1,0:T(8,128)(2,1)S(1)} %get-tuple-element.97.refs_2_), channel_id=1, source_target_pairs={{0,2},{2,0},{1,3},{3,1},{4,6},{6,4},{5,7},{7,5},{8,10},{10,8},{9,1... | collective-permute-start | bytes 491528 | tf_op jit(solution)/shard_map/ppermute | solution.py:288
  55.8 11.4 %collective-permute-start.19 = (bf16[640,128]{1,0:T(8,128)(2,1)S(1)}, bf16[640,128]{1,0:T(8,128)(2,1)S(1)}, u32[]{:S(2)}, u32[]{:S(2)}) collective-permute-start(bf16[640,128]{1,0:T(8,128)(2,1)S(1)} %get-tuple-element.101.refs_4_), channel_id=1, source_target_pairs={{0,2},{2,0},{1,3},{3,1},{4,6},{6,4},{5,7},{7,5},{8,10},{10,8},{9,1... | collective-permute-start | bytes 491528 | tf_op jit(solution)/shard_map/ppermute | solution.py:288
  57.3 18.6 %collective-permute-start.14 = (bf16[2,320,128]{2,1,0:T(8,128)(2,1)S(1)}, bf16[2,320,128]{2,1,0:T(8,128)(2,1)S(1)}, u32[]{:S(2)}, u32[]{:S(2)}) collective-permute-start(bf16[2,320,128]{2,1,0:T(8,128)(2,1)S(1)} %get-tuple-element.110), channel_id=1, source_target_pairs={{0,8},{2,10},{4,12},{6,14},{8,0},{10,2},{12,4},{14,6},{1,9},{3,11}... | collective-permute-start | bytes 491528 | tf_op jit(solution)/shard_map/ppermute | solution.py:298
  60.4 19.1 %collective-permute-start.15 = (bf16[2,320,128]{2,1,0:T(8,128)(2,1)S(1)}, bf16[2,320,128]{2,1,0:T(8,128)(2,1)S(1)}, u32[]{:S(2)}, u32[]{:S(2)}) collective-permute-start(bf16[2,320,128]{2,1,0:T(8,128)(2,1)S(1)} %get-tuple-element.111), channel_id=1, source_target_pairs={{0,10},{2,8},{4,14},{6,12},{8,2},{10,0},{12,6},{14,4},{1,11},{3,9}... | collective-permute-start | bytes 491528 | tf_op jit(solution)/shard_map/ppermute | solution.py:298
  62.6 16.9 %collective-permute-start.13 = (bf16[2,320,128]{2,1,0:T(8,128)(2,1)S(1)}, bf16[2,320,128]{2,1,0:T(8,128)(2,1)S(1)}, u32[]{:S(2)}, u32[]{:S(2)}) collective-permute-start(bf16[2,320,128]{2,1,0:T(8,128)(2,1)S(1)} %get-tuple-element.109), channel_id=1, source_target_pairs={{0,6},{2,4},{4,10},{6,8},{8,14},{10,12},{12,2},{14,0},{1,7},{3,5},... | collective-permute-start | bytes 491528 | tf_op jit(solution)/shard_map/ppermute | solution.py:298
  62.6 16.9 %collective-permute-start.17 = (bf16[2,320,128]{2,1,0:T(8,128)(2,1)S(1)}, bf16[2,320,128]{2,1,0:T(8,128)(2,1)S(1)}, u32[]{:S(2)}, u32[]{:S(2)}) collective-permute-start(bf16[2,320,128]{2,1,0:T(8,128)(2,1)S(1)} %get-tuple-element.115), channel_id=1, source_target_pairs={{0,14},{2,12},{4,2},{6,0},{8,6},{10,4},{12,10},{14,8},{1,15},{3,13... | collective-permute-start | bytes 491528 | tf_op jit(solution)/shard_map/ppermute | solution.py:298

commit v4 on v3

--- a/solution.py
+++ b/solution.py
@@ -324,11 +324,11 @@
         4 * shard_rows * shard_rows * half_count, after=(scale,),
     )(meta, legendre[0], table_beside)
 
-    def exchanged(blocks, ahead):
+    def exchanged(blocks, ahead, leads):
         arrived = {(0, 0): blocks[0]}
         for k, d in ((2, 0), (1, 0), (3, 0), (0, 1)):
             arrived[k, d] = moved(blocks[k * levs + d], k, d)
-        for k, first in ((2, (0, 1)), (1, (1, 0)), (3, (3, 0))):
+        for k, first in zip((2, 1, 3), leads):
             value, arrived[first], *_ = behind(blocks[k * levs + 1], arrived[first], *ahead)
             arrived[k, 1] = moved(value, k, 1)
         return arrived
@@ -336,11 +336,11 @@
     def listed(arrived):
         return [arrived[k, d] for k in range(wide) for d in range(levs)]
 
-    arrived = exchanged(blocks, (near[0], scale))
+    arrived = exchanged(blocks, (near[0], scale), ((0, 1), (2, 0), (3, 0)))
     half_shard = shard_rows // 2
     own_table, _ = behind(legendre[0], blocks[0])
     first = over_lev(lax.dynamic_slice_in_dim(own_table, lax.axis_index("ens") * half_shard, half_shard, 0))
-    steps = [(1, 0), (2, 0), (3, 0), (0, 1)]
+    steps = [(2, 0), (3, 0), (0, 1)]
     first, *ahead = behind(first, *(arrived[step] for step in steps))
     arrived |= dict(zip(steps, ahead))
     second = shifted(first, "ens", 2, 1)
@@ -348,7 +348,7 @@
         far_table_body, shape(shard_rows, half_count), "split_table", 2 * shard_rows * shard_rows * half_count,
         scratch=[pltpu.VMEM((shard_rows, half_count), bf16)],
     )(meta, first, second)
-    steps = [(1, 1), (2, 1), (3, 1)]
+    steps = [(1, 0), (1, 1), (2, 1), (3, 1)]
     far, *ahead = behind(far, *(arrived[step] for step in steps))
     arrived |= dict(zip(steps, ahead))
     far = [far, beside(far)]
@@ -366,7 +366,7 @@
         functools.partial(inverse_body, wide), (shape(2, latitudes, lanes),) * (wide * levs),
         "inverse_legendre", transform_flops, scratch=[pltpu.VMEM((2, half_count, columns), bf16)],
     )(meta, *near_spectral, *far_spectral, *near, *far)
-    arrived = exchanged(grid, ())
+    arrived = exchanged(grid, (), ((0, 1), (1, 0), (3, 0)))
     result = listed(arrived)
     spectral_rows = call(
         functools.partial(rows_body, sizes, 32), shape(degree_count * fields, lanes), "order_spectral", move_flops,

time: 81.8 us -> 83.2 us (1.017)
  starting transfers between devices: 26.6 us -> 28.9 us
    ppermute x6, waiting for transfers between devices: 4.48 us -> 1.47 us  [shifted(): lax.ppermute(value, axis, [(i, (i + step) % count) for i in range(count)])]
    ppermute x14, waiting for transfers between devices: 32.8 us -> 35.1 us  [moved(): return lax.ppermute(value, ('wide', 'lev'), pairs)]
    ppermute x14, starting transfers between devices: 20 us -> 22.2 us  [moved(): return lax.ppermute(value, ('wide', 'lev'), pairs)]
  transfers between devices with their start and end apart: 20 -> 20, of which waited for: 9 -> 12; matrix products, arithmetic and copies ran while one was open for 0% -> 0% of each run, Pallas kernels for 11% -> 11%
where the time goes in v4:
time: 83.2 us; the launch traced here: 82.9 us
  waiting for transfers between devices  36.6 us (44%)
  starting transfers between devices  28.9 us (35%)
  Pallas kernels  14.4 us (17%)
  local copies, waits for them, and re-layouts  1.61 us (2%)
  between operations  1.42 us (2%)
    ppermute x14, waiting for transfers between devices, moved(): return lax.ppermute(value, ('wide', 'lev'), pairs)  35.1 us
    ppermute x14, starting transfers between devices, moved(): return lax.ppermute(value, ('wide', 'lev'), pairs)  22.2 us
    pallas_call x9, Pallas kernels, run(): pl.pallas_call(kernel, out_shape=out_shape, in_specs=[smem] * scalars + [...  14.4 us
    ppermute x6, starting transfers between devices, shifted(): lax.ppermute(value, axis, [(i, (i + step) % count) for i in range(count)])  6.66 us
  transfers between devices with their start and end apart: 20, of which 12 were waited for; matrix products, arithmetic and copies ran while one was open for 0% of the time, Pallas kernels for 11%

profile of v4, /device:TPU:0, one launch (start us, length us, event | category | flops | bytes accessed | tf_op | source)
XLA Modules:
  0.0 82.9 jit_solution(15724499713038439365)
XLA Ops:
  0.6 0.5 collective-permute-start
  1.8 0.1 stack.19.refs_0_
  1.9 0.0 copy-start
  1.9 0.1 broadcast_in_dim.10.refs_2_
  2.0 0.0 copy-start.4
  2.1 1.4 %copy-done.4 = bf16[2,320,4,2,128]{4,3,2,1,0:T(2,128)(2,1)S(1)} copy-done((bf16[2,320,4,2,128]{4,3,2,1,0:T(2,128)(2,1)S(1)}, bf16[2,320,4,2,128]{4,3,2,1,0:T(2,128)(2,1)}, u32[]{:S(2)}) %copy-start.4) | copy-done | bytes 1310744
  3.4 1.1 %split_hemispheres.1 = (bf16[2,320,128]{2,1,0:T(8,128)(2,1)S(1)}, bf16[2,320,128]{2,1,0:T(8,128)(2,1)S(1)}, bf16[2,320,128]{2,1,0:T(8,128)(2,1)S(1)}, bf16[2,320...) custom-call(s32[5]{0:T(128)S(1)} %stack.19.refs_0_, ...), custom_call_target="tpu_custom_call" | custom-call | flops 671088640 | tf_op jit(solution)/shard_map/split_hemispheres/pallas_call | solution.py:55
  4.6 2.6 %collective-permute-start.1 = (bf16[160,1280]{1,0:T(8,128)(2,1)S(1)}, bf16[160,1280]{1,0:T(8,128)(2,1)S(1)}, u32[]{:S(2)}, u32[]{:S(2)}) collective-permute-start(bf16[160,1280]{1,0:T(8,128)(2,1)S(1)} %constant_dynamic-slice_fusion), channel_id=1, source_target_pairs={{0,2},{2,0},{1,3},{3,1},{4,6},{6,4},{5,7},{7,5},{8,10},{10,8},{9,1... | collective-permute-start | bytes 1228808 | tf_op jit(solution)/shard_map/ppermute | solution.py:288
  7.2 0.1 collective-permute-start.4
  7.3 4.0 %collective-permute-start.3 = (bf16[2,320,128]{2,1,0:T(8,128)(2,1)S(1)}, bf16[2,320,128]{2,1,0:T(8,128)(2,1)S(1)}, u32[]{:S(2)}, u32[]{:S(2)}) collective-permute-start(bf16[2,320,128]{2,1,0:T(8,128)(2,1)S(1)} %get-tuple-element.79), channel_id=1, source_target_pairs={{0,12},{2,14},{4,0},{6,2},{8,4},{10,6},{12,8},{14,10},{1,13},{3,15... | collective-permute-start | bytes 491528 | tf_op jit(solution)/shard_map/ppermute | solution.py:298
  11.4 1.1 %spread_modes.1 = (bf16[256,256]{1,0:T(8,128)(2,1)S(1)}, bf16[256,256]{1,0:T(8,128)(2,1)S(1)}, f32[1280,128]{1,0:T(8,128)S(1)}) custom-call(s32[5]{0:T(128)S(1)} %stack.19.refs_0_, bf16[128,128]{1,0:T(8,128)(2,1)S(1)} %copy-done.1, bf16[128,128]{1,0:T(8,128)(2,1)S(1)} %copy-done.2, f32[1,128]{1,0:T(1,128)S(1)} %bitcast.12, ...), custom_call_target="tpu_custom_call" | custom-call | flops 25165824 | tf_op jit(solution)/shard_map/spread_modes/pallas_call | solution.py:55
  12.5 1.6 %split_table.2 = (bf16[320,1280]{1,0:T(8,128)(2,1)S(1)}, bf16[320,1280]{1,0:T(8,128)(2,1)S(1)}) custom-call(s32[5]{0:T(128)S(1)} %stack.19.refs_0_, bf16[320,1280]{1,0:T(8,128)(2,1)S(1)} %bitcast.11, bf16[320,1280]{1,0:T(8,128)(2,1)S(1)} %collective-permute-done.refs_2_, f32[1280,128]{1,0:T(8,128)S(1)} %get-tuple-element.70.refs_3_.refs_2_), custom_call_target="tpu_custom_call" | custom-call | flops 524288000 | tf_op jit(solution)/shard_map/split_table/pallas_call | solution.py:55
  14.1 6.8 %collective-permute-done.4.refs_7_ = bf16[2,320,128]{2,1,0:T(8,128)(2,1)S(1)} collective-permute-done((bf16[2,320,128]{2,1,0:T(8,128)(2,1)S(1)}, bf16[2,320,128]{2,1,0:T(8,128)(2,1)S(1)}, u32[]{:S(2)}, u32[]{:S(2)}) %collective-permute-start.4) | collective-permute-done | bytes 163872 | tf_op jit(solution)/shard_map/ppermute | solution.py:298
  20.8 0.0 collective-permute-done.3.refs_12_
  20.8 1.0 %collective-permute-done.2.refs_10_ = bf16[2,320,128]{2,1,0:T(8,128)(2,1)S(1)} collective-permute-done((bf16[2,320,128]{2,1,0:T(8,128)(2,1)S(1)}, bf16[2,320,128]{2,1,0:T(8,128)(2,1)S(1)}, u32[]{:S(2)}, u32[]{:S(2)}) %collective-permute-start.2) | collective-permute-done | bytes 163872 | tf_op jit(solution)/shard_map/ppermute | solution.py:298
  21.8 0.0 collective-permute-done.1.refs_1_
  21.8 1.5 %collective-permute-start.5 = (bf16[160,1280]{1,0:T(8,128)(2,1)S(1)}, bf16[160,1280]{1,0:T(8,128)(2,1)S(1)}, u32[]{:S(2)}, u32[]{:S(2)}) collective-permute-start(bf16[160,1280]{1,0:T(8,128)(2,1)S(1)} %collective-permute-done.1.refs_1_), channel_id=1, source_target_pairs={{0,16},{16,0},{1,17},{17,1},{2,18},{18,2},{3,19},{19,3},{4,20},{20... | collective-permute-start | bytes 1228808 | tf_op jit(solution)/shard_map/ppermute | solution.py:288
  23.3 0.9 %collective-permute-start.6 = (bf16[2,320,128]{2,1,0:T(8,128)(2,1)S(1)}, bf16[2,320,128]{2,1,0:T(8,128)(2,1)S(1)}, u32[]{:S(2)}, u32[]{:S(2)}) collective-permute-start(bf16[2,320,128]{2,1,0:T(8,128)(2,1)S(1)} %get-tuple-element.86), channel_id=1, source_target_pairs={{0,4},{2,6},{4,8},{6,10},{8,12},{10,14},{12,0},{14,2},{1,5},{3,7},... | collective-permute-start | bytes 491528 | tf_op jit(solution)/shard_map/ppermute | solution.py:298
  24.3 2.5 %collective-permute-start.7 = (bf16[2,320,128]{2,1,0:T(8,128)(2,1)S(1)}, bf16[2,320,128]{2,1,0:T(8,128)(2,1)S(1)}, u32[]{:S(2)}, u32[]{:S(2)}) collective-permute-start(bf16[2,320,128]{2,1,0:T(8,128)(2,1)S(1)} %get-tuple-element.87), channel_id=1, source_target_pairs={{0,6},{2,4},{4,10},{6,8},{8,14},{10,12},{12,2},{14,0},{1,7},{3,5},... | collective-permute-start | bytes 491528 | tf_op jit(solution)/shard_map/ppermute | solution.py:298
  26.8 2.2 %collective-permute-start.9 = (bf16[2,320,128]{2,1,0:T(8,128)(2,1)S(1)}, bf16[2,320,128]{2,1,0:T(8,128)(2,1)S(1)}, u32[]{:S(2)}, u32[]{:S(2)}) collective-permute-start(bf16[2,320,128]{2,1,0:T(8,128)(2,1)S(1)} %get-tuple-element.89), channel_id=1, source_target_pairs={{0,14},{2,12},{4,2},{6,0},{8,6},{10,4},{12,10},{14,8},{1,15},{3,13... | collective-permute-start | bytes 491528 | tf_op jit(solution)/shard_map/ppermute | solution.py:298
  29.0 2.4 %collective-permute-start.8 = (bf16[2,320,128]{2,1,0:T(8,128)(2,1)S(1)}, bf16[2,320,128]{2,1,0:T(8,128)(2,1)S(1)}, u32[]{:S(2)}, u32[]{:S(2)}) collective-permute-start(bf16[2,320,128]{2,1,0:T(8,128)(2,1)S(1)} %get-tuple-element.88), channel_id=1, source_target_pairs={{0,10},{2,8},{4,14},{6,12},{8,2},{10,0},{12,6},{14,4},{1,11},{3,9}... | collective-permute-start | bytes 491528 | tf_op jit(solution)/shard_map/ppermute | solution.py:298
  31.4 1.3 %collective-permute-done.5.refs_2_ = bf16[160,1280]{1,0:T(8,128)(2,1)S(1)} collective-permute-done((bf16[160,1280]{1,0:T(8,128)(2,1)S(1)}, bf16[160,1280]{1,0:T(8,128)(2,1)S(1)}, u32[]{:S(2)}, u32[]{:S(2)}) %collective-permute-start.5) | collective-permute-done | bytes 409632 | tf_op jit(solution)/shard_map/ppermute | solution.py:288
  32.8 1.2 %split_table.3.refs_3_.refs_7_ = bf16[320,1280]{1,0:T(8,128)(2,1)S(1)} custom-call(s32[5]{0:T(128)S(1)} %stack.19.refs_0_, bf16[160,1280]{1,0:T(8,128)(2,1)S(1)} %collective-permute-done.1.refs_1_, bf16[160,1280]{1,0:T(8,128)(2,1)S(1)} %collective-permute-done.5.refs_2_), custom_call_target="tpu_custom_call" | custom-call | flops 262144000 | tf_op jit(solution)/shard_map/split_table/pallas_call | solution.py:55
  34.0 2.8 %collective-permute-done.7.refs_9_ = bf16[2,320,128]{2,1,0:T(8,128)(2,1)S(1)} collective-permute-done((bf16[2,320,128]{2,1,0:T(8,128)(2,1)S(1)}, bf16[2,320,128]{2,1,0:T(8,128)(2,1)S(1)}, u32[]{:S(2)}, u32[]{:S(2)}) %collective-permute-start.7) | collective-permute-done | bytes 163872 | tf_op jit(solution)/shard_map/ppermute | solution.py:298
  36.8 1.7 %collective-permute-done.9.refs_13_ = bf16[2,320,128]{2,1,0:T(8,128)(2,1)S(1)} collective-permute-done((bf16[2,320,128]{2,1,0:T(8,128)(2,1)S(1)}, bf16[2,320,128]{2,1,0:T(8,128)(2,1)S(1)}, u32[]{:S(2)}, u32[]{:S(2)}) %collective-permute-start.9) | collective-permute-done | bytes 163872 | tf_op jit(solution)/shard_map/ppermute | solution.py:298
  38.5 7.0 %collective-permute-done.8.refs_11_ = bf16[2,320,128]{2,1,0:T(8,128)(2,1)S(1)} collective-permute-done((bf16[2,320,128]{2,1,0:T(8,128)(2,1)S(1)}, bf16[2,320,128]{2,1,0:T(8,128)(2,1)S(1)}, u32[]{:S(2)}, u32[]{:S(2)}) %collective-permute-start.8) | collective-permute-done | bytes 163872 | tf_op jit(solution)/shard_map/ppermute | solution.py:298
  45.5 0.0 collective-permute-start.10
  45.5 2.2 %direct_legendre_and_solve.2 = (bf16[640,128]{1,0:T(8,128)(2,1)S(1)}, bf16[640,128]{1,0:T(8,128)(2,1)S(1)}, bf16[2,1280,256]{2,1,0:T(8,128)(2,1)S(1)}) custom-call(s32[5]{0:T(128)S(1)} %stack.19.refs_0_, bf16[256,256]{1,0:T(8,128)(2,1)S(1)} %get-tuple-element.68.refs_1_.refs_0_, bf16[256,256]{1,0:T(8,128)(2,1)S(1)} %get-tuple-element.69.refs_2_.refs_1_, ...), custom_call_target="tpu_custom_call" | custom-call | flops 419430400 | tf_op jit(solution)/shard_map/direct_legendre_and_solve/pallas_call | solution.py:55
  47.7 0.1 collective-permute-done.10.refs_4_.refs_8_
  47.9 1.5 %direct_legendre_and_solve.3 = (bf16[640,128]{1,0:T(8,128)(2,1)S(1)}, bf16[640,128]{1,0:T(8,128)(2,1)S(1)}) custom-call(bf16[256,256]{1,0:T(8,128)(2,1)S(1)} %get-tuple-element.68.refs_1_.refs_0_, bf16[256,256]{1,0:T(8,128)(2,1)S(1)} %get-tuple-element.69.refs_2_.refs_1_, f32[1280,128]{1,0:T(8,128)S(1)} %get-tuple-element.70.refs_3_.refs_2_, ...), custom_call_target="tpu_custom_call" | custom-call | flops 419430400 | tf_op jit(solution)/shard_map/direct_legendre_and_solve/pallas_call | solution.py:55
  49.3 2.0 %inverse_legendre.1 = (bf16[2,320,128]{2,1,0:T(8,128)(2,1)S(1)}, bf16[2,320,128]{2,1,0:T(8,128)(2,1)S(1)}, bf16[2,320,128]{2,1,0:T(8,128)(2,1)S(1)}, bf16[2,320,...) custom-call(s32[5]{0:T(128)S(1)} %stack.19.refs_0_, ...), custom_call_target="tpu_custom_call" | custom-call | flops 838860800 | tf_op jit(solution)/shard_map/inverse_legendre/pallas_call | solution.py:55
  51.4 0.6 collective-permute-start.11
  52.0 0.0 collective-permute-start.12
  52.0 3.8 %collective-permute-start.16 = (bf16[2,320,128]{2,1,0:T(8,128)(2,1)S(1)}, bf16[2,320,128]{2,1,0:T(8,128)(2,1)S(1)}, u32[]{:S(2)}, u32[]{:S(2)}) collective-permute-start(bf16[2,320,128]{2,1,0:T(8,128)(2,1)S(1)} %get-tuple-element.113), channel_id=1, source_target_pairs={{0,12},{2,14},{4,0},{6,2},{8,4},{10,6},{12,8},{14,10},{1,13},{3,15... | collective-permute-start | bytes 491528 | tf_op jit(solution)/shard_map/ppermute | solution.py:298
  55.8 1.5 %collective-permute-start.18 = (bf16[640,128]{1,0:T(8,128)(2,1)S(1)}, bf16[640,128]{1,0:T(8,128)(2,1)S(1)}, u32[]{:S(2)}, u32[]{:S(2)}) collective-permute-start(bf16[640,128]{1,0:T(8,128)(2,1)S(1)} %get-tuple-element.97.refs_2_), channel_id=1, source_target_pairs={{0,2},{2,0},{1,3},{3,1},{4,6},{6,4},{5,7},{7,5},{8,10},{10,8},{9,1... | collective-permute-start | bytes 491528 | tf_op jit(solution)/shard_map/ppermute | solution.py:288
  57.3 0.5 collective-permute-start.19
  57.8 0.1 collective-permute-done.11.refs_2_
  57.9 0.0 collective-permute-start.14
  57.9 3.0 %collective-permute-done.12.refs_3_ = bf16[2,320,128]{2,1,0:T(8,128)(2,1)S(1)} collective-permute-done((bf16[2,320,128]{2,1,0:T(8,128)(2,1)S(1)}, bf16[2,320,128]{2,1,0:T(8,128)(2,1)S(1)}, u32[]{:S(2)}, u32[]{:S(2)}) %collective-permute-start.12) | collective-permute-done | bytes 163872 | tf_op jit(solution)/shard_map/ppermute | solution.py:298
  60.9 0.8 collective-permute-start.15
  61.7 0.6 collective-permute-done.16.refs_7_
  62.3 1.6 %collective-permute-start.13 = (bf16[2,320,128]{2,1,0:T(8,128)(2,1)S(1)}, bf16[2,320,128]{2,1,0:T(8,128)(2,1)S(1)}, u32[]{:S(2)}, u32[]{:S(2)}) collective-permute-start(bf16[2,320,128]{2,1,0:T(8,128)(2,1)S(1)} %get-tuple-element.109), channel_id=1, source_target_pairs={{0,6},{2,4},{4,10},{6,8},{8,14},{10,12},{12,2},{14,0},{1,7},{3,5},... | collective-permute-start | bytes 491528 | tf_op jit(solution)/shard_map/ppermute | solution.py:298
  64.0 0.0 collective-permute-done.18.refs_3_
  64.0 3.1 %collective-permute-start.17 = (bf16[2,320,128]{2,1,0:T(8,128)(2,1)S(1)}, bf16[2,320,128]{2,1,0:T(8,128)(2,1)S(1)}, u32[]{:S(2)}, u32[]{:S(2)}) collective-permute-start(bf16[2,320,128]{2,1,0:T(8,128)(2,1)S(1)} %get-tuple-element.115), channel_id=1, source_target_pairs={{0,14},{2,12},{4,2},{6,0},{8,6},{10,4},{12,10},{14,8},{1,15},{3,13... | collective-permute-start | bytes 491528 | tf_op jit(solution)/shard_map/ppermute | solution.py:298
  67.0 1.8 %order_spectral.1 = bf16[2560,128]{1,0:T(8,128)(2,1)} custom-call(s32[5]{0:T(128)S(1)} %stack.19.refs_0_, bf16[640,128]{1,0:T(8,128)(2,1)S(1)} %get-tuple-element.96.refs_1_, bf16[640,128]{1,0:T(8,128)(2,1)S(1)} %get-tuple-element.100.refs_3_.refs_2_, bf16[640,128]{1,0:T(8,128)(2,1)S(1)} %collective-permute-done.18.refs_3_, ...), custom_call_target="tpu_custom_call" | custom-call | flops 671088640 | tf_op jit(solution)/shard_map/order_spectral/pallas_call | solution.py:55
  68.8 7.7 %collective-permute-done.14.refs_5_ = bf16[2,320,128]{2,1,0:T(8,128)(2,1)S(1)} collective-permute-done((bf16[2,320,128]{2,1,0:T(8,128)(2,1)S(1)}, bf16[2,320,128]{2,1,0:T(8,128)(2,1)S(1)}, u32[]{:S(2)}, u32[]{:S(2)}) %collective-permute-start.14) | collective-permute-done | bytes 163872 | tf_op jit(solution)/shard_map/ppermute | solution.py:298
  76.5 4.5 %collective-permute-done.15.refs_6_ = bf16[2,320,128]{2,1,0:T(8,128)(2,1)S(1)} collective-permute-done((bf16[2,320,128]{2,1,0:T(8,128)(2,1)S(1)}, bf16[2,320,128]{2,1,0:T(8,128)(2,1)S(1)}, u32[]{:S(2)}, u32[]{:S(2)}) %collective-permute-start.15) | collective-permute-done | bytes 163872 | tf_op jit(solution)/shard_map/ppermute | solution.py:298
  81.0 2.0 %join_hemispheres.1 = bf16[2,2560,128]{2,1,0:T(8,128)(2,1)} custom-call(s32[5]{0:T(128)S(1)} %stack.19.refs_0_, bf16[2,320,128]{2,1,0:T(8,128)(2,1)S(1)} %get-tuple-element.102.refs_1_, bf16[2,320,128]{2,1,0:T(8,128)(2,1)S(1)} %collective-permute-done.11.refs_2_, bf16[2,320,128]{2,1,0:T(8,128)(2,1)S(1)} %collective-permute-done.12.refs_3_, ...), custom_call_target="tpu_custom_call" | custom-call | flops 671088640 | tf_op jit(solution)/shard_map/join_hemispheres/pallas_call | solution.py:55
  (15 shorter events, 0.1 us)
Async XLA Ops:
  0.6 3.9 %collective-permute-start = (bf16[320,1280]{1,0:T(8,128)(2,1)}, bf16[320,1280]{1,0:T(8,128)(2,1)S(1)}, u32[]{:S(2)}, u32[]{:S(2)}) collective-permute-start(bf16[320,1280]{1,0:T(8,128)(2,1)} %bitcast.9), channel_id=1, source_target_pairs={{0,1},{1,0},{2,3},{3,2},{4,5},{5,4},{6,7},{7,6},{8,9},{9,8},{10,11... | collective-permute-start | bytes 2457608 | tf_op jit(solution)/shard_map/ppermute | solution.py:288
  1.9 2.6 %copy-start = (bf16[1,320,1280]{2,1,0:T(8,128)(2,1)S(1)}, bf16[1,320,1280]{2,1,0:T(8,128)(2,1)}, u32[]{:S(2)}) copy-start(bf16[1,320,1280]{2,1,0:T(8,128)(2,1)} %param.7) | copy-start | bytes 2457604
  2.0 1.4 %copy-start.4 = (bf16[2,320,4,2,128]{4,3,2,1,0:T(2,128)(2,1)S(1)}, bf16[2,320,4,2,128]{4,3,2,1,0:T(2,128)(2,1)}, u32[]{:S(2)}) copy-start(bf16[2,320,4,2,128]{4,3,2,1,0:T(2,128)(2,1)} %param.6) | copy-start | bytes 3932164
  3.4 7.9 %copy-start.1 = (bf16[128,128]{1,0:T(8,128)(2,1)S(1)}, bf16[128,128]{1,0:T(8,128)(2,1)}, u32[]{:S(2)}) copy-start(bf16[128,128]{1,0:T(8,128)(2,1)} %refs_1_.1) | copy-start | bytes 98308
  3.4 7.9 %copy-start.2 = (bf16[128,128]{1,0:T(8,128)(2,1)S(1)}, bf16[128,128]{1,0:T(8,128)(2,1)}, u32[]{:S(2)}) copy-start(bf16[128,128]{1,0:T(8,128)(2,1)} %refs_2_.1) | copy-start | bytes 98308
  3.4 7.9 %copy-start.3 = (f32[128]{0:T(128)S(1)}, f32[128]{0:T(128)}, u32[]{:S(2)}) copy-start(f32[128]{0:T(128)} %param.11) | copy-start | bytes 1540
  4.6 17.2 %collective-permute-start.1 = (bf16[160,1280]{1,0:T(8,128)(2,1)S(1)}, bf16[160,1280]{1,0:T(8,128)(2,1)S(1)}, u32[]{:S(2)}, u32[]{:S(2)}) collective-permute-start(bf16[160,1280]{1,0:T(8,128)(2,1)S(1)} %constant_dynamic-slice_fusion), channel_id=1, source_target_pairs={{0,2},{2,0},{1,3},{3,1},{4,6},{6,4},{5,7},{7,5},{8,10},{10,8},{9,1... | collective-permute-start | bytes 1228808 | tf_op jit(solution)/shard_map/ppermute | solution.py:288
  7.2 13.6 %collective-permute-start.4 = (bf16[2,320,128]{2,1,0:T(8,128)(2,1)S(1)}, bf16[2,320,128]{2,1,0:T(8,128)(2,1)S(1)}, u32[]{:S(2)}, u32[]{:S(2)}) collective-permute-start(bf16[2,320,128]{2,1,0:T(8,128)(2,1)S(1)} %get-tuple-element.82), channel_id=1, source_target_pairs={{0,2},{2,0},{4,6},{6,4},{8,10},{10,8},{12,14},{14,12},{1,3},{3,1},... | collective-permute-start | bytes 491528 | tf_op jit(solution)/shard_map/ppermute | solution.py:298
  7.3 13.6 %collective-permute-start.3 = (bf16[2,320,128]{2,1,0:T(8,128)(2,1)S(1)}, bf16[2,320,128]{2,1,0:T(8,128)(2,1)S(1)}, u32[]{:S(2)}, u32[]{:S(2)}) collective-permute-start(bf16[2,320,128]{2,1,0:T(8,128)(2,1)S(1)} %get-tuple-element.79), channel_id=1, source_target_pairs={{0,12},{2,14},{4,0},{6,2},{8,4},{10,6},{12,8},{14,10},{1,13},{3,15... | collective-permute-start | bytes 491528 | tf_op jit(solution)/shard_map/ppermute | solution.py:298
  11.3 10.5 %collective-permute-start.2 = (bf16[2,320,128]{2,1,0:T(8,128)(2,1)S(1)}, bf16[2,320,128]{2,1,0:T(8,128)(2,1)S(1)}, u32[]{:S(2)}, u32[]{:S(2)}) collective-permute-start(bf16[2,320,128]{2,1,0:T(8,128)(2,1)S(1)} %get-tuple-element.76), channel_id=1, source_target_pairs={{0,8},{2,10},{4,12},{6,14},{8,0},{10,2},{12,4},{14,6},{1,9},{3,11}... | collective-permute-start | bytes 491528 | tf_op jit(solution)/shard_map/ppermute | solution.py:298
  21.8 10.9 %collective-permute-start.5 = (bf16[160,1280]{1,0:T(8,128)(2,1)S(1)}, bf16[160,1280]{1,0:T(8,128)(2,1)S(1)}, u32[]{:S(2)}, u32[]{:S(2)}) collective-permute-start(bf16[160,1280]{1,0:T(8,128)(2,1)S(1)} %collective-permute-done.1.refs_1_), channel_id=1, source_target_pairs={{0,16},{16,0},{1,17},{17,1},{2,18},{18,2},{3,19},{19,3},{4,20},{20... | collective-permute-start | bytes 1228808 | tf_op jit(solution)/shard_map/ppermute | solution.py:288
  23.3 10.6 %collective-permute-start.6 = (bf16[2,320,128]{2,1,0:T(8,128)(2,1)S(1)}, bf16[2,320,128]{2,1,0:T(8,128)(2,1)S(1)}, u32[]{:S(2)}, u32[]{:S(2)}) collective-permute-start(bf16[2,320,128]{2,1,0:T(8,128)(2,1)S(1)} %get-tuple-element.86), channel_id=1, source_target_pairs={{0,4},{2,6},{4,8},{6,10},{8,12},{10,14},{12,0},{14,2},{1,5},{3,7},... | collective-permute-start | bytes 491528 | tf_op jit(solution)/shard_map/ppermute | solution.py:298
  24.3 12.5 %collective-permute-start.7 = (bf16[2,320,128]{2,1,0:T(8,128)(2,1)S(1)}, bf16[2,320,128]{2,1,0:T(8,128)(2,1)S(1)}, u32[]{:S(2)}, u32[]{:S(2)}) collective-permute-start(bf16[2,320,128]{2,1,0:T(8,128)(2,1)S(1)} %get-tuple-element.87), channel_id=1, source_target_pairs={{0,6},{2,4},{4,10},{6,8},{8,14},{10,12},{12,2},{14,0},{1,7},{3,5},... | collective-permute-start | bytes 491528 | tf_op jit(solution)/shard_map/ppermute | solution.py:298
  26.8 11.7 %collective-permute-start.9 = (bf16[2,320,128]{2,1,0:T(8,128)(2,1)S(1)}, bf16[2,320,128]{2,1,0:T(8,128)(2,1)S(1)}, u32[]{:S(2)}, u32[]{:S(2)}) collective-permute-start(bf16[2,320,128]{2,1,0:T(8,128)(2,1)S(1)} %get-tuple-element.89), channel_id=1, source_target_pairs={{0,14},{2,12},{4,2},{6,0},{8,6},{10,4},{12,10},{14,8},{1,15},{3,13... | collective-permute-start | bytes 491528 | tf_op jit(solution)/shard_map/ppermute | solution.py:298
  29.0 16.5 %collective-permute-start.8 = (bf16[2,320,128]{2,1,0:T(8,128)(2,1)S(1)}, bf16[2,320,128]{2,1,0:T(8,128)(2,1)S(1)}, u32[]{:S(2)}, u32[]{:S(2)}) collective-permute-start(bf16[2,320,128]{2,1,0:T(8,128)(2,1)S(1)} %get-tuple-element.88), channel_id=1, source_target_pairs={{0,10},{2,8},{4,14},{6,12},{8,2},{10,0},{12,6},{14,4},{1,11},{3,9}... | collective-permute-start | bytes 491528 | tf_op jit(solution)/shard_map/ppermute | solution.py:298
  45.5 2.3 %collective-permute-start.10 = (bf16[320,1280]{1,0:T(8,128)(2,1)S(1)}, bf16[320,1280]{1,0:T(8,128)(2,1)S(1)}, u32[]{:S(2)}, u32[]{:S(2)}) collective-permute-start(bf16[320,1280]{1,0:T(8,128)(2,1)S(1)} %split_table.3.refs_3_.refs_7_), channel_id=1, source_target_pairs={{0,1},{1,0},{2,3},{3,2},{4,5},{5,4},{6,7},{7,6},{8,9},{9,8},{10,11... | collective-permute-start | bytes 2457608 | tf_op jit(solution)/shard_map/ppermute | solution.py:288
  51.4 6.6 %collective-permute-start.11 = (bf16[2,320,128]{2,1,0:T(8,128)(2,1)S(1)}, bf16[2,320,128]{2,1,0:T(8,128)(2,1)S(1)}, u32[]{:S(2)}, u32[]{:S(2)}) collective-permute-start(bf16[2,320,128]{2,1,0:T(8,128)(2,1)S(1)} %get-tuple-element.104), channel_id=1, source_target_pairs={{0,2},{2,0},{4,6},{6,4},{8,10},{10,8},{12,14},{14,12},{1,3},{3,1},... | collective-permute-start | bytes 491528 | tf_op jit(solution)/shard_map/ppermute | solution.py:298
  52.0 8.9 %collective-permute-start.12 = (bf16[2,320,128]{2,1,0:T(8,128)(2,1)S(1)}, bf16[2,320,128]{2,1,0:T(8,128)(2,1)S(1)}, u32[]{:S(2)}, u32[]{:S(2)}) collective-permute-start(bf16[2,320,128]{2,1,0:T(8,128)(2,1)S(1)} %get-tuple-element.107), channel_id=1, source_target_pairs={{0,4},{2,6},{4,8},{6,10},{8,12},{10,14},{12,0},{14,2},{1,5},{3,7},... | collective-permute-start | bytes 491528 | tf_op jit(solution)/shard_map/ppermute | solution.py:298
  52.0 10.3 %collective-permute-start.16 = (bf16[2,320,128]{2,1,0:T(8,128)(2,1)S(1)}, bf16[2,320,128]{2,1,0:T(8,128)(2,1)S(1)}, u32[]{:S(2)}, u32[]{:S(2)}) collective-permute-start(bf16[2,320,128]{2,1,0:T(8,128)(2,1)S(1)} %get-tuple-element.113), channel_id=1, source_target_pairs={{0,12},{2,14},{4,0},{6,2},{8,4},{10,6},{12,8},{14,10},{1,13},{3,15... | collective-permute-start | bytes 491528 | tf_op jit(solution)/shard_map/ppermute | solution.py:298
  55.8 8.1 %collective-permute-start.18 = (bf16[640,128]{1,0:T(8,128)(2,1)S(1)}, bf16[640,128]{1,0:T(8,128)(2,1)S(1)}, u32[]{:S(2)}, u32[]{:S(2)}) collective-permute-start(bf16[640,128]{1,0:T(8,128)(2,1)S(1)} %get-tuple-element.97.refs_2_), channel_id=1, source_target_pairs={{0,2},{2,0},{1,3},{3,1},{4,6},{6,4},{5,7},{7,5},{8,10},{10,8},{9,1... | collective-permute-start | bytes 491528 | tf_op jit(solution)/shard_map/ppermute | solution.py:288
  57.3 9.7 %collective-permute-start.19 = (bf16[640,128]{1,0:T(8,128)(2,1)S(1)}, bf16[640,128]{1,0:T(8,128)(2,1)S(1)}, u32[]{:S(2)}, u32[]{:S(2)}) collective-permute-start(bf16[640,128]{1,0:T(8,128)(2,1)S(1)} %get-tuple-element.101.refs_4_), channel_id=1, source_target_pairs={{0,2},{2,0},{1,3},{3,1},{4,6},{6,4},{5,7},{7,5},{8,10},{10,8},{9,1... | collective-permute-start | bytes 491528 | tf_op jit(solution)/shard_map/ppermute | solution.py:288
  57.9 18.6 %collective-permute-start.14 = (bf16[2,320,128]{2,1,0:T(8,128)(2,1)S(1)}, bf16[2,320,128]{2,1,0:T(8,128)(2,1)S(1)}, u32[]{:S(2)}, u32[]{:S(2)}) collective-permute-start(bf16[2,320,128]{2,1,0:T(8,128)(2,1)S(1)} %get-tuple-element.110), channel_id=1, source_target_pairs={{0,8},{2,10},{4,12},{6,14},{8,0},{10,2},{12,4},{14,6},{1,9},{3,11}... | collective-permute-start | bytes 491528 | tf_op jit(solution)/shard_map/ppermute | solution.py:298
  60.9 20.1 %collective-permute-start.15 = (bf16[2,320,128]{2,1,0:T(8,128)(2,1)S(1)}, bf16[2,320,128]{2,1,0:T(8,128)(2,1)S(1)}, u32[]{:S(2)}, u32[]{:S(2)}) collective-permute-start(bf16[2,320,128]{2,1,0:T(8,128)(2,1)S(1)} %get-tuple-element.111), channel_id=1, source_target_pairs={{0,10},{2,8},{4,14},{6,12},{8,2},{10,0},{12,6},{14,4},{1,11},{3,9}... | collective-permute-start | bytes 491528 | tf_op jit(solution)/shard_map/ppermute | solution.py:298
  62.3 18.6 %collective-permute-start.13 = (bf16[2,320,128]{2,1,0:T(8,128)(2,1)S(1)}, bf16[2,320,128]{2,1,0:T(8,128)(2,1)S(1)}, u32[]{:S(2)}, u32[]{:S(2)}) collective-permute-start(bf16[2,320,128]{2,1,0:T(8,128)(2,1)S(1)} %get-tuple-element.109), channel_id=1, source_target_pairs={{0,6},{2,4},{4,10},{6,8},{8,14},{10,12},{12,2},{14,0},{1,7},{3,5},... | collective-permute-start | bytes 491528 | tf_op jit(solution)/shard_map/ppermute | solution.py:298
  64.0 17.0 %collective-permute-start.17 = (bf16[2,320,128]{2,1,0:T(8,128)(2,1)S(1)}, bf16[2,320,128]{2,1,0:T(8,128)(2,1)S(1)}, u32[]{:S(2)}, u32[]{:S(2)}) collective-permute-start(bf16[2,320,128]{2,1,0:T(8,128)(2,1)S(1)} %get-tuple-element.115), channel_id=1, source_target_pairs={{0,14},{2,12},{4,2},{6,0},{8,6},{10,4},{12,10},{14,8},{1,15},{3,13... | collective-permute-start | bytes 491528 | tf_op jit(solution)/shard_map/ppermute | solution.py:298
